TPU v7x, 128 devices: a whole 4x4x4 slice. The times are simulated.
128 devices in a mesh: dp: 16 (over y_lo, x, core), mp: 8 (over z, y_hi).
Axes of the slice: x: 4, y: 4 (y_hi: 2, y_lo: 2; y = y_hi * 2 + y_lo), z: 4, core: 2. Of those that a mesh axis runs over, the one named last changes fastest.
Arguments:
- tokens: bfloat16 [128, 98304], P('dp', 'mp'), may hold values from -6 to 6
- norm_gain: float32 [1536], replicated, may hold values from 0.25 to 1.75
- qkv_weight: bfloat16 [3, 1536, 1536], P(None, 'mp'), may hold values from -0.15625 to 0.15625
- out_weight: bfloat16 [1536, 1536], P('mp'), may hold values from -0.15625 to 0.15625
- text_embed: bfloat16 [128, 1536], P(('dp', 'mp')), may hold values from -0.1875 to 0.1875
- log_temp: float32 [1], replicated, may hold values from 0.5 to 1.5
- logit_bias: float32 [1], replicated, may hold values from -3 to -1
Outputs:
- text_grad: float32 [128, 1536], P(('dp', 'mp'))
- qkv_grad: float32 [3, 1536, 1536], P(None, 'mp', 'dp')
- out_grad: float32 [1536, 1536], P('mp', 'dp')
All inputs are finite; a program needn't handle non-finite values.
Results may differ from a plain program's by a relative error of at most 0.03.
Values may be sent and summed in bfloat16 or wider, within the bound.
No kernel may reach another device: no remote copies, remote signals or barrier semaphores. Data moves between devices by JAX's collectives and lax.ppermute only.
A program may use at most 64 MiB of HBM per device.

v0:
```python
import math

import jax
import jax.numpy as jnp
from jax import lax
from jax.sharding import PartitionSpec as P

D = 1536
DH = 96
P_SIZE = 64


EPS = 1e-06


def from_behind(block, axis, distance):
    devices = range(lax.axis_size(axis))
    route = [((i - distance) % len(devices), i) for i in devices]
    return lax.ppermute(block, axis, route)


def unit_rows(matrix):
    values = matrix.astype(jnp.float32)
    inverse = lax.rsqrt(jnp.sum(values * values, axis=-1, keepdims=True) + EPS)
    return (values * inverse, inverse)


def body(tokens, norm_gain, qkv_weight, out_weight, text_embed, log_temp, logit_bias):
    count = tokens.shape[0]
    gathered = lax.all_gather(tokens, "mp", axis=1, tiled=True).reshape(count, P_SIZE, D)
    wide_input = gathered.astype(jnp.float32)
    center = wide_input - jnp.mean(wide_input, axis=-1, keepdims=True)
    spread = jnp.mean(center * center, axis=-1, keepdims=True)
    normed = (center * lax.rsqrt(spread + EPS) * norm_gain).astype(jnp.bfloat16)
    length, width = (P_SIZE, qkv_weight.shape[1])
    heads_here = width // DH
    mixed = jnp.einsum(
        "bpd,cfd->bpcf", normed, qkv_weight, preferred_element_type=jnp.float32
    ).astype(jnp.bfloat16)
    shaped = mixed.reshape(count, length, 3, heads_here, DH)
    query_rows, key_rows, value_rows = (shaped[:, :, 0], shaped[:, :, 1], shaped[:, :, 2])
    scores = jnp.einsum(
        "bqhd,bkhd->bhqk", query_rows, key_rows, preferred_element_type=jnp.float32
    ) / math.sqrt(DH)
    weights = jnp.exp(scores)
    probs = (weights / jnp.sum(weights, axis=-1, keepdims=True)).astype(jnp.bfloat16)
    attended = jnp.einsum(
        "bhqk,bkhd->bqhd", probs, value_rows, preferred_element_type=jnp.float32
    ).astype(jnp.bfloat16)
    attended = attended.reshape(count, length, width)
    attend_total = jnp.sum(attended, axis=1, dtype=jnp.float32)
    partial_value = jnp.einsum(
        "bpf,fd->bpd", attended, out_weight, preferred_element_type=jnp.float32
    )
    summed = lax.psum(partial_value.astype(jnp.bfloat16), "mp").astype(jnp.float32)
    pooled = jnp.mean(wide_input + summed, axis=1)
    scale = jnp.exp(log_temp[0])
    shift_value = logit_bias[0]
    image_unit, image_inv = unit_rows(pooled)
    text_rows = text_embed.shape[0]
    feature_count = text_embed.shape[1]
    cycle_size = lax.axis_size("dp")
    my_slot = lax.axis_index("mp")
    image_ids = jnp.arange(count)
    diagonal = (image_ids[:, None] == my_slot * text_rows + jnp.arange(text_rows)[None, :]).astype(
        jnp.float32
    )

    def visit(turn_index, carry):
        block, block_grad, image_acc = carry
        block_unit, unused = unit_rows(block)
        logits = (
            scale * jnp.dot(image_unit, block_unit.T, precision=lax.Precision.HIGHEST) + shift_value
        )
        own_block = (turn_index == 0).astype(jnp.float32)
        pair_grad = jax.nn.sigmoid(logits) - own_block * diagonal
        image_acc = image_acc + scale * jnp.dot(
            pair_grad, block_unit, precision=lax.Precision.HIGHEST
        )
        block_grad = block_grad + scale * jnp.dot(
            pair_grad.T, image_unit, precision=lax.Precision.HIGHEST
        )
        block = from_behind(block, "dp", 1)
        block_grad = from_behind(block_grad, "dp", 1)
        return (block, block_grad, image_acc)

    start = (
        text_embed,
        jnp.zeros((text_rows, feature_count), jnp.float32),
        jnp.zeros((count, feature_count), jnp.float32),
    )
    unused, unit_grad, image_unit_grad = lax.fori_loop(0, cycle_size, visit, start)
    text_unit, text_inv = unit_rows(text_embed)
    text_grad = (
        unit_grad - text_unit * jnp.sum(text_unit * unit_grad, axis=-1, keepdims=True)
    ) * text_inv
    image_unit_grad = lax.psum(image_unit_grad.astype(jnp.bfloat16), "mp").astype(jnp.float32)
    pooled_grad = (
        image_unit_grad - image_unit * jnp.sum(image_unit * image_unit_grad, axis=-1, keepdims=True)
    ) * image_inv
    resid_grad = (pooled_grad / length).astype(jnp.bfloat16)
    out_term = jnp.dot(
        attend_total.T, resid_grad.astype(jnp.float32), precision=lax.Precision.HIGHEST
    )
    out_grad = lax.psum_scatter(
        out_term.astype(jnp.bfloat16), "dp", scatter_dimension=1, tiled=True
    ).astype(jnp.float32)
    attend_grad = jnp.dot(resid_grad, out_weight.T, preferred_element_type=jnp.float32).astype(
        jnp.bfloat16
    )
    attend_grad = attend_grad.reshape(count, heads_here, DH)
    prob_grad = jnp.einsum(
        "bhd,bkhd->bhk", attend_grad, value_rows, preferred_element_type=jnp.float32
    )[:, :, None, :]
    prob_vals = probs.astype(jnp.float32)
    value_grad = jnp.einsum(
        "bhqk,bhd->bkhd", probs, attend_grad, preferred_element_type=jnp.float32
    ).astype(jnp.bfloat16)
    score_grad = (
        prob_vals
        * (prob_grad - jnp.sum(prob_vals * prob_grad, axis=-1, keepdims=True))
        / math.sqrt(DH)
    ).astype(jnp.bfloat16)
    query_grad = jnp.einsum(
        "bhqk,bkhd->bqhd", score_grad, key_rows, preferred_element_type=jnp.float32
    ).astype(jnp.bfloat16)
    key_grad = jnp.einsum(
        "bhqk,bqhd->bkhd", score_grad, query_rows, preferred_element_type=jnp.float32
    ).astype(jnp.bfloat16)
    stacked = jnp.stack([query_grad, key_grad, value_grad], axis=2).reshape(count, length, 3, width)
    qkv_term = jnp.einsum("bpcf,bpd->cfd", stacked, normed, preferred_element_type=jnp.float32)
    qkv_grad = lax.psum_scatter(
        qkv_term.astype(jnp.bfloat16), "dp", scatter_dimension=2, tiled=True
    ).astype(jnp.float32)
    return (text_grad, qkv_grad, out_grad)


def solution(mesh):
    placed = (
        P("dp", "mp"),
        P(),
        P(None, "mp", None),
        P("mp", None),
        P(("dp", "mp"), None),
        P(),
        P(),
    )
    return jax.shard_map(
        body,
        mesh=mesh,
        in_specs=placed,
        out_specs=(P(("dp", "mp"), None), P(None, "mp", "dp"), P("mp", "dp")),
        check_vma=False,
    )
```

profile of v0, /device:TPU:1, one launch (start us, length us, event | category | flops | bytes accessed | tf_op | source)
XLA Modules:
  0.0 465.1 jit_solution(2730483370754382097)
XLA Ops:
  8.0 54.9 %all-gather.2.cloned.1.call-done = bf16[8,98304]{1,0:T(8,128)(2,1)} async-done(((bf16[8,12288]{1,0:T(8,128)(2,1)}), bf16[8,98304]{1,0:T(8,128)(2,1)}) %all-gather.2.cloned.1.call-update) | async-done | bytes 1572880 | tf_op jit(solution)/shard_map/all_gather | solution.py:30
  62.8 1.8 convert.5
  64.7 1.7 bitcast_reduce_fusion
  66.4 1.7 multiply_reduce_fusion.1
  68.7 2.9 fusion.20
  73.7 2.8 convolution_convert_fusion
  78.7 90.3 %all-reduce.2.cloned.1.call-done = bf16[8,64,1536]{2,1,0:T(8,128)(2,1)} async-done(((bf16[8,64,1536]{2,1,0:T(8,128)(2,1)}), bf16[8,64,1536]{2,1,0:T(8,128)(2,1)}) %all-reduce.2.cloned.1.call-update) | async-done | bytes 1572880 | tf_op jit(solution)/shard_map/psum | solution.py:55
  169.0 4.2 fusion.15
  173.4 121.3 %while.18 = (s32[]{:T(128)}, bf16[1,1536]{1,0:T(2,128)(2,1)S(1)}, f32[1,1536]{1,0:T(1,128)S(1)}, f32[8,1536]{1,0:T(8,128)S(1)}, f32[]{:T(128)}, /*index=5*/f32[8...) while((s32[]{:T(128)}, bf16[1,1536]{1,0:T(2,128)(2,1)S(1)}, ...), condition=%wide.region_8.9_spmd.clone, body=%wide.region_6.8_spmd.clone.sunk | while | flops 357956 | bytes 298340 | solution.py:92
  173.5 5.2 %collective-permute-start = (bf16[1,1536]{1,0:T(2,128)(2,1)S(1)}, bf16[1,1536]{1,0:T(2,128)(2,1)S(1)}, u32[]{:S(2)}, u32[]{:S(2)}) collective-permute-start(bf16[1,1536]{1,0:T(2,128)(2,1)S(1)} %copy.81), channel_id=1, source_target_pairs={{120,0},{0,8},{8,16},{16,24},{24,32},{32,40},{40,48},{48,56},{56,6... | collective-permute-start | bytes 9224 | tf_op jit(solution)/shard_map/while/body/eval_jaxpr/ppermute | solution.py:19
  182.2 2.0 collective-permute-start
  186.7 1.6 collective-permute-done.1
  188.3 1.4 collective-permute-start
  193.5 2.4 collective-permute-done.1
  198.5 2.7 collective-permute-done
  201.1 2.4 collective-permute-done.1
  206.1 2.7 collective-permute-done
  208.7 2.4 collective-permute-done.1
  213.7 2.7 collective-permute-done
  216.3 2.4 collective-permute-done.1
  221.3 2.7 collective-permute-done
  224.0 2.4 collective-permute-done.1
  228.9 2.7 collective-permute-done
  231.6 2.4 collective-permute-done.1
  236.5 2.7 collective-permute-done
  239.2 2.4 collective-permute-done.1
  244.1 2.7 collective-permute-done
  246.8 2.4 collective-permute-done.1
  251.7 2.7 collective-permute-done
  254.4 2.4 collective-permute-done.1
  259.3 2.7 collective-permute-done
  262.0 2.4 collective-permute-done.1
  266.9 2.7 collective-permute-done
  269.6 2.4 collective-permute-done.1
  274.5 2.7 collective-permute-done
  277.2 2.4 collective-permute-done.1
  282.1 2.7 collective-permute-done
  284.8 2.4 collective-permute-done.1
  289.7 2.7 collective-permute-done
  292.4 2.4 collective-permute-done.1
  294.8 32.0 %psum.15 = bf16[8,1536]{1,0:T(8,128)(2,1)S(1)} all-reduce(bf16[8,1536]{1,0:T(8,128)(2,1)S(1)} %convert_element_type.121), channel_id=1, replica_groups=mesh['dp'=16,'mp'=8] {'mp'}, use_global_device_ids=true, to_apply=%region_11.0 | all-reduce | flops 12288 | bytes 49152 | tf_op jit(solution)/shard_map/psum | solution.py:97
  330.6 1.7 fusion.31
  333.5 1.5 fusion.32
  337.7 4.8 %bitcast_convert_fusion = bf16[3,192,1536]{2,1,0:T(8,128)(2,1)S(1)} fusion(bf16[8,64,1,192]{3,1,0,2:T(8,128)(2,1)} %stack.14, bf16[8,64,1,192]{3,1,0,2:T(8,128)(2,1)} %stack.13, bf16[8,64,1,192]{3,1,0,2:T(8,128)(2,1)} %stack.12, f32[1,8,64,1536]{3,1,2,0:T(8,128)} %copy-done.1, f32[1536]{0:T(1024)} %param.10, f32[8,64]{1,0:T(8,128)S(1)} %copy-done.7, ...), kind=kOutput, calls=%fused_computation.22 | convolution fusion | flops 910589952 | bytes 5515264 | tf_op jit(solution)/shard_map/bpcf,bpd->cfd/dot_general | solution.py:131
  342.5 3.6 copy.38
  346.1 7.1 %reshape.138 = bf16[1536,576]{1,0:T(8,128)(2,1)} reshape(bf16[1536,3,192]{2,1,0:T(4,128)(2,1)} %bitcast.127) | data formatting | bytes 3538944
  356.3 36.5 %reduce-scatter.9.cloned.1.call-done = bf16[96,192]{1,0:T(8,128)(2,1)} async-done(((bf16[1536,192]{1,0:T(8,128)(2,1)}), bf16[96,192]{1,0:T(8,128)(2,1)}) %reduce-scatter.9.cloned.1.call-update) | async-done | bytes 36880
  394.4 62.1 %reduce-scatter.7.cloned.1.call-done = bf16[96,576]{1,0:T(8,128)(2,1)} async-done(((bf16[1536,576]{1,0:T(8,128)(2,1)}), bf16[96,576]{1,0:T(8,128)(2,1)}) %reduce-scatter.7.cloned.1.call-update) | async-done | bytes 110608
  (226 shorter events, 51.6 us)
Async XLA Ops:
  7.2 61.6 %copy-start = (bf16[3,192,1536]{2,1,0:T(8,128)(2,1)S(1)}, bf16[3,192,1536]{2,1,0:T(8,128)(2,1)}, u32[]{:S(2)}) copy-start(bf16[3,192,1536]{2,1,0:T(8,128)(2,1)} %param.11) | copy-start | bytes 5308420
  7.2 55.7 %all-gather.2.cloned.1.call-start = ((), (), s32[]{:S(2)}) async-start(), calls=%async_computation.2 | async-start | bytes 1769472 | tf_op jit(solution)/shard_map/all_gather | solution.py:30
  7.9 161.1 %all-reduce.2.cloned.1.call-start = ((), (), s32[]{:S(2)}) async-start(), calls=%async_computation.3 | async-start | bytes 3145728 | tf_op jit(solution)/shard_map/psum | solution.py:55
  64.6 3.5 copy-start.1
  64.6 4.1 copy-start.8
  66.4 1.7 copy-start.4
  68.1 0.6 copy-start.6
  76.5 316.3 %reduce-scatter.9.cloned.1.call-start = ((), (), s32[]{:S(2)}) async-start(), calls=%async_computation.5 | async-start | bytes 835584
  78.6 94.9 %copy-start.3 = (bf16[1,1536]{1,0:T(2,128)(2,1)S(1)}, bf16[1,1536]{1,0:T(2,128)(2,1)}, u32[]{:S(2)}) copy-start(bf16[1,1536]{1,0:T(2,128)(2,1)} %param.13) | copy-start | bytes 9220
  173.5 7.7 %collective-permute-start = (bf16[1,1536]{1,0:T(2,128)(2,1)S(1)}, bf16[1,1536]{1,0:T(2,128)(2,1)S(1)}, u32[]{:S(2)}, u32[]{:S(2)}) collective-permute-start(bf16[1,1536]{1,0:T(2,128)(2,1)S(1)} %copy.81), channel_id=1, source_target_pairs={{120,0},{0,8},{8,16},{16,24},{24,32},{32,40},{40,48},{48,56},{56,6... | collective-permute-start | bytes 9224 | tf_op jit(solution)/shard_map/while/body/eval_jaxpr/ppermute | solution.py:19
  181.0 1.2 collective-permute-start.1
  182.2 4.4 collective-permute-start
  186.5 1.8 collective-permute-start.1
  188.3 5.2 %collective-permute-start = (bf16[1,1536]{1,0:T(2,128)(2,1)S(1)}, bf16[1,1536]{1,0:T(2,128)(2,1)S(1)}, u32[]{:S(2)}, u32[]{:S(2)}) collective-permute-start(bf16[1,1536]{1,0:T(2,128)(2,1)S(1)} %copy.81), channel_id=1, source_target_pairs={{120,0},{0,8},{8,16},{16,24},{24,32},{32,40},{40,48},{48,56},{56,6... | collective-permute-start | bytes 9224 | tf_op jit(solution)/shard_map/while/body/eval_jaxpr/ppermute | solution.py:19
  192.0 3.9 collective-permute-start.1
  195.9 5.2 %collective-permute-start = (bf16[1,1536]{1,0:T(2,128)(2,1)S(1)}, bf16[1,1536]{1,0:T(2,128)(2,1)S(1)}, u32[]{:S(2)}, u32[]{:S(2)}) collective-permute-start(bf16[1,1536]{1,0:T(2,128)(2,1)S(1)} %copy.81), channel_id=1, source_target_pairs={{120,0},{0,8},{8,16},{16,24},{24,32},{32,40},{40,48},{48,56},{56,6... | collective-permute-start | bytes 9224 | tf_op jit(solution)/shard_map/while/body/eval_jaxpr/ppermute | solution.py:19
  198.3 5.2 %collective-permute-start.1 = (f32[1,1536]{1,0:T(1,128)S(1)}, f32[1,1536]{1,0:T(1,128)S(1)}, u32[]{:S(2)}, u32[]{:S(2)}) collective-permute-start(f32[1,1536]{1,0:T(1,128)S(1)} %reshape_add_fusion.2), channel_id=1, source_target_pairs={{120,0},{0,8},{8,16},{16,24},{24,32},{32,40},{40,48},{48,56},{56,6... | collective-permute-start | bytes 18440 | tf_op jit(solution)/shard_map/while/body/eval_jaxpr/ppermute | solution.py:19
  203.5 5.2 %collective-permute-start = (bf16[1,1536]{1,0:T(2,128)(2,1)S(1)}, bf16[1,1536]{1,0:T(2,128)(2,1)S(1)}, u32[]{:S(2)}, u32[]{:S(2)}) collective-permute-start(bf16[1,1536]{1,0:T(2,128)(2,1)S(1)} %copy.81), channel_id=1, source_target_pairs={{120,0},{0,8},{8,16},{16,24},{24,32},{32,40},{40,48},{48,56},{56,6... | collective-permute-start | bytes 9224 | tf_op jit(solution)/shard_map/while/body/eval_jaxpr/ppermute | solution.py:19
  205.9 5.2 %collective-permute-start.1 = (f32[1,1536]{1,0:T(1,128)S(1)}, f32[1,1536]{1,0:T(1,128)S(1)}, u32[]{:S(2)}, u32[]{:S(2)}) collective-permute-start(f32[1,1536]{1,0:T(1,128)S(1)} %reshape_add_fusion.2), channel_id=1, source_target_pairs={{120,0},{0,8},{8,16},{16,24},{24,32},{32,40},{40,48},{48,56},{56,6... | collective-permute-start | bytes 18440 | tf_op jit(solution)/shard_map/while/body/eval_jaxpr/ppermute | solution.py:19
  211.1 5.2 %collective-permute-start = (bf16[1,1536]{1,0:T(2,128)(2,1)S(1)}, bf16[1,1536]{1,0:T(2,128)(2,1)S(1)}, u32[]{:S(2)}, u32[]{:S(2)}) collective-permute-start(bf16[1,1536]{1,0:T(2,128)(2,1)S(1)} %copy.81), channel_id=1, source_target_pairs={{120,0},{0,8},{8,16},{16,24},{24,32},{32,40},{40,48},{48,56},{56,6... | collective-permute-start | bytes 9224 | tf_op jit(solution)/shard_map/while/body/eval_jaxpr/ppermute | solution.py:19
  213.5 5.2 %collective-permute-start.1 = (f32[1,1536]{1,0:T(1,128)S(1)}, f32[1,1536]{1,0:T(1,128)S(1)}, u32[]{:S(2)}, u32[]{:S(2)}) collective-permute-start(f32[1,1536]{1,0:T(1,128)S(1)} %reshape_add_fusion.2), channel_id=1, source_target_pairs={{120,0},{0,8},{8,16},{16,24},{24,32},{32,40},{40,48},{48,56},{56,6... | collective-permute-start | bytes 18440 | tf_op jit(solution)/shard_map/while/body/eval_jaxpr/ppermute | solution.py:19
  218.7 5.2 %collective-permute-start = (bf16[1,1536]{1,0:T(2,128)(2,1)S(1)}, bf16[1,1536]{1,0:T(2,128)(2,1)S(1)}, u32[]{:S(2)}, u32[]{:S(2)}) collective-permute-start(bf16[1,1536]{1,0:T(2,128)(2,1)S(1)} %copy.81), channel_id=1, source_target_pairs={{120,0},{0,8},{8,16},{16,24},{24,32},{32,40},{40,48},{48,56},{56,6... | collective-permute-start | bytes 9224 | tf_op jit(solution)/shard_map/while/body/eval_jaxpr/ppermute | solution.py:19
  221.1 5.2 %collective-permute-start.1 = (f32[1,1536]{1,0:T(1,128)S(1)}, f32[1,1536]{1,0:T(1,128)S(1)}, u32[]{:S(2)}, u32[]{:S(2)}) collective-permute-start(f32[1,1536]{1,0:T(1,128)S(1)} %reshape_add_fusion.2), channel_id=1, source_target_pairs={{120,0},{0,8},{8,16},{16,24},{24,32},{32,40},{40,48},{48,56},{56,6... | collective-permute-start | bytes 18440 | tf_op jit(solution)/shard_map/while/body/eval_jaxpr/ppermute | solution.py:19
  226.3 5.2 %collective-permute-start = (bf16[1,1536]{1,0:T(2,128)(2,1)S(1)}, bf16[1,1536]{1,0:T(2,128)(2,1)S(1)}, u32[]{:S(2)}, u32[]{:S(2)}) collective-permute-start(bf16[1,1536]{1,0:T(2,128)(2,1)S(1)} %copy.81), channel_id=1, source_target_pairs={{120,0},{0,8},{8,16},{16,24},{24,32},{32,40},{40,48},{48,56},{56,6... | collective-permute-start | bytes 9224 | tf_op jit(solution)/shard_map/while/body/eval_jaxpr/ppermute | solution.py:19
  228.7 5.2 %collective-permute-start.1 = (f32[1,1536]{1,0:T(1,128)S(1)}, f32[1,1536]{1,0:T(1,128)S(1)}, u32[]{:S(2)}, u32[]{:S(2)}) collective-permute-start(f32[1,1536]{1,0:T(1,128)S(1)} %reshape_add_fusion.2), channel_id=1, source_target_pairs={{120,0},{0,8},{8,16},{16,24},{24,32},{32,40},{40,48},{48,56},{56,6... | collective-permute-start | bytes 18440 | tf_op jit(solution)/shard_map/while/body/eval_jaxpr/ppermute | solution.py:19
  233.9 5.2 %collective-permute-start = (bf16[1,1536]{1,0:T(2,128)(2,1)S(1)}, bf16[1,1536]{1,0:T(2,128)(2,1)S(1)}, u32[]{:S(2)}, u32[]{:S(2)}) collective-permute-start(bf16[1,1536]{1,0:T(2,128)(2,1)S(1)} %copy.81), channel_id=1, source_target_pairs={{120,0},{0,8},{8,16},{16,24},{24,32},{32,40},{40,48},{48,56},{56,6... | collective-permute-start | bytes 9224 | tf_op jit(solution)/shard_map/while/body/eval_jaxpr/ppermute | solution.py:19
  236.3 5.2 %collective-permute-start.1 = (f32[1,1536]{1,0:T(1,128)S(1)}, f32[1,1536]{1,0:T(1,128)S(1)}, u32[]{:S(2)}, u32[]{:S(2)}) collective-permute-start(f32[1,1536]{1,0:T(1,128)S(1)} %reshape_add_fusion.2), channel_id=1, source_target_pairs={{120,0},{0,8},{8,16},{16,24},{24,32},{32,40},{40,48},{48,56},{56,6... | collective-permute-start | bytes 18440 | tf_op jit(solution)/shard_map/while/body/eval_jaxpr/ppermute | solution.py:19
  241.5 5.2 %collective-permute-start = (bf16[1,1536]{1,0:T(2,128)(2,1)S(1)}, bf16[1,1536]{1,0:T(2,128)(2,1)S(1)}, u32[]{:S(2)}, u32[]{:S(2)}) collective-permute-start(bf16[1,1536]{1,0:T(2,128)(2,1)S(1)} %copy.81), channel_id=1, source_target_pairs={{120,0},{0,8},{8,16},{16,24},{24,32},{32,40},{40,48},{48,56},{56,6... | collective-permute-start | bytes 9224 | tf_op jit(solution)/shard_map/while/body/eval_jaxpr/ppermute | solution.py:19
  243.9 5.2 %collective-permute-start.1 = (f32[1,1536]{1,0:T(1,128)S(1)}, f32[1,1536]{1,0:T(1,128)S(1)}, u32[]{:S(2)}, u32[]{:S(2)}) collective-permute-start(f32[1,1536]{1,0:T(1,128)S(1)} %reshape_add_fusion.2), channel_id=1, source_target_pairs={{120,0},{0,8},{8,16},{16,24},{24,32},{32,40},{40,48},{48,56},{56,6... | collective-permute-start | bytes 18440 | tf_op jit(solution)/shard_map/while/body/eval_jaxpr/ppermute | solution.py:19
  249.2 5.2 %collective-permute-start = (bf16[1,1536]{1,0:T(2,128)(2,1)S(1)}, bf16[1,1536]{1,0:T(2,128)(2,1)S(1)}, u32[]{:S(2)}, u32[]{:S(2)}) collective-permute-start(bf16[1,1536]{1,0:T(2,128)(2,1)S(1)} %copy.81), channel_id=1, source_target_pairs={{120,0},{0,8},{8,16},{16,24},{24,32},{32,40},{40,48},{48,56},{56,6... | collective-permute-start | bytes 9224 | tf_op jit(solution)/shard_map/while/body/eval_jaxpr/ppermute | solution.py:19
  251.5 5.2 %collective-permute-start.1 = (f32[1,1536]{1,0:T(1,128)S(1)}, f32[1,1536]{1,0:T(1,128)S(1)}, u32[]{:S(2)}, u32[]{:S(2)}) collective-permute-start(f32[1,1536]{1,0:T(1,128)S(1)} %reshape_add_fusion.2), channel_id=1, source_target_pairs={{120,0},{0,8},{8,16},{16,24},{24,32},{32,40},{40,48},{48,56},{56,6... | collective-permute-start | bytes 18440 | tf_op jit(solution)/shard_map/while/body/eval_jaxpr/ppermute | solution.py:19
  256.8 5.2 %collective-permute-start = (bf16[1,1536]{1,0:T(2,128)(2,1)S(1)}, bf16[1,1536]{1,0:T(2,128)(2,1)S(1)}, u32[]{:S(2)}, u32[]{:S(2)}) collective-permute-start(bf16[1,1536]{1,0:T(2,128)(2,1)S(1)} %copy.81), channel_id=1, source_target_pairs={{120,0},{0,8},{8,16},{16,24},{24,32},{32,40},{40,48},{48,56},{56,6... | collective-permute-start | bytes 9224 | tf_op jit(solution)/shard_map/while/body/eval_jaxpr/ppermute | solution.py:19
  259.1 5.2 %collective-permute-start.1 = (f32[1,1536]{1,0:T(1,128)S(1)}, f32[1,1536]{1,0:T(1,128)S(1)}, u32[]{:S(2)}, u32[]{:S(2)}) collective-permute-start(f32[1,1536]{1,0:T(1,128)S(1)} %reshape_add_fusion.2), channel_id=1, source_target_pairs={{120,0},{0,8},{8,16},{16,24},{24,32},{32,40},{40,48},{48,56},{56,6... | collective-permute-start | bytes 18440 | tf_op jit(solution)/shard_map/while/body/eval_jaxpr/ppermute | solution.py:19
  264.4 5.2 %collective-permute-start = (bf16[1,1536]{1,0:T(2,128)(2,1)S(1)}, bf16[1,1536]{1,0:T(2,128)(2,1)S(1)}, u32[]{:S(2)}, u32[]{:S(2)}) collective-permute-start(bf16[1,1536]{1,0:T(2,128)(2,1)S(1)} %copy.81), channel_id=1, source_target_pairs={{120,0},{0,8},{8,16},{16,24},{24,32},{32,40},{40,48},{48,56},{56,6... | collective-permute-start | bytes 9224 | tf_op jit(solution)/shard_map/while/body/eval_jaxpr/ppermute | solution.py:19
  266.7 5.2 %collective-permute-start.1 = (f32[1,1536]{1,0:T(1,128)S(1)}, f32[1,1536]{1,0:T(1,128)S(1)}, u32[]{:S(2)}, u32[]{:S(2)}) collective-permute-start(f32[1,1536]{1,0:T(1,128)S(1)} %reshape_add_fusion.2), channel_id=1, source_target_pairs={{120,0},{0,8},{8,16},{16,24},{24,32},{32,40},{40,48},{48,56},{56,6... | collective-permute-start | bytes 18440 | tf_op jit(solution)/shard_map/while/body/eval_jaxpr/ppermute | solution.py:19
  272.0 5.2 %collective-permute-start = (bf16[1,1536]{1,0:T(2,128)(2,1)S(1)}, bf16[1,1536]{1,0:T(2,128)(2,1)S(1)}, u32[]{:S(2)}, u32[]{:S(2)}) collective-permute-start(bf16[1,1536]{1,0:T(2,128)(2,1)S(1)} %copy.81), channel_id=1, source_target_pairs={{120,0},{0,8},{8,16},{16,24},{24,32},{32,40},{40,48},{48,56},{56,6... | collective-permute-start | bytes 9224 | tf_op jit(solution)/shard_map/while/body/eval_jaxpr/ppermute | solution.py:19
  274.3 5.2 %collective-permute-start.1 = (f32[1,1536]{1,0:T(1,128)S(1)}, f32[1,1536]{1,0:T(1,128)S(1)}, u32[]{:S(2)}, u32[]{:S(2)}) collective-permute-start(f32[1,1536]{1,0:T(1,128)S(1)} %reshape_add_fusion.2), channel_id=1, source_target_pairs={{120,0},{0,8},{8,16},{16,24},{24,32},{32,40},{40,48},{48,56},{56,6... | collective-permute-start | bytes 18440 | tf_op jit(solution)/shard_map/while/body/eval_jaxpr/ppermute | solution.py:19
  279.6 5.2 %collective-permute-start = (bf16[1,1536]{1,0:T(2,128)(2,1)S(1)}, bf16[1,1536]{1,0:T(2,128)(2,1)S(1)}, u32[]{:S(2)}, u32[]{:S(2)}) collective-permute-start(bf16[1,1536]{1,0:T(2,128)(2,1)S(1)} %copy.81), channel_id=1, source_target_pairs={{120,0},{0,8},{8,16},{16,24},{24,32},{32,40},{40,48},{48,56},{56,6... | collective-permute-start | bytes 9224 | tf_op jit(solution)/shard_map/while/body/eval_jaxpr/ppermute | solution.py:19
  281.9 5.2 %collective-permute-start.1 = (f32[1,1536]{1,0:T(1,128)S(1)}, f32[1,1536]{1,0:T(1,128)S(1)}, u32[]{:S(2)}, u32[]{:S(2)}) collective-permute-start(f32[1,1536]{1,0:T(1,128)S(1)} %reshape_add_fusion.2), channel_id=1, source_target_pairs={{120,0},{0,8},{8,16},{16,24},{24,32},{32,40},{40,48},{48,56},{56,6... | collective-permute-start | bytes 18440 | tf_op jit(solution)/shard_map/while/body/eval_jaxpr/ppermute | solution.py:19
  287.2 5.2 %collective-permute-start = (bf16[1,1536]{1,0:T(2,128)(2,1)S(1)}, bf16[1,1536]{1,0:T(2,128)(2,1)S(1)}, u32[]{:S(2)}, u32[]{:S(2)}) collective-permute-start(bf16[1,1536]{1,0:T(2,128)(2,1)S(1)} %copy.81), channel_id=1, source_target_pairs={{120,0},{0,8},{8,16},{16,24},{24,32},{32,40},{40,48},{48,56},{56,6... | collective-permute-start | bytes 9224 | tf_op jit(solution)/shard_map/while/body/eval_jaxpr/ppermute | solution.py:19
  289.6 5.2 %collective-permute-start.1 = (f32[1,1536]{1,0:T(1,128)S(1)}, f32[1,1536]{1,0:T(1,128)S(1)}, u32[]{:S(2)}, u32[]{:S(2)}) collective-permute-start(f32[1,1536]{1,0:T(1,128)S(1)} %reshape_add_fusion.2), channel_id=1, source_target_pairs={{120,0},{0,8},{8,16},{16,24},{24,32},{32,40},{40,48},{48,56},{56,6... | collective-permute-start | bytes 18440 | tf_op jit(solution)/shard_map/while/body/eval_jaxpr/ppermute | solution.py:19
  330.3 7.4 %copy-start.5 = (f32[8,64]{1,0:T(8,128)S(1)}, f32[8,64]{1,0:T(8,128)}, u32[]{:S(2)}) copy-start(f32[8,64]{1,0:T(8,128)} %copy-done.4) | copy-start | bytes 6148
  330.3 7.4 %copy-start.7 = (f32[8,64]{1,0:T(8,128)S(1)}, f32[8,64]{1,0:T(8,128)}, u32[]{:S(2)}) copy-start(f32[8,64]{1,0:T(8,128)} %copy-done.6) | copy-start | bytes 6148
  330.3 126.2 %reduce-scatter.7.cloned.1.call-start = ((), (), s32[]{:S(2)}) async-start(), calls=%async_computation.4 | async-start | bytes 2088960
  346.1 7.1 %copy-start.2 = (bf16[1,1536]{1,0:T(2,128)(2,1)S(1)}, bf16[1,1536]{1,0:T(2,128)(2,1)}, u32[]{:S(2)}) copy-start(bf16[1,1536]{1,0:T(2,128)(2,1)} %param.13) | copy-start | bytes 9220
Sparse Core Ops, SparseCore 0:
  10.3 52.4 all-gather.1
  76.7 92.3 all-reduce.1
  330.5 62.3 reduce-scatter.8
  395.3 61.2 reduce-scatter.6
where the time goes:
time: 470 us; the launch traced here: 465 us
  waiting for transfers between devices  316 us (67%)
  matrix products  34.6 us (7%)
  blocking collectives  32 us (7%)
  other arithmetic  25.4 us (5%)
  local copies, waits for them, and re-layouts  19.7 us (4%)
  between operations  15.4 us (3%)
  starting transfers between devices  11.2 us (2%)
  loops' own time  10.4 us (2%)
    unnamed x6, waiting for transfers between devices  99.4 us
    psum x1, waiting for transfers between devices, body(): lax.psum(partial_value.astype(jnp.bfloat16), 'mp').astype(jnp.float32)  90.3 us
    ppermute x32, waiting for transfers between devices, from_behind(): return lax.ppermute(block, axis, route)  71.9 us
    all_gather x1, waiting for transfers between devices, body(): lax.all_gather(tokens, 'mp', axis=1, tiled=True).reshape(count, P_SIZE, D)  54.9 us
    psum x1, blocking collectives, body(): lax.psum(image_unit_grad.astype(jnp.bfloat16), 'mp').astype(jnp.float32)  32 us
    unnamed x24, local copies, waits for them, and re-layouts  14.6 us
    dot_general x16, matrix products, visit(): jnp.dot(image_unit, block_unit.T, precision=lax.Precision.HIGHEST)  13.3 us
    ppermute x32, starting transfers between devices, from_behind(): return lax.ppermute(block, axis, route)  10.8 us
  transfers between devices with their start and end apart: 36, of which 34 were waited for; matrix products, arithmetic and copies ran while one was open for 12% of the time, Pallas kernels for 0%

commit v1 on v0

v1 whole, which is shorter than its diff:
```python
import math

import jax
import jax.numpy as jnp
from jax import lax
from jax.experimental import pallas as pl
from jax.experimental.pallas import tpu as pltpu
from jax.sharding import PartitionSpec as P

D = 1536
DH = 96
TOK = 64
IMG = 8
MP = 8
DP = 16
TEXT = DP * MP
WIDTH = 192
EPS = 1e-06
F32 = jnp.float32
BF16 = jnp.bfloat16
SCALE = 1.0 / math.sqrt(DH)
ROWS = 400
LAST = (((1,), (1,)), ((), ()))
FIRST = (((0,), (0,)), ((), ()))
PARAMS = pltpu.CompilerParams(vmem_limit_bytes=48 * 1024 * 1024)


def dot(a, b, dims):
    return lax.dot_general(a, b, dims, preferred_element_type=F32)


def pieces(a, n):
    out = []
    for _ in range(n):
        p = a.astype(BF16)
        out.append(p)
        a = a - p.astype(F32)
    return out


def lanes(shape):
    return lax.broadcasted_iota(jnp.int32, shape, len(shape) - 1)


def norm_kernel(tok_ref, gain_ref, text_ref, out_ref, sum_ref, rows_ref):
    gain = gain_ref[...]
    total = jnp.zeros((IMG, D), F32)
    for t in range(8):
        x = tok_ref[:, t * D:(t + 1) * D].astype(F32)
        center = x - jnp.mean(x, axis=-1, keepdims=True)
        spread = jnp.mean(center * center, axis=-1, keepdims=True)
        row = center * lax.rsqrt(spread + EPS) * gain
        for i in range(12):
            rows_ref[pl.ds(i * 64 + t, IMG, stride=8), :] = row[:, i * 128:(i + 1) * 128]
        total = total + x
    sum_ref[...] = total
    normed = jnp.concatenate([rows_ref[i * 64:(i + 1) * 64, :] for i in range(12)], axis=1)
    normed = normed.astype(BF16)
    text = text_ref[...]
    for d in range(MP):
        out_ref[d, 0:64, :] = normed
        out_ref[d, 64:80, :] = text


def forward_kernel(g_ref, w_ref, wo_ref, sum_ref, part_ref, qkv_ref, probs_ref, att_ref, wide_ref):
    normed = g_ref[:, 0:64, :].reshape(512, D)
    for c in range(3):
        wide_ref[...] = dot(normed, w_ref[c], LAST)
        for b in range(IMG):
            block = jnp.concatenate(
                [wide_ref[(s * 8 + b) * 8:(s * 8 + b) * 8 + 8, :] for s in range(MP)], axis=0
            )
            qkv_ref[c, b * 64:(b + 1) * 64, :] = block.astype(BF16)
    lane = lanes((64, WIDTH))
    for b in range(IMG):
        rows = slice(b * 64, (b + 1) * 64)
        q, k = qkv_ref[0, rows, :], qkv_ref[1, rows, :]
        v = qkv_ref[2, rows, :].astype(F32)
        columns = []
        for h in range(2):
            inside = lane < DH if h == 0 else lane >= DH
            score = dot(k, jnp.where(inside, q, jnp.zeros_like(q)), LAST) * SCALE
            weights = jnp.exp(score)
            probs = (weights / jnp.sum(weights, axis=0, keepdims=True)).astype(BF16)
            probs_ref[b * 2 + h] = probs
            columns.append(jnp.sum(probs.astype(F32), axis=1, keepdims=True))
        attended = jnp.sum(jnp.where(lane < DH, columns[0], columns[1]) * v, axis=0, keepdims=True)
        att_ref[b:b + 1, :] = attended
    high, low = pieces(att_ref[...], 2)
    branch = dot(jnp.concatenate([high, low], axis=0), wo_ref[...], (((1,), (0,)), ((), ())))
    part = ((branch[0:8] + branch[8:16] + sum_ref[...]) * (1.0 / TOK)).astype(BF16)
    for d in range(MP):
        part_ref[d] = part


def backward_kernel(
    g_ref, part_ref, qkv_ref, probs_ref, att_ref, wo_ref, temp_ref, bias_ref,
    keep_ref, give_ref, grad_ref, turn_ref, text_ref, both_ref,
):
    me = lax.axis_index("dp")
    slot = lax.axis_index("mp")
    core = lax.rem(me, 2)
    pooled = jnp.zeros((IMG, D), F32)
    for s in range(MP):
        pooled = pooled + part_ref[s].astype(F32)
    scale = jnp.exp(temp_ref[...])
    image_inv = lax.rsqrt(jnp.sum(pooled * pooled, axis=-1, keepdims=True) + EPS)
    unit = pooled * image_inv
    text = g_ref[:, 64:80, :].reshape(TEXT, D)
    wide_text = text.astype(F32)
    square = pieces(wide_text * wide_text, 2)
    ones = jnp.ones((IMG, D), BF16)
    text_inv = lax.rsqrt(dot(ones, square[0], LAST) + dot(ones, square[1], LAST) + EPS)
    cosine = dot(jnp.concatenate(pieces(unit, 3), axis=0), text, LAST)
    cosine = (cosine[0:8] + cosine[8:16] + cosine[16:24]) * text_inv
    logits = scale * cosine + bias_ref[...]
    image_row = lax.broadcasted_iota(jnp.int32, (IMG, TEXT), 0)
    own = lanes((IMG, TEXT)) == image_row * DP + me
    pair = scale * (jax.nn.sigmoid(logits) - jnp.where(own, 1.0, 0.0))
    unit_grad = dot(
        jnp.concatenate(pieces(pair * text_inv, 3), axis=0), text, (((1,), (0,)), ((), ()))
    )
    unit_grad = unit_grad[0:8] + unit_grad[8:16] + unit_grad[16:24]
    pooled_grad = (unit_grad - unit * jnp.sum(unit * unit_grad, axis=-1, keepdims=True)) * image_inv
    resid = (pooled_grad * (1.0 / TOK)).astype(BF16)
    mine = pltpu.roll(pair, lax.rem(TEXT - slot * DP, TEXT), axis=1)
    pair_high, pair_low = pieces(mine, 2)
    unit_high, unit_low = pieces(unit, 2)
    text_grad = dot(
        jnp.concatenate([pair_high, pair_high, pair_low], axis=0),
        jnp.concatenate([unit_high, unit_low, unit_high], axis=0),
        FIRST,
    )
    text_ref[...] = jnp.zeros_like(text_ref)
    for i in range(12):
        text_ref[pl.ds(i, DP, stride=16), :] = text_grad[0:DP, i * 128:(i + 1) * 128]
    attend = dot(resid, wo_ref[...], LAST).astype(BF16)
    wide_attend = attend.astype(F32)
    lane = lanes((64, WIDTH))
    slim = lanes((64, 64))
    for b in range(IMG):
        rows = slice(b * 64, (b + 1) * 64)
        q, k = qkv_ref[0, rows, :], qkv_ref[1, rows, :]
        product = qkv_ref[2, rows, :].astype(F32) * wide_attend[b:b + 1, :]
        query_grad, key_grad, factor = [], [], jnp.zeros((64, 64), F32)
        for h in range(2):
            inside = lane < DH if h == 0 else lane >= DH
            prob_grad = jnp.sum(jnp.where(inside, product, 0.0), axis=1, keepdims=True)
            probs = probs_ref[b * 2 + h].astype(F32)
            mean = jnp.sum(probs * prob_grad, axis=0, keepdims=True)
            score_grad = (probs * (prob_grad - mean) * SCALE).astype(BF16)
            query_grad.append(dot(score_grad, k, FIRST))
            key_grad.append(dot(score_grad, q, (((1,), (0,)), ((), ()))))
            column = jnp.sum(probs, axis=1, keepdims=True)
            factor = factor + jnp.where(slim == h * 8 + b, column, 0.0)
        query_grad = jnp.where(lane < DH, query_grad[0], query_grad[1])
        key_grad = jnp.where(lane < DH, key_grad[0], key_grad[1])
        first = jnp.where(core == 0, factor, 0.0)
        full = jnp.concatenate([query_grad, first, key_grad, factor - first], axis=1)
        for s in range(MP):
            grad_ref[(s * 8 + b) * 8:(s * 8 + b) * 8 + 8, :] = full[s * 8:s * 8 + 8, :]
    turn_ref[...] = jnp.zeros_like(turn_ref)
    start = pl.multiple_of(core * 128, 128)
    for h in range(2):
        part = slice(h * DH, (h + 1) * DH)
        turn_ref[pl.ds(start + 96 + h * 8, 8), 0:DH] = wide_attend[:, part]
        turn_ref[pl.ds(start + 112 + h * 8, 8), 0:DH] = att_ref[:, part]
    turned = [turn_ref[i * 128:(i + 1) * 128, :].T[0:DH, :] for i in range(2)]
    place = lanes((IMG, 512)) - lax.broadcasted_iota(jnp.int32, (IMG, 512), 0) - core * 256
    spot = jnp.where((place == 208) | (place == 216), 1.0, 0.0).astype(BF16)
    normed = g_ref[:, 0:64, :].reshape(512, D)
    grads = grad_ref[...].astype(BF16)
    for c in range(4):
        columns = slice(c * 384, (c + 1) * 384)
        y = dot(normed[:, columns], grads, FIRST) + dot(resid[:, columns], spot, FIRST)
        for j in range(4):
            d = c * 4 + j
            for i in range(4):
                block = y[j * 96:(j + 1) * 96, i * 128:(i + 1) * 128]
                if i % 2 == 1:
                    block = block + turned[i // 2]
                both_ref[d % 2, d // 2, i * 96:(i + 1) * 96, :] = block.astype(BF16)
            both_ref[d % 2, d // 2, 384:400, :] = text_ref[d * 16:(d + 1) * 16, :].astype(BF16)
    keep_ref[...] = both_ref[core]
    give_ref[...] = both_ref[1 - core]


def finish_kernel(r_ref, text_ref, text_out, qkv_out, out_out, stack_ref):
    total = r_ref[0].astype(F32)
    for s in range(1, 8):
        total = total + r_ref[s].astype(F32)
    unit_grad = total[384:396, :]
    text = text_ref[...].astype(F32)
    inv = lax.rsqrt(jnp.sum(text * text, keepdims=True) + EPS)
    unit = text * inv
    text_out[...] = (unit_grad - unit * jnp.sum(unit * unit_grad, keepdims=True)) * inv
    pad = jnp.zeros((32, 128), F32)
    for c in range(2):
        for i in range(2):
            at = (c * 2 + i) * 96
            turned = jnp.concatenate([total[at:at + 96, :], pad], axis=0).T
            rows = 128 if i == 0 else 64
            qkv_out[c, i * 128:i * 128 + rows, :] = turned[0:rows, 0:96]
    lane = lanes((96, 128))
    group = lax.shift_right_logical(lane, 3) - 8
    factors = []
    for s in range(8):
        for c in range(2):
            block = r_ref[s, (c * 2 + 1) * 96:(c * 2 + 2) * 96, :]
            factors.append(block)
            rolled = pltpu.roll(block.astype(F32), 96, axis=1)
            for g in range(4):
                at = (s * 2 + c) * 128
                stack_ref[g * 96:(g + 1) * 96, at:at + 128] = jnp.where(
                    group == g, rolled, 0.0
                ).astype(BF16)
    product = dot(stack_ref[...], jnp.concatenate(factors, axis=1), LAST)
    qkv_out[2] = product[0:192, :]
    out_out[...] = product[192:384, :]


def call(kernel, outs, scratch, *args):
    return pl.pallas_call(
        kernel,
        out_shape=[jax.ShapeDtypeStruct(*o) for o in outs],
        scratch_shapes=[pltpu.VMEM(*s) for s in scratch],
        compiler_params=PARAMS,
    )(*args)


def body(tokens, norm_gain, qkv_weight, out_weight, text_embed, log_temp, logit_bias):
    texts = lax.all_to_all(
        jnp.broadcast_to(text_embed[None], (DP, 1, D)), "dp", 0, 0
    ).reshape(DP, D)
    copies, token_sum = call(
        norm_kernel,
        [((MP, 80, D), BF16), ((IMG, D), F32)],
        [((12 * 64, 128), F32)],
        tokens, norm_gain.reshape(1, D), texts,
    )
    gathered = lax.all_to_all(copies, "mp", 0, 0)
    part, qkv, probs, attended = call(
        forward_kernel,
        [((MP, IMG, D), BF16), ((3, 512, WIDTH), BF16), ((16, 64, 64), BF16), ((IMG, WIDTH), F32)],
        [((512, WIDTH), F32)],
        gathered, qkv_weight, out_weight, token_sum,
    )
    parts = lax.all_to_all(part, "mp", 0, 0)
    keep, give = call(
        backward_kernel,
        [((8, ROWS, 128), BF16)] * 2,
        [((512, 512), F32), ((256, 128), F32), ((256, 128), F32), ((2, 8, ROWS, 128), BF16)],
        gathered, parts, qkv, probs, attended, out_weight,
        log_temp.reshape(1, 1), logit_bias.reshape(1, 1),
    )
    other = lax.ppermute(give, "dp", [(i, i ^ 1) for i in range(DP)])
    send = (keep.astype(F32) + other.astype(F32)).astype(BF16)
    received = lax.all_to_all(
        send, "dp", 0, 0, axis_index_groups=[list(range(c, DP, 2)) for c in range(2)]
    )
    text_grad, qkv_grad, out_grad = call(
        finish_kernel,
        [((12, 128), F32), ((3, WIDTH, 96), F32), ((WIDTH, 96), F32)],
        [((384, 2048), BF16)],
        received, text_embed.reshape(12, 128),
    )
    return (text_grad.reshape(1, D), qkv_grad, out_grad)


def solution(mesh):
    placed = (
        P("dp", "mp"),
        P(),
        P(None, "mp", None),
        P("mp", None),
        P(("dp", "mp"), None),
        P(),
        P(),
    )
    return jax.shard_map(
        body,
        mesh=mesh,
        in_specs=placed,
        out_specs=(P(("dp", "mp"), None), P(None, "mp", "dp"), P("mp", "dp")),
        check_vma=False,
    )
```

time: 470 us -> 93.5 us (0.20)
  waiting for transfers between devices: 316 us -> 13.2 us
  matrix products: 34.6 us -> 0 us
  other arithmetic: 25.4 us -> 1.85 us
  blocking collectives: 32 us -> 49.3 us
  local copies, waits for them, and re-layouts: 19.7 us -> 5.82 us
  between operations: 15.4 us -> 2.01 us
  loops' own time: 10.4 us -> 0 us
  Pallas kernels: 0 us -> 7.7 us
    unnamed x6 -> x0, waiting for transfers between devices: 99.4 us -> none
    psum x1 -> x0, waiting for transfers between devices: 90.3 us -> none  [body(): lax.psum(partial_value.astype(jnp.bfloat16), 'mp').astype(jnp.float32)]
    ppermute x32 -> x1, waiting for transfers between devices: 71.9 us -> 1.96 us  [body(): other = lax.ppermute(give, 'dp', [(i, i ^ 1) for i in range(DP)])]
    all_gather x1 -> x0, waiting for transfers between devices: 54.9 us -> none  [body(): lax.all_gather(tokens, 'mp', axis=1, tiled=True).reshape(count, P_SIZE, D)]
    all_to_all x0 -> x2, blocking collectives: none -> 49.3 us  [the longest x1 33.5 us: body(): gathered = lax.all_to_all(copies, 'mp', 0, 0)]
    dot_general x42 -> x0, matrix products: 33.5 us -> none  [the longest x16 13.3 us: visit(): jnp.dot(image_unit, block_unit.T, precision=lax.Precision.HIGHEST)]
    psum x1 -> x0, blocking collectives: 32 us -> none  [body(): lax.psum(image_unit_grad.astype(jnp.bfloat16), 'mp').astype(jnp.float32)]
    reduce_sum x23 -> x0, other arithmetic: 18.4 us -> none  [the longest x18 10 us: unit_rows(): inverse = lax.rsqrt(jnp.sum(values * values, axis=-1, keepdims=True) + EPS)]
  transfers between devices with their start and end apart: 36 -> 3, of which waited for: 34 -> 3; matrix products, arithmetic and copies ran while one was open for 12% -> 1% of each run, Pallas kernels for 0% -> 0%
where the time goes in v1:
time: 93.5 us; the launch traced here: 93 us
  blocking collectives  49.3 us (53%)
  waiting for transfers between devices  13.2 us (14%)
  starting transfers between devices  13.1 us (14%)
  Pallas kernels  7.7 us (8%)
  local copies, waits for them, and re-layouts  5.82 us (6%)
  between operations  2.01 us (2%)
  other arithmetic  1.85 us (2%)
    all_to_all x1, blocking collectives, body(): gathered = lax.all_to_all(copies, 'mp', 0, 0)  33.5 us
    all_to_all x1, blocking collectives, body(): lax.all_to_all(send, 'dp', 0, 0, axis_index_groups=[list(range(c, DP, 2))...  15.7 us
    pallas_call x4, Pallas kernels, call(): pl.pallas_call(kernel, out_shape=[jax.ShapeDtypeStruct(*o) for o in outs]...  7.7 us
    all_to_all x1, starting transfers between devices, body(): lax.all_to_all(jnp.broadcast_to(text_embed[None], (DP, 1, D)), 'dp', 0, 0)  6.83 us
    all_to_all x1, waiting for transfers between devices, body(): parts = lax.all_to_all(part, 'mp', 0, 0)  6.15 us
    all_to_all x1, waiting for transfers between devices, body(): lax.all_to_all(jnp.broadcast_to(text_embed[None], (DP, 1, D)), 'dp', 0, 0)  5.11 us
    unnamed x16, local copies, waits for them, and re-layouts  4.55 us
    all_to_all x1, starting transfers between devices, body(): parts = lax.all_to_all(part, 'mp', 0, 0)  3.39 us
  transfers between devices with their start and end apart: 3, of which 3 were waited for; matrix products, arithmetic and copies ran while one was open for 1% of the time, Pallas kernels for 0%

profile of v1, /device:TPU:1, one launch (start us, length us, event | category | flops | bytes accessed | tf_op | source)
XLA Modules:
  0.0 93.0 jit_solution(17604306035348526474)
XLA Ops:
  0.6 0.7 reduce
  1.4 0.1 broadcast_in_dim.9
  1.4 0.5 broadcast.3
  1.9 0.9 reduce.2
  2.8 0.6 reshape.35
  3.5 6.8 %all-to-all-start = ((bf16[16,2,768]{2,1,0:T(2,128)(2,1)}), bf16[16,2,768]{2,1,0:T(2,128)(2,1)S(1)}, u32[]{:S(2)}, u32[]{:S(2)}) async-start(bf16[16,2,768]{2,1,0:T(2,128)(2,1)} %reshape.35), calls=%async_computation | async-start | bytes 98304 | tf_op jit(solution)/shard_map/all_to_all | solution.py:232
  10.3 0.7 reshape.27.gain_ref
  11.0 5.1 %all-to-all-done = bf16[16,2,768]{2,1,0:T(2,128)(2,1)S(1)} async-done(((bf16[16,2,768]{2,1,0:T(2,128)(2,1)}), bf16[16,2,768]{2,1,0:T(2,128)(2,1)S(1)}, u32[]{:S(2)}, u32[]{:S(2)}) %all-to-all-start) | async-done | bytes 49184 | tf_op jit(solution)/shard_map/all_to_all | solution.py:232
  16.2 0.0 copy-start.5
  16.2 0.9 copy-done.5
  17.1 0.4 shard_map.94
  17.5 0.0 copy-start
  17.6 0.0 copy-start.1
  17.6 33.5 %all_to_all.20.g_ref = bf16[8,80,1536]{2,1,0:T(8,128)(2,1)S(1)} all-to-all(bf16[8,80,1536]{2,1,0:T(8,128)(2,1)S(1)} %get-tuple-element.14), channel_id=1, replica_groups=mesh['dp'=16,'mp'=8] {'mp'}, dimensions={0} | all-to-all | bytes 3932160 | tf_op jit(solution)/shard_map/all_to_all | solution.py:241
  51.1 0.0 copy-done
  51.1 0.0 copy-done.1
  51.1 2.1 %shard_map.95 = (bf16[8,8,1536]{2,1,0:T(8,128)(2,1)S(1)}, bf16[3,512,192]{2,1,0:T(8,128)(2,1)S(1)}, bf16[16,64,64]{2,1,0:T(8,128)(2,1)S(1)}, f32[8,192]{1,0:T(8,128)S(1)}) custom-call(bf16[8,80,1536]{2,1,0:T(8,128)(2,1)S(1)} %all_to_all.20.g_ref, bf16[3,192,1536]{2,1,0:T(8,128)(2,1)S(1)} %copy-done.1, bf16[192,1536]{1,0:T(8,128)(2,1)S(1)} %copy-done, ...), custom_call_target="tpu_custom_call" | custom-call | tf_op jit(solution)/shard_map/pallas_call | solution.py:223
  53.2 0.0 copy-start.2
  53.2 0.7 copy-done.2
  53.9 0.0 copy-start.4
  53.9 0.7 copy-done.4
  54.6 3.4 %all-to-all-start.2 = ((bf16[8,8,1536]{2,1,0:T(8,128)(2,1)}), bf16[8,8,1536]{2,1,0:T(8,128)(2,1)S(1)}, u32[]{:S(2)}, u32[]{:S(2)}) async-start(bf16[8,8,1536]{2,1,0:T(8,128)(2,1)} %copy-done.4), calls=%async_computation.2 | async-start | bytes 393216 | tf_op jit(solution)/shard_map/all_to_all | solution.py:248
  59.3 6.1 %all-to-all-done.2.part_ref = bf16[8,8,1536]{2,1,0:T(8,128)(2,1)S(1)} async-done(((bf16[8,8,1536]{2,1,0:T(8,128)(2,1)}), bf16[8,8,1536]{2,1,0:T(8,128)(2,1)S(1)}, u32[]{:S(2)}, u32[]{:S(2)}) %all-to-all-start.2) | async-done | bytes 196640 | tf_op jit(solution)/shard_map/all_to_all | solution.py:248
  65.4 0.0 copy-start.3
  65.4 0.9 %copy-done.3 = bf16[16,64,64]{2,1,0:T(8,128)(2,1)S(1)} copy-done((bf16[16,64,64]{2,1,0:T(8,128)(2,1)S(1)}, bf16[16,64,64]{2,1,0:T(8,128)(2,1)}, u32[]{:S(2)}) %copy-start.3) | copy-done | bytes 131096
  66.4 3.6 %shard_map.96 = (bf16[8,400,128]{2,1,0:T(8,128)(2,1)S(1)}, bf16[8,400,128]{2,1,0:T(8,128)(2,1)S(1)}) custom-call(bf16[8,80,1536]{2,1,0:T(8,128)(2,1)S(1)} %all_to_all.20.g_ref, bf16[8,8,1536]{2,1,0:T(8,128)(2,1)S(1)} %all-to-all-done.2.part_ref, bf16[3,512,192]{2,1,0:T(8,128)(2,1)S(1)} %get-tuple-element.17.qkv_ref, bf16[16,64,64]{2,1,0:T(8,128)(2,1)S(1)} %copy-done.3, ...), custom_call_target="tpu_custom_call" | custom-call | tf_op jit(solution)/shard_map/pallas_call | solution.py:223
  70.0 2.9 %collective-permute-start = (bf16[8,400,128]{2,1,0:T(8,128)(2,1)S(1)}, bf16[8,400,128]{2,1,0:T(8,128)(2,1)S(1)}, u32[]{:S(2)}, u32[]{:S(2)}) collective-permute-start(bf16[8,400,128]{2,1,0:T(8,128)(2,1)S(1)} %get-tuple-element.21), channel_id=1, source_target_pairs={{0,8},{8,0},{16,24},{24,16},{32,40},{40,32},{48,56},{56,48},{64,72... | collective-permute-start | bytes 2457608 | tf_op jit(solution)/shard_map/ppermute | solution.py:256
  72.9 2.0 %collective-permute-done = bf16[8,400,128]{2,1,0:T(8,128)(2,1)S(1)} collective-permute-done((bf16[8,400,128]{2,1,0:T(8,128)(2,1)S(1)}, bf16[8,400,128]{2,1,0:T(8,128)(2,1)S(1)}, u32[]{:S(2)}, u32[]{:S(2)}) %collective-permute-start) | collective-permute-done | bytes 819232 | tf_op jit(solution)/shard_map/ppermute | solution.py:256
  74.9 0.2 add_convert_fusion
  75.1 15.7 %all_to_all.21.r_ref = bf16[8,400,128]{2,1,0:T(8,128)(2,1)S(1)} all-to-all(bf16[8,400,128]{2,1,0:T(8,128)(2,1)S(1)} %add_convert_fusion), channel_id=1, replica_groups={{0,16,32,48,64,80,96,112},{8,24,40,56,72,88,104,120},{1,17,33,49,65,81,..., dimensions={0} | all-to-all | bytes 1638400 | tf_op jit(solution)/shard_map/all_to_all | solution.py:258
  90.8 1.6 %shard_map.97 = (f32[12,128]{1,0:T(8,128)S(1)}, f32[3,192,96]{2,1,0:T(8,128)}, f32[192,96]{1,0:T(8,128)}) custom-call(bf16[8,400,128]{2,1,0:T(8,128)(2,1)S(1)} %all_to_all.21.r_ref, bf16[12,128]{1,0:T(8,128)(2,1)S(1)} %bitcast.14), custom_call_target="tpu_custom_call" | custom-call | tf_op jit(solution)/shard_map/pallas_call | solution.py:223
  92.4 0.6 copy.15
  (2 shorter events, 0.0 us)
Async XLA Ops:
  3.5 12.6 %all-to-all-start = ((bf16[16,2,768]{2,1,0:T(2,128)(2,1)}), bf16[16,2,768]{2,1,0:T(2,128)(2,1)S(1)}, u32[]{:S(2)}, u32[]{:S(2)}) async-start(bf16[16,2,768]{2,1,0:T(2,128)(2,1)} %reshape.35), calls=%async_computation | async-start | bytes 98304 | tf_op jit(solution)/shard_map/all_to_all | solution.py:232
  16.2 0.9 copy-start.5
  17.5 33.6 %copy-start = (bf16[192,1536]{1,0:T(8,128)(2,1)S(1)}, bf16[192,1536]{1,0:T(8,128)(2,1)}, u32[]{:S(2)}) copy-start(bf16[192,1536]{1,0:T(8,128)(2,1)} %wo_ref.3) | copy-start | bytes 1769476
  17.6 33.5 %copy-start.1 = (bf16[3,192,1536]{2,1,0:T(8,128)(2,1)S(1)}, bf16[3,192,1536]{2,1,0:T(8,128)(2,1)}, u32[]{:S(2)}) copy-start(bf16[3,192,1536]{2,1,0:T(8,128)(2,1)} %w_ref.1) | copy-start | bytes 5308420
  53.2 0.7 copy-start.2
  53.9 0.7 copy-start.4
  54.6 10.8 %all-to-all-start.2 = ((bf16[8,8,1536]{2,1,0:T(8,128)(2,1)}), bf16[8,8,1536]{2,1,0:T(8,128)(2,1)S(1)}, u32[]{:S(2)}, u32[]{:S(2)}) async-start(bf16[8,8,1536]{2,1,0:T(8,128)(2,1)} %copy-done.4), calls=%async_computation.2 | async-start | bytes 393216 | tf_op jit(solution)/shard_map/all_to_all | solution.py:248
  65.4 1.0 %copy-start.3 = (bf16[16,64,64]{2,1,0:T(8,128)(2,1)S(1)}, bf16[16,64,64]{2,1,0:T(8,128)(2,1)}, u32[]{:S(2)}) copy-start(bf16[16,64,64]{2,1,0:T(8,128)(2,1)} %copy-done.2) | copy-start | bytes 393220
  70.0 4.9 %collective-permute-start = (bf16[8,400,128]{2,1,0:T(8,128)(2,1)S(1)}, bf16[8,400,128]{2,1,0:T(8,128)(2,1)S(1)}, u32[]{:S(2)}, u32[]{:S(2)}) collective-permute-start(bf16[8,400,128]{2,1,0:T(8,128)(2,1)S(1)} %get-tuple-element.21), channel_id=1, source_target_pairs={{0,8},{8,0},{16,24},{24,16},{32,40},{40,32},{48,56},{56,48},{64,72... | collective-permute-start | bytes 2457608 | tf_op jit(solution)/shard_map/ppermute | solution.py:256

commit v2 on v1

--- a/solution.py
+++ b/solution.py
@@ -42,28 +42,34 @@
     return lax.broadcasted_iota(jnp.int32, shape, len(shape) - 1)
 
 
-def norm_kernel(tok_ref, gain_ref, text_ref, out_ref, sum_ref, rows_ref):
-    gain = gain_ref[...]
+def norm_kernel(tok_ref, gain_ref, text_ref, out_ref, sum_ref, text_out, rows_ref, line_ref):
     total = jnp.zeros((IMG, D), F32)
     for t in range(8):
         x = tok_ref[:, t * D:(t + 1) * D].astype(F32)
         center = x - jnp.mean(x, axis=-1, keepdims=True)
         spread = jnp.mean(center * center, axis=-1, keepdims=True)
-        row = center * lax.rsqrt(spread + EPS) * gain
+        row = center * lax.rsqrt(spread + EPS)
         for i in range(12):
-            rows_ref[pl.ds(i * 64 + t, IMG, stride=8), :] = row[:, i * 128:(i + 1) * 128]
+            rows_ref[pl.ds(i * 64 + t, IMG, stride=8), :] = (
+                row[:, i * 128:(i + 1) * 128] * gain_ref[i:i + 1, :]
+            )
         total = total + x
     sum_ref[...] = total
-    normed = jnp.concatenate([rows_ref[i * 64:(i + 1) * 64, :] for i in range(12)], axis=1)
-    normed = normed.astype(BF16)
-    text = text_ref[...]
-    for d in range(MP):
-        out_ref[d, 0:64, :] = normed
-        out_ref[d, 64:80, :] = text
-
-
-def forward_kernel(g_ref, w_ref, wo_ref, sum_ref, part_ref, qkv_ref, probs_ref, att_ref, wide_ref):
-    normed = g_ref[:, 0:64, :].reshape(512, D)
+    out_ref[...] = jnp.concatenate(
+        [rows_ref[i * 64:(i + 1) * 64, :] for i in range(12)], axis=1
+    ).astype(BF16)
+    line_ref[...] = jnp.zeros_like(line_ref)
+    for i in range(12):
+        line_ref[i:i + 1, :] = text_ref[:, i * 128:(i + 1) * 128].astype(F32)
+    line = line_ref[...].astype(BF16)
+    for d in range(DP):
+        text_out[d] = line
+
+
+def forward_kernel(*refs):
+    shards, (w_ref, wo_ref, sum_ref, text_ref), refs = refs[:MP], refs[MP:MP + 4], refs[MP + 4:]
+    part_ref, qkv_ref, probs_ref, att_ref, wide_ref, line_ref = refs
+    normed = jnp.concatenate([r[...] for r in shards], axis=0)
     for c in range(3):
         wide_ref[...] = dot(normed, w_ref[c], LAST)
         for b in range(IMG):
@@ -89,24 +95,29 @@
     high, low = pieces(att_ref[...], 2)
     branch = dot(jnp.concatenate([high, low], axis=0), wo_ref[...], (((1,), (0,)), ((), ())))
     part = ((branch[0:8] + branch[8:16] + sum_ref[...]) * (1.0 / TOK)).astype(BF16)
+    line_ref[...] = text_ref[...].astype(F32).reshape(DP * 16, 128)
+    texts = jnp.concatenate(
+        [line_ref[pl.ds(i, DP, stride=16), :] for i in range(12)], axis=1
+    ).astype(BF16)
     for d in range(MP):
-        part_ref[d] = part
-
-
-def backward_kernel(
-    g_ref, part_ref, qkv_ref, probs_ref, att_ref, wo_ref, temp_ref, bias_ref,
-    keep_ref, give_ref, grad_ref, turn_ref, text_ref, both_ref,
-):
+        part_ref[d, 0:16, :] = texts
+        part_ref[d, 16:24, :] = part
+
+
+def backward_kernel(*refs):
+    shards, refs = refs[:MP], refs[MP:]
+    part_ref, qkv_ref, probs_ref, att_ref, wo_ref, temp_ref, bias_ref = refs[:7]
+    keep_ref, give_ref, grad_ref, turn_ref, text_ref, both_ref = refs[7:]
     me = lax.axis_index("dp")
     slot = lax.axis_index("mp")
     core = lax.rem(me, 2)
     pooled = jnp.zeros((IMG, D), F32)
     for s in range(MP):
-        pooled = pooled + part_ref[s].astype(F32)
+        pooled = pooled + part_ref[s, 16:24, :].astype(F32)
     scale = jnp.exp(temp_ref[...])
     image_inv = lax.rsqrt(jnp.sum(pooled * pooled, axis=-1, keepdims=True) + EPS)
     unit = pooled * image_inv
-    text = g_ref[:, 64:80, :].reshape(TEXT, D)
+    text = part_ref[:, 0:16, :].reshape(TEXT, D)
     wide_text = text.astype(F32)
     square = pieces(wide_text * wide_text, 2)
     ones = jnp.ones((IMG, D), BF16)
@@ -168,7 +179,7 @@
     turned = [turn_ref[i * 128:(i + 1) * 128, :].T[0:DH, :] for i in range(2)]
     place = lanes((IMG, 512)) - lax.broadcasted_iota(jnp.int32, (IMG, 512), 0) - core * 256
     spot = jnp.where((place == 208) | (place == 216), 1.0, 0.0).astype(BF16)
-    normed = g_ref[:, 0:64, :].reshape(512, D)
+    normed = jnp.concatenate([r[...] for r in shards], axis=0)
     grads = grad_ref[...].astype(BF16)
     for c in range(4):
         columns = slice(c * 384, (c + 1) * 384)
@@ -185,15 +196,19 @@
     give_ref[...] = both_ref[1 - core]
 
 
-def finish_kernel(r_ref, text_ref, text_out, qkv_out, out_out, stack_ref):
+def finish_kernel(r_ref, text_ref, text_out, qkv_out, out_out, stack_ref, line_ref):
     total = r_ref[0].astype(F32)
     for s in range(1, 8):
         total = total + r_ref[s].astype(F32)
     unit_grad = total[384:396, :]
-    text = text_ref[...].astype(F32)
+    for i in range(12):
+        line_ref[i:i + 1, :] = text_ref[:, i * 128:(i + 1) * 128].astype(F32)
+    text = line_ref[...]
     inv = lax.rsqrt(jnp.sum(text * text, keepdims=True) + EPS)
     unit = text * inv
-    text_out[...] = (unit_grad - unit * jnp.sum(unit * unit_grad, keepdims=True)) * inv
+    line_ref[...] = (unit_grad - unit * jnp.sum(unit * unit_grad, keepdims=True)) * inv
+    for i in range(12):
+        text_out[:, i * 128:(i + 1) * 128] = line_ref[i:i + 1, :]
     pad = jnp.zeros((32, 128), F32)
     for c in range(2):
         for i in range(2):
@@ -228,29 +243,39 @@
     )(*args)
 
 
+def over_mp(block, dz, dy):
+    route = [(i, ((i // 2 + dz) % 4) * 2 + (i % 2 + dy) % 2) for i in range(MP)]
+    return lax.ppermute(block, "mp", route)
+
+
 def body(tokens, norm_gain, qkv_weight, out_weight, text_embed, log_temp, logit_bias):
-    texts = lax.all_to_all(
-        jnp.broadcast_to(text_embed[None], (DP, 1, D)), "dp", 0, 0
-    ).reshape(DP, D)
-    copies, token_sum = call(
+    own, token_sum, text_copies = call(
         norm_kernel,
-        [((MP, 80, D), BF16), ((IMG, D), F32)],
-        [((12 * 64, 128), F32)],
-        tokens, norm_gain.reshape(1, D), texts,
-    )
-    gathered = lax.all_to_all(copies, "mp", 0, 0)
+        [((64, D), BF16), ((IMG, D), F32), ((DP, 16, 128), BF16)],
+        [((12 * 64, 128), F32), ((16, 128), F32)],
+        tokens, norm_gain.reshape(12, 128), text_embed,
+    )
+    across = over_mp(own, 0, 1)
+    ahead = over_mp(own, 1, 0)
+    behind = over_mp(own, 3, 0)
+    far = over_mp(own, 2, 0)
+    texts = lax.all_to_all(text_copies, "dp", 0, 0)
+    shards = [
+        own, across, ahead, behind, far,
+        over_mp(across, 1, 0), over_mp(across, 3, 0), over_mp(far, 0, 1),
+    ]
     part, qkv, probs, attended = call(
         forward_kernel,
-        [((MP, IMG, D), BF16), ((3, 512, WIDTH), BF16), ((16, 64, 64), BF16), ((IMG, WIDTH), F32)],
-        [((512, WIDTH), F32)],
-        gathered, qkv_weight, out_weight, token_sum,
+        [((MP, 24, D), BF16), ((3, 512, WIDTH), BF16), ((16, 64, 64), BF16), ((IMG, WIDTH), F32)],
+        [((512, WIDTH), F32), ((DP * 16, 128), F32)],
+        *shards, qkv_weight, out_weight, token_sum, texts,
     )
     parts = lax.all_to_all(part, "mp", 0, 0)
     keep, give = call(
         backward_kernel,
         [((8, ROWS, 128), BF16)] * 2,
         [((512, 512), F32), ((256, 128), F32), ((256, 128), F32), ((2, 8, ROWS, 128), BF16)],
-        gathered, parts, qkv, probs, attended, out_weight,
+        *shards, parts, qkv, probs, attended, out_weight,
         log_temp.reshape(1, 1), logit_bias.reshape(1, 1),
     )
     other = lax.ppermute(give, "dp", [(i, i ^ 1) for i in range(DP)])
@@ -260,11 +285,11 @@
     )
     text_grad, qkv_grad, out_grad = call(
         finish_kernel,
-        [((12, 128), F32), ((3, WIDTH, 96), F32), ((WIDTH, 96), F32)],
-        [((384, 2048), BF16)],
-        received, text_embed.reshape(12, 128),
-    )
-    return (text_grad.reshape(1, D), qkv_grad, out_grad)
+        [((1, D), F32), ((3, WIDTH, 96), F32), ((WIDTH, 96), F32)],
+        [((384, 2048), BF16), ((12, 128), F32)],
+        received, text_embed,
+    )
+    return (text_grad, qkv_grad, out_grad)
 
 
 def solution(mesh):

time: 93.5 us -> 81.1 us (0.87)
  blocking collectives: 49.3 us -> 29 us
  starting transfers between devices: 13.1 us -> 22.1 us
  other arithmetic: 1.85 us -> 0.21 us
  local copies, waits for them, and re-layouts: 5.82 us -> 7.33 us
    all_to_all x1, blocking collectives: 33.5 us -> 13.3 us  [body(): texts = lax.all_to_all(text_copies, 'dp', 0, 0)]
    ppermute x0 -> x7, starting transfers between devices: none -> 14.7 us  [over_mp(): return lax.ppermute(block, 'mp', route)]
    all_to_all x1 -> x0, starting transfers between devices: 6.83 us -> none  [body(): lax.all_to_all(jnp.broadcast_to(text_embed[None], (DP, 1, D)), 'dp', 0, 0)]
    all_to_all x1 -> x0, waiting for transfers between devices: 5.11 us -> none  [body(): lax.all_to_all(jnp.broadcast_to(text_embed[None], (DP, 1, D)), 'dp', 0, 0)]
    all_to_all x1, waiting for transfers between devices: 6.15 us -> 10.1 us  [body(): parts = lax.all_to_all(part, 'mp', 0, 0)]
    unnamed x16 -> x20, local copies, waits for them, and re-layouts: 4.55 us -> 7.33 us
    all_to_all x1, starting transfers between devices: 3.39 us -> 5.47 us  [body(): parts = lax.all_to_all(part, 'mp', 0, 0)]
    ppermute x1, starting transfers between devices: 2.93 us -> 1.93 us  [body(): other = lax.ppermute(give, 'dp', [(i, i ^ 1) for i in range(DP)])]
  transfers between devices with their start and end apart: 3 -> 9, of which waited for: 3 -> 3; matrix products, arithmetic and copies ran while one was open for 1% -> 0% of each run, Pallas kernels for 0% -> 0%
where the time goes in v2:
time: 81.1 us; the launch traced here: 80.6 us
  blocking collectives  29 us (36%)
  starting transfers between devices  22.1 us (27%)
  waiting for transfers between devices  12.3 us (15%)
  Pallas kernels  7.65 us (9%)
  local copies, waits for them, and re-layouts  7.33 us (9%)
  between operations  2 us (2%)
    all_to_all x1, blocking collectives, body(): lax.all_to_all(send, 'dp', 0, 0, axis_index_groups=[list(range(c, DP, 2))...  15.7 us
    ppermute x7, starting transfers between devices, over_mp(): return lax.ppermute(block, 'mp', route)  14.7 us
    all_to_all x1, blocking collectives, body(): texts = lax.all_to_all(text_copies, 'dp', 0, 0)  13.3 us
    all_to_all x1, waiting for transfers between devices, body(): parts = lax.all_to_all(part, 'mp', 0, 0)  10.1 us
    pallas_call x4, Pallas kernels, call(): pl.pallas_call(kernel, out_shape=[jax.ShapeDtypeStruct(*o) for o in outs]...  7.65 us
    unnamed x20, local copies, waits for them, and re-layouts  7.33 us
    all_to_all x1, starting transfers between devices, body(): parts = lax.all_to_all(part, 'mp', 0, 0)  5.47 us
    ppermute x1, waiting for transfers between devices, body(): other = lax.ppermute(give, 'dp', [(i, i ^ 1) for i in range(DP)])  1.96 us
  transfers between devices with their start and end apart: 9, of which 3 were waited for; matrix products, arithmetic and copies ran while one was open for 0% of the time, Pallas kernels for 0%

profile of v2, /device:TPU:1, one launch (start us, length us, event | category | flops | bytes accessed | tf_op | source)
XLA Modules:
  0.0 80.6 jit_solution(14170985315909132724)
XLA Ops:
  0.6 0.0 copy-start.6
  0.6 0.9 %copy-done.6 = bf16[8,12288]{1,0:T(8,128)(2,1)S(1)} copy-done((bf16[8,12288]{1,0:T(8,128)(2,1)S(1)}, bf16[8,12288]{1,0:T(8,128)(2,1)}, u32[]{:S(2)}) %copy-start.6) | copy-done | bytes 196632
  1.6 0.0 copy-start.7
  1.6 0.7 copy-done.7
  2.2 0.0 copy-start.9
  2.3 0.7 copy-done.9
  2.9 0.3 shard_map.94
  3.3 4.5 %collective-permute-start.3 = (bf16[64,1536]{1,0:T(8,128)(2,1)S(1)}, bf16[64,1536]{1,0:T(8,128)(2,1)S(1)}, u32[]{:S(2)}, u32[]{:S(2)}) collective-permute-start(bf16[64,1536]{1,0:T(8,128)(2,1)S(1)} %get-tuple-element.12.refs_0_), channel_id=1, source_target_pairs={{0,4},{1,5},{2,6},{3,7},{4,0},{5,1},{6,2},{7,3},{8,12},{9,13},{10,... | collective-permute-start | bytes 589832 | tf_op jit(solution)/shard_map/ppermute | solution.py:248
  7.8 2.9 %collective-permute-start = (bf16[64,1536]{1,0:T(8,128)(2,1)S(1)}, bf16[64,1536]{1,0:T(8,128)(2,1)S(1)}, u32[]{:S(2)}, u32[]{:S(2)}) collective-permute-start(bf16[64,1536]{1,0:T(8,128)(2,1)S(1)} %get-tuple-element.12.refs_0_), channel_id=1, source_target_pairs={{0,1},{1,0},{2,3},{3,2},{4,5},{5,4},{6,7},{7,6},{8,9},{9,8},{10,11... | collective-permute-start | bytes 589832 | tf_op jit(solution)/shard_map/ppermute | solution.py:248
  10.7 0.4 collective-permute-start.2
  11.1 1.0 %collective-permute-start.1 = (bf16[64,1536]{1,0:T(8,128)(2,1)S(1)}, bf16[64,1536]{1,0:T(8,128)(2,1)S(1)}, u32[]{:S(2)}, u32[]{:S(2)}) collective-permute-start(bf16[64,1536]{1,0:T(8,128)(2,1)S(1)} %get-tuple-element.12.refs_0_), channel_id=1, source_target_pairs={{0,2},{1,3},{2,4},{3,5},{4,6},{5,7},{6,0},{7,1},{8,10},{9,11},{10,... | collective-permute-start | bytes 589832 | tf_op jit(solution)/shard_map/ppermute | solution.py:248
  12.2 0.2 collective-permute-done.3.refs_4_
  12.4 2.9 %collective-permute-start.6 = (bf16[64,1536]{1,0:T(8,128)(2,1)S(1)}, bf16[64,1536]{1,0:T(8,128)(2,1)S(1)}, u32[]{:S(2)}, u32[]{:S(2)}) collective-permute-start(bf16[64,1536]{1,0:T(8,128)(2,1)S(1)} %collective-permute-done.3.refs_4_), channel_id=1, source_target_pairs={{0,1},{1,0},{2,3},{3,2},{4,5},{5,4},{6,7},{7,6},{8,9},{9,8},{10,11... | collective-permute-start | bytes 589832 | tf_op jit(solution)/shard_map/ppermute | solution.py:248
  15.3 0.0 collective-permute-done.refs_1_
  15.3 2.9 %collective-permute-start.5 = (bf16[64,1536]{1,0:T(8,128)(2,1)S(1)}, bf16[64,1536]{1,0:T(8,128)(2,1)S(1)}, u32[]{:S(2)}, u32[]{:S(2)}) collective-permute-start(bf16[64,1536]{1,0:T(8,128)(2,1)S(1)} %collective-permute-done.refs_1_), channel_id=1, source_target_pairs={{0,6},{1,7},{2,0},{3,1},{4,2},{5,3},{6,4},{7,5},{8,14},{9,15},{10,... | collective-permute-start | bytes 589832 | tf_op jit(solution)/shard_map/ppermute | solution.py:248
  18.2 0.0 collective-permute-start.4
  18.2 13.3 %all_to_all.15.refs_11_ = bf16[16,16,128]{2,1,0:T(8,128)(2,1)S(1)} all-to-all(bf16[16,16,128]{2,1,0:T(8,128)(2,1)S(1)} %get-tuple-element.14), channel_id=1, replica_groups=mesh['dp'=16,'mp'=8] {'dp'}, dimensions={0} | all-to-all | bytes 131072 | tf_op jit(solution)/shard_map/all_to_all | solution.py:262
  31.5 0.0 collective-permute-done.2.refs_3_
  31.5 0.0 collective-permute-done.1.refs_2_
  31.5 0.0 collective-permute-done.6.refs_7_
  31.5 0.0 collective-permute-done.5.refs_6_
  31.5 0.0 collective-permute-done.4.refs_5_
  31.5 0.0 copy-start
  31.5 1.1 %copy-done = bf16[192,1536]{1,0:T(8,128)(2,1)S(1)} copy-done((bf16[192,1536]{1,0:T(8,128)(2,1)S(1)}, bf16[192,1536]{1,0:T(8,128)(2,1)}, u32[]{:S(2)}) %copy-start) | copy-done | bytes 589848
  32.6 0.0 copy-start.2
  32.6 1.5 %copy-done.2 = bf16[3,192,1536]{2,1,0:T(8,128)(2,1)S(1)} copy-done((bf16[3,192,1536]{2,1,0:T(8,128)(2,1)S(1)}, bf16[3,192,1536]{2,1,0:T(8,128)(2,1)}, u32[]{:S(2)}) %copy-start.2) | copy-done | bytes 1769496
  34.0 0.0 copy-start.1
  34.0 2.1 %shard_map.95 = (bf16[8,24,1536]{2,1,0:T(8,128)(2,1)S(1)}, bf16[3,512,192]{2,1,0:T(8,128)(2,1)S(1)}, bf16[16,64,64]{2,1,0:T(8,128)(2,1)S(1)}, f32[8,192]{1,0:T(8,128)S(1)}) custom-call(bf16[64,1536]{1,0:T(8,128)(2,1)S(1)} %get-tuple-element.12.refs_0_, bf16[64,1536]{1,0:T(8,128)(2,1)S(1)} %collective-permute-done.refs_1_, ...), custom_call_target="tpu_custom_call" | custom-call | tf_op jit(solution)/shard_map/pallas_call | solution.py:238
  36.1 0.0 copy-start.3
  36.1 0.8 %copy-done.3 = bf16[8,24,1536]{2,1,0:T(8,128)(2,1)} copy-done((bf16[8,24,1536]{2,1,0:T(8,128)(2,1)}, bf16[8,24,1536]{2,1,0:T(8,128)(2,1)S(1)}, u32[]{:S(2)}) %copy-start.3) | copy-done | bytes 589848
  37.0 0.0 copy-start.4
  37.0 0.7 copy-done.4
  37.7 5.5 %all-to-all-start.1 = ((bf16[8,24,1536]{2,1,0:T(8,128)(2,1)}), bf16[8,24,1536]{2,1,0:T(8,128)(2,1)S(1)}, u32[]{:S(2)}, u32[]{:S(2)}) async-start(bf16[8,24,1536]{2,1,0:T(8,128)(2,1)} %copy-done.3), calls=%async_computation.1 | async-start | bytes 1179648 | tf_op jit(solution)/shard_map/all_to_all | solution.py:273
  44.4 10.1 %all-to-all-done.1.refs_8_ = bf16[8,24,1536]{2,1,0:T(8,128)(2,1)S(1)} async-done(((bf16[8,24,1536]{2,1,0:T(8,128)(2,1)}), bf16[8,24,1536]{2,1,0:T(8,128)(2,1)S(1)}, u32[]{:S(2)}, u32[]{:S(2)}) %all-to-all-start.1) | async-done | bytes 589856 | tf_op jit(solution)/shard_map/all_to_all | solution.py:273
  54.5 0.0 copy-done.1
  54.5 0.0 copy-start.5
  54.5 0.9 %copy-done.5 = bf16[16,64,64]{2,1,0:T(8,128)(2,1)S(1)} copy-done((bf16[16,64,64]{2,1,0:T(8,128)(2,1)S(1)}, bf16[16,64,64]{2,1,0:T(8,128)(2,1)}, u32[]{:S(2)}) %copy-start.5) | copy-done | bytes 131096
  55.5 3.6 %shard_map.96 = (bf16[8,400,128]{2,1,0:T(8,128)(2,1)S(1)}, bf16[8,400,128]{2,1,0:T(8,128)(2,1)S(1)}) custom-call(bf16[64,1536]{1,0:T(8,128)(2,1)S(1)} %get-tuple-element.12.refs_0_, bf16[64,1536]{1,0:T(8,128)(2,1)S(1)} %collective-permute-done.refs_1_, bf16[64,1536]{1,0:T(8,128)(2,1)S(1)} %collective-permute-done.1.refs_2_, ...), custom_call_target="tpu_custom_call" | custom-call | tf_op jit(solution)/shard_map/pallas_call | solution.py:238
  59.1 1.9 %collective-permute-start.7 = (bf16[8,400,128]{2,1,0:T(8,128)(2,1)S(1)}, bf16[8,400,128]{2,1,0:T(8,128)(2,1)S(1)}, u32[]{:S(2)}, u32[]{:S(2)}) collective-permute-start(bf16[8,400,128]{2,1,0:T(8,128)(2,1)S(1)} %get-tuple-element.20), channel_id=1, source_target_pairs={{0,8},{8,0},{16,24},{24,16},{32,40},{40,32},{48,56},{56,48},{64,72... | collective-permute-start | bytes 2457608 | tf_op jit(solution)/shard_map/ppermute | solution.py:281
  61.0 2.0 %collective-permute-done.7 = bf16[8,400,128]{2,1,0:T(8,128)(2,1)S(1)} collective-permute-done((bf16[8,400,128]{2,1,0:T(8,128)(2,1)S(1)}, bf16[8,400,128]{2,1,0:T(8,128)(2,1)S(1)}, u32[]{:S(2)}, u32[]{:S(2)}) %collective-permute-start.7) | collective-permute-done | bytes 819232 | tf_op jit(solution)/shard_map/ppermute | solution.py:281
  63.0 0.0 copy-start.8
  63.0 0.2 add_convert_fusion
  63.2 15.7 %all_to_all.16.r_ref = bf16[8,400,128]{2,1,0:T(8,128)(2,1)S(1)} all-to-all(bf16[8,400,128]{2,1,0:T(8,128)(2,1)S(1)} %add_convert_fusion), channel_id=1, replica_groups={{0,16,32,48,64,80,96,112},{8,24,40,56,72,88,104,120},{1,17,33,49,65,81,..., dimensions={0} | all-to-all | bytes 1638400 | tf_op jit(solution)/shard_map/all_to_all | solution.py:283
  79.0 0.0 copy-done.8
  79.0 1.6 %shard_map.97 = (f32[1,1536]{1,0:T(1,128)}, f32[3,192,96]{2,1,0:T(8,128)}, f32[192,96]{1,0:T(8,128)}) custom-call(bf16[8,400,128]{2,1,0:T(8,128)(2,1)S(1)} %all_to_all.16.r_ref, bf16[1,1536]{1,0:T(2,128)(2,1)S(1)} %copy-done.8), custom_call_target="tpu_custom_call" | custom-call | tf_op jit(solution)/shard_map/pallas_call | solution.py:238
Async XLA Ops:
  0.6 0.9 %copy-start.6 = (bf16[8,12288]{1,0:T(8,128)(2,1)S(1)}, bf16[8,12288]{1,0:T(8,128)(2,1)}, u32[]{:S(2)}) copy-start(bf16[8,12288]{1,0:T(8,128)(2,1)} %tok_ref.1) | copy-start | bytes 589828
  1.6 0.7 copy-start.7
  2.2 0.7 copy-start.9
  3.3 9.1 %collective-permute-start.3 = (bf16[64,1536]{1,0:T(8,128)(2,1)S(1)}, bf16[64,1536]{1,0:T(8,128)(2,1)S(1)}, u32[]{:S(2)}, u32[]{:S(2)}) collective-permute-start(bf16[64,1536]{1,0:T(8,128)(2,1)S(1)} %get-tuple-element.12.refs_0_), channel_id=1, source_target_pairs={{0,4},{1,5},{2,6},{3,7},{4,0},{5,1},{6,2},{7,3},{8,12},{9,13},{10,... | collective-permute-start | bytes 589832 | tf_op jit(solution)/shard_map/ppermute | solution.py:248
  7.8 7.5 %collective-permute-start = (bf16[64,1536]{1,0:T(8,128)(2,1)S(1)}, bf16[64,1536]{1,0:T(8,128)(2,1)S(1)}, u32[]{:S(2)}, u32[]{:S(2)}) collective-permute-start(bf16[64,1536]{1,0:T(8,128)(2,1)S(1)} %get-tuple-element.12.refs_0_), channel_id=1, source_target_pairs={{0,1},{1,0},{2,3},{3,2},{4,5},{5,4},{6,7},{7,6},{8,9},{9,8},{10,11... | collective-permute-start | bytes 589832 | tf_op jit(solution)/shard_map/ppermute | solution.py:248
  10.7 20.8 %collective-permute-start.2 = (bf16[64,1536]{1,0:T(8,128)(2,1)S(1)}, bf16[64,1536]{1,0:T(8,128)(2,1)S(1)}, u32[]{:S(2)}, u32[]{:S(2)}) collective-permute-start(bf16[64,1536]{1,0:T(8,128)(2,1)S(1)} %get-tuple-element.12.refs_0_), channel_id=1, source_target_pairs={{0,6},{1,7},{2,0},{3,1},{4,2},{5,3},{6,4},{7,5},{8,14},{9,15},{10,... | collective-permute-start | bytes 589832 | tf_op jit(solution)/shard_map/ppermute | solution.py:248
  11.1 20.3 %collective-permute-start.1 = (bf16[64,1536]{1,0:T(8,128)(2,1)S(1)}, bf16[64,1536]{1,0:T(8,128)(2,1)S(1)}, u32[]{:S(2)}, u32[]{:S(2)}) collective-permute-start(bf16[64,1536]{1,0:T(8,128)(2,1)S(1)} %get-tuple-element.12.refs_0_), channel_id=1, source_target_pairs={{0,2},{1,3},{2,4},{3,5},{4,6},{5,7},{6,0},{7,1},{8,10},{9,11},{10,... | collective-permute-start | bytes 589832 | tf_op jit(solution)/shard_map/ppermute | solution.py:248
  12.4 19.1 %collective-permute-start.6 = (bf16[64,1536]{1,0:T(8,128)(2,1)S(1)}, bf16[64,1536]{1,0:T(8,128)(2,1)S(1)}, u32[]{:S(2)}, u32[]{:S(2)}) collective-permute-start(bf16[64,1536]{1,0:T(8,128)(2,1)S(1)} %collective-permute-done.3.refs_4_), channel_id=1, source_target_pairs={{0,1},{1,0},{2,3},{3,2},{4,5},{5,4},{6,7},{7,6},{8,9},{9,8},{10,11... | collective-permute-start | bytes 589832 | tf_op jit(solution)/shard_map/ppermute | solution.py:248
  15.3 16.2 %collective-permute-start.5 = (bf16[64,1536]{1,0:T(8,128)(2,1)S(1)}, bf16[64,1536]{1,0:T(8,128)(2,1)S(1)}, u32[]{:S(2)}, u32[]{:S(2)}) collective-permute-start(bf16[64,1536]{1,0:T(8,128)(2,1)S(1)} %collective-permute-done.refs_1_), channel_id=1, source_target_pairs={{0,6},{1,7},{2,0},{3,1},{4,2},{5,3},{6,4},{7,5},{8,14},{9,15},{10,... | collective-permute-start | bytes 589832 | tf_op jit(solution)/shard_map/ppermute | solution.py:248
  18.2 13.3 %collective-permute-start.4 = (bf16[64,1536]{1,0:T(8,128)(2,1)S(1)}, bf16[64,1536]{1,0:T(8,128)(2,1)S(1)}, u32[]{:S(2)}, u32[]{:S(2)}) collective-permute-start(bf16[64,1536]{1,0:T(8,128)(2,1)S(1)} %collective-permute-done.refs_1_), channel_id=1, source_target_pairs={{0,2},{1,3},{2,4},{3,5},{4,6},{5,7},{6,0},{7,1},{8,10},{9,11},{10,... | collective-permute-start | bytes 589832 | tf_op jit(solution)/shard_map/ppermute | solution.py:248
  31.5 1.1 %copy-start = (bf16[192,1536]{1,0:T(8,128)(2,1)S(1)}, bf16[192,1536]{1,0:T(8,128)(2,1)}, u32[]{:S(2)}) copy-start(bf16[192,1536]{1,0:T(8,128)(2,1)} %refs_12_.1) | copy-start | bytes 1769476
  32.6 1.5 %copy-start.2 = (bf16[3,192,1536]{2,1,0:T(8,128)(2,1)S(1)}, bf16[3,192,1536]{2,1,0:T(8,128)(2,1)}, u32[]{:S(2)}) copy-start(bf16[3,192,1536]{2,1,0:T(8,128)(2,1)} %refs_8_.1) | copy-start | bytes 5308420
  34.0 20.5 %copy-start.1 = (bf16[192,1536]{1,0:T(8,128)(2,1)S(1)}, bf16[192,1536]{1,0:T(8,128)(2,1)}, u32[]{:S(2)}) copy-start(bf16[192,1536]{1,0:T(8,128)(2,1)} %refs_12_.1) | copy-start | bytes 1769476
  36.1 0.8 %copy-start.3 = (bf16[8,24,1536]{2,1,0:T(8,128)(2,1)}, bf16[8,24,1536]{2,1,0:T(8,128)(2,1)S(1)}, u32[]{:S(2)}) copy-start(bf16[8,24,1536]{2,1,0:T(8,128)(2,1)S(1)} %get-tuple-element.15) | copy-start | bytes 1769476
  37.0 0.7 copy-start.4
  37.7 16.9 %all-to-all-start.1 = ((bf16[8,24,1536]{2,1,0:T(8,128)(2,1)}), bf16[8,24,1536]{2,1,0:T(8,128)(2,1)S(1)}, u32[]{:S(2)}, u32[]{:S(2)}) async-start(bf16[8,24,1536]{2,1,0:T(8,128)(2,1)} %copy-done.3), calls=%async_computation.1 | async-start | bytes 1179648 | tf_op jit(solution)/shard_map/all_to_all | solution.py:273
  54.5 1.0 %copy-start.5 = (bf16[16,64,64]{2,1,0:T(8,128)(2,1)S(1)}, bf16[16,64,64]{2,1,0:T(8,128)(2,1)}, u32[]{:S(2)}) copy-start(bf16[16,64,64]{2,1,0:T(8,128)(2,1)} %copy-done.4) | copy-start | bytes 393220
  59.1 3.9 %collective-permute-start.7 = (bf16[8,400,128]{2,1,0:T(8,128)(2,1)S(1)}, bf16[8,400,128]{2,1,0:T(8,128)(2,1)S(1)}, u32[]{:S(2)}, u32[]{:S(2)}) collective-permute-start(bf16[8,400,128]{2,1,0:T(8,128)(2,1)S(1)} %get-tuple-element.20), channel_id=1, source_target_pairs={{0,8},{8,0},{16,24},{24,16},{32,40},{40,32},{48,56},{56,48},{64,72... | collective-permute-start | bytes 2457608 | tf_op jit(solution)/shard_map/ppermute | solution.py:281
  63.0 16.0 %copy-start.8 = (bf16[1,1536]{1,0:T(2,128)(2,1)S(1)}, bf16[1,1536]{1,0:T(2,128)(2,1)}, u32[]{:S(2)}) copy-start(bf16[1,1536]{1,0:T(2,128)(2,1)} %text_ref.3) | copy-start | bytes 9220

commit v3 on v2

--- a/solution.py
+++ b/solution.py
@@ -22,6 +22,7 @@
 ROWS = 400
 LAST = (((1,), (1,)), ((), ()))
 FIRST = (((0,), (0,)), ((), ()))
+FULL = 48 * 1024 * 1024
 PARAMS = pltpu.CompilerParams(vmem_limit_bytes=48 * 1024 * 1024)
 
 
@@ -42,7 +43,16 @@
     return lax.broadcasted_iota(jnp.int32, shape, len(shape) - 1)
 
 
-def norm_kernel(tok_ref, gain_ref, text_ref, out_ref, sum_ref, text_out, rows_ref, line_ref):
+def line_kernel(text_ref, out_ref, line_ref):
+    line_ref[...] = jnp.zeros_like(line_ref)
+    for i in range(12):
+        line_ref[i:i + 1, :] = text_ref[:, i * 128:(i + 1) * 128].astype(F32)
+    line = line_ref[...].astype(BF16)
+    for d in range(DP):
+        out_ref[d] = line
+
+
+def norm_kernel(tok_ref, gain_ref, out_ref, sum_ref, rows_ref):
     total = jnp.zeros((IMG, D), F32)
     for t in range(8):
         x = tok_ref[:, t * D:(t + 1) * D].astype(F32)
@@ -58,17 +68,13 @@
     out_ref[...] = jnp.concatenate(
         [rows_ref[i * 64:(i + 1) * 64, :] for i in range(12)], axis=1
     ).astype(BF16)
-    line_ref[...] = jnp.zeros_like(line_ref)
-    for i in range(12):
-        line_ref[i:i + 1, :] = text_ref[:, i * 128:(i + 1) * 128].astype(F32)
-    line = line_ref[...].astype(BF16)
-    for d in range(DP):
-        text_out[d] = line
 
 
 def forward_kernel(*refs):
-    shards, (w_ref, wo_ref, sum_ref, text_ref), refs = refs[:MP], refs[MP:MP + 4], refs[MP + 4:]
-    part_ref, qkv_ref, probs_ref, att_ref, wide_ref, line_ref = refs
+    shards, (w_ref, wo_ref, sum_ref, temp_ref, bias_ref), refs = refs[:MP], refs[MP:MP + 5], refs[MP + 5:]
+    part_ref, qkv_ref, probs_ref, att_ref, scalar_ref, wide_ref = refs
+    scalar_ref[0:1, :] = jnp.exp(jnp.full((1, 128), temp_ref[0], F32))
+    scalar_ref[1:2, :] = jnp.full((1, 128), bias_ref[0], F32)
     normed = jnp.concatenate([r[...] for r in shards], axis=0)
     for c in range(3):
         wide_ref[...] = dot(normed, w_ref[c], LAST)
@@ -95,26 +101,31 @@
     high, low = pieces(att_ref[...], 2)
     branch = dot(jnp.concatenate([high, low], axis=0), wo_ref[...], (((1,), (0,)), ((), ())))
     part = ((branch[0:8] + branch[8:16] + sum_ref[...]) * (1.0 / TOK)).astype(BF16)
+    part_ref[...] = part
+
+
+def join_kernel(part_ref, text_ref, out_ref, line_ref):
     line_ref[...] = text_ref[...].astype(F32).reshape(DP * 16, 128)
     texts = jnp.concatenate(
         [line_ref[pl.ds(i, DP, stride=16), :] for i in range(12)], axis=1
     ).astype(BF16)
+    part = part_ref[...]
     for d in range(MP):
-        part_ref[d, 0:16, :] = texts
-        part_ref[d, 16:24, :] = part
+        out_ref[d, 0:16, :] = texts
+        out_ref[d, 16:24, :] = part
 
 
 def backward_kernel(*refs):
     shards, refs = refs[:MP], refs[MP:]
-    part_ref, qkv_ref, probs_ref, att_ref, wo_ref, temp_ref, bias_ref = refs[:7]
-    keep_ref, give_ref, grad_ref, turn_ref, text_ref, both_ref = refs[7:]
+    part_ref, qkv_ref, probs_ref, att_ref, scalar_ref, wo_ref = refs[:6]
+    keep_ref, give_ref, grad_ref, turn_ref, text_ref, both_ref = refs[6:]
     me = lax.axis_index("dp")
     slot = lax.axis_index("mp")
     core = lax.rem(me, 2)
     pooled = jnp.zeros((IMG, D), F32)
     for s in range(MP):
         pooled = pooled + part_ref[s, 16:24, :].astype(F32)
-    scale = jnp.exp(temp_ref[...])
+    scale = scalar_ref[0:1, :]
     image_inv = lax.rsqrt(jnp.sum(pooled * pooled, axis=-1, keepdims=True) + EPS)
     unit = pooled * image_inv
     text = part_ref[:, 0:16, :].reshape(TEXT, D)
@@ -124,7 +135,7 @@
     text_inv = lax.rsqrt(dot(ones, square[0], LAST) + dot(ones, square[1], LAST) + EPS)
     cosine = dot(jnp.concatenate(pieces(unit, 3), axis=0), text, LAST)
     cosine = (cosine[0:8] + cosine[8:16] + cosine[16:24]) * text_inv
-    logits = scale * cosine + bias_ref[...]
+    logits = scale * cosine + scalar_ref[1:2, :]
     image_row = lax.broadcasted_iota(jnp.int32, (IMG, TEXT), 0)
     own = lanes((IMG, TEXT)) == image_row * DP + me
     pair = scale * (jax.nn.sigmoid(logits) - jnp.where(own, 1.0, 0.0))
@@ -234,12 +245,19 @@
     out_out[...] = product[192:384, :]
 
 
-def call(kernel, outs, scratch, *args):
+HERE = pl.BlockSpec(memory_space=pltpu.VMEM)
+ANY = pl.BlockSpec(memory_space=pl.ANY)
+SMEM = pl.BlockSpec(memory_space=pltpu.SMEM)
+
+
+def call(kernel, outs, scratch, *args, specs=None, params=PARAMS):
     return pl.pallas_call(
         kernel,
         out_shape=[jax.ShapeDtypeStruct(*o) for o in outs],
-        scratch_shapes=[pltpu.VMEM(*s) for s in scratch],
-        compiler_params=PARAMS,
+        in_specs=specs or [HERE] * len(args),
+        out_specs=[HERE] * len(outs),
+        scratch_shapes=[pltpu.VMEM(*s) if isinstance(s, tuple) else s for s in scratch],
+        compiler_params=params,
     )(*args)
 
 
@@ -249,34 +267,44 @@
 
 
 def body(tokens, norm_gain, qkv_weight, out_weight, text_embed, log_temp, logit_bias):
-    own, token_sum, text_copies = call(
+    own, token_sum = call(
         norm_kernel,
-        [((64, D), BF16), ((IMG, D), F32), ((DP, 16, 128), BF16)],
-        [((12 * 64, 128), F32), ((16, 128), F32)],
-        tokens, norm_gain.reshape(12, 128), text_embed,
+        [((64, D), BF16), ((IMG, D), F32)],
+        [((12 * 64, 128), F32)],
+        tokens, norm_gain.reshape(12, 128),
     )
     across = over_mp(own, 0, 1)
+    far = over_mp(own, 2, 0)
     ahead = over_mp(own, 1, 0)
     behind = over_mp(own, 3, 0)
-    far = over_mp(own, 2, 0)
-    texts = lax.all_to_all(text_copies, "dp", 0, 0)
+    own, text_embed = lax.optimization_barrier((own, text_embed))
+    lines, = call(line_kernel, [((DP, 16, 128), BF16)], [((16, 128), F32)], text_embed)
+    across, lines = lax.optimization_barrier((across, lines))
+    texts = lax.all_to_all(lines, "dp", 0, 0)
     shards = [
         own, across, ahead, behind, far,
         over_mp(across, 1, 0), over_mp(across, 3, 0), over_mp(far, 0, 1),
     ]
-    part, qkv, probs, attended = call(
+    part, qkv, probs, attended, scalars = call(
         forward_kernel,
-        [((MP, 24, D), BF16), ((3, 512, WIDTH), BF16), ((16, 64, 64), BF16), ((IMG, WIDTH), F32)],
-        [((512, WIDTH), F32), ((DP * 16, 128), F32)],
-        *shards, qkv_weight, out_weight, token_sum, texts,
-    )
-    parts = lax.all_to_all(part, "mp", 0, 0)
+        [
+            ((IMG, D), BF16), ((3, 512, WIDTH), BF16), ((16, 64, 64), BF16),
+            ((IMG, WIDTH), F32), ((2, 128), F32),
+        ],
+        [((512, WIDTH), F32)],
+        *shards, qkv_weight, out_weight, token_sum, log_temp, logit_bias,
+        specs=[HERE] * (MP + 3) + [SMEM] * 2,
+        params=pltpu.CompilerParams(vmem_limit_bytes=FULL),
+    )
+    joined, = call(join_kernel, [((MP, 24, D), BF16)], [((DP * 16, 128), F32)], part, texts)
+    parts = lax.all_to_all(joined, "mp", 0, 0)
     keep, give = call(
         backward_kernel,
         [((8, ROWS, 128), BF16)] * 2,
-        [((512, 512), F32), ((256, 128), F32), ((256, 128), F32), ((2, 8, ROWS, 128), BF16)],
-        *shards, parts, qkv, probs, attended, out_weight,
-        log_temp.reshape(1, 1), logit_bias.reshape(1, 1),
+        [
+            ((512, 512), F32), ((256, 128), F32), ((256, 128), F32), ((2, 8, ROWS, 128), BF16),
+        ],
+        *shards, parts, qkv, probs, attended, scalars, out_weight,
     )
     other = lax.ppermute(give, "dp", [(i, i ^ 1) for i in range(DP)])
     send = (keep.astype(F32) + other.astype(F32)).astype(BF16)

time: 81.1 us -> 77.9 us (0.961)
  waiting for transfers between devices: 12.3 us -> 3.48 us
  blocking collectives: 29 us -> 35.9 us
  local copies, waits for them, and re-layouts: 7.33 us -> 4.85 us
    all_to_all x1, waiting for transfers between devices: 10.1 us -> 0.01 us  [body(): texts = lax.all_to_all(lines, 'dp', 0, 0)]
    all_to_all x1, blocking collectives: 13.3 us -> 18.3 us  [body(): parts = lax.all_to_all(joined, 'mp', 0, 0)]
    all_to_all x1, starting transfers between devices: 5.47 us -> 8.95 us  [body(): texts = lax.all_to_all(lines, 'dp', 0, 0)]
    ppermute x7, starting transfers between devices: 14.7 us -> 12 us  [over_mp(): return lax.ppermute(block, 'mp', route)]
    unnamed x20 -> x14, local copies, waits for them, and re-layouts: 7.33 us -> 4.85 us
    all_to_all x1, blocking collectives: 15.7 us -> 17.5 us  [body(): lax.all_to_all(send, 'dp', 0, 0, axis_index_groups=[list(range(c, DP, 2))...]
    ppermute x7, waiting for transfers between devices: 0.26 us -> 1.51 us  [over_mp(): return lax.ppermute(block, 'mp', route)]
    pallas_call x4 -> x6, Pallas kernels: 7.65 us -> 8.43 us  [call(): pl.pallas_call(kernel, out_shape=[jax.ShapeDtypeStruct(*o) for o in outs]...]
  transfers between devices with their start and end apart: 9 -> 9, of which waited for: 3 -> 2; matrix products, arithmetic and copies ran while one was open for 0% -> 0% of each run, Pallas kernels for 0% -> 4%
where the time goes in v3:
time: 77.9 us; the launch traced here: 77.5 us
  blocking collectives  35.9 us (46%)
  starting transfers between devices  22.6 us (29%)
  Pallas kernels  8.43 us (11%)
  local copies, waits for them, and re-layouts  4.85 us (6%)
  waiting for transfers between devices  3.48 us (4%)
  between operations  2.03 us (3%)
    all_to_all x1, blocking collectives, body(): parts = lax.all_to_all(joined, 'mp', 0, 0)  18.3 us
    all_to_all x1, blocking collectives, body(): lax.all_to_all(send, 'dp', 0, 0, axis_index_groups=[list(range(c, DP, 2))...  17.5 us
    ppermute x7, starting transfers between devices, over_mp(): return lax.ppermute(block, 'mp', route)  12 us
    all_to_all x1, starting transfers between devices, body(): texts = lax.all_to_all(lines, 'dp', 0, 0)  8.95 us
    pallas_call x6, Pallas kernels, call(): pl.pallas_call(kernel, out_shape=[jax.ShapeDtypeStruct(*o) for o in outs]...  8.43 us
    unnamed x14, local copies, waits for them, and re-layouts  4.85 us
    ppermute x1, waiting for transfers between devices, body(): other = lax.ppermute(give, 'dp', [(i, i ^ 1) for i in range(DP)])  1.96 us
    ppermute x1, starting transfers between devices, body(): other = lax.ppermute(give, 'dp', [(i, i ^ 1) for i in range(DP)])  1.63 us
  transfers between devices with their start and end apart: 9, of which 2 were waited for; matrix products, arithmetic and copies ran while one was open for 0% of the time, Pallas kernels for 4%

profile of v3, /device:TPU:1, one launch (start us, length us, event | category | flops | bytes accessed | tf_op | source)
XLA Modules:
  0.0 77.5 jit_solution(12538734254143023409)
XLA Ops:
  0.6 0.0 copy-start.3
  0.6 0.9 %copy-done.3 = bf16[8,12288]{1,0:T(8,128)(2,1)S(1)} copy-done((bf16[8,12288]{1,0:T(8,128)(2,1)S(1)}, bf16[8,12288]{1,0:T(8,128)(2,1)}, u32[]{:S(2)}) %copy-start.3) | copy-done | bytes 196632
  1.6 0.0 copy-start.6
  1.6 0.7 copy-done.6
  2.3 0.3 shard_map.94
  2.6 3.8 %collective-permute-start = (bf16[64,1536]{1,0:T(8,128)(2,1)S(1)}, bf16[64,1536]{1,0:T(8,128)(2,1)S(1)}, u32[]{:S(2)}, u32[]{:S(2)}) collective-permute-start(bf16[64,1536]{1,0:T(8,128)(2,1)S(1)} %get-tuple-element.17.refs_0_), channel_id=1, source_target_pairs={{0,1},{1,0},{2,3},{3,2},{4,5},{5,4},{6,7},{7,6},{8,9},{9,8},{10,11... | collective-permute-start | bytes 589832 | tf_op jit(solution)/shard_map/ppermute | solution.py:266
  6.4 3.6 %collective-permute-start.3 = (bf16[64,1536]{1,0:T(8,128)(2,1)S(1)}, bf16[64,1536]{1,0:T(8,128)(2,1)S(1)}, u32[]{:S(2)}, u32[]{:S(2)}) collective-permute-start(bf16[64,1536]{1,0:T(8,128)(2,1)S(1)} %get-tuple-element.17.refs_0_), channel_id=1, source_target_pairs={{0,4},{1,5},{2,6},{3,7},{4,0},{5,1},{6,2},{7,3},{8,12},{9,13},{10,... | collective-permute-start | bytes 589832 | tf_op jit(solution)/shard_map/ppermute | solution.py:266
  10.0 0.4 collective-permute-start.2
  10.4 1.0 %collective-permute-start.1 = (bf16[64,1536]{1,0:T(8,128)(2,1)S(1)}, bf16[64,1536]{1,0:T(8,128)(2,1)S(1)}, u32[]{:S(2)}, u32[]{:S(2)}) collective-permute-start(bf16[64,1536]{1,0:T(8,128)(2,1)S(1)} %get-tuple-element.17.refs_0_), channel_id=1, source_target_pairs={{0,2},{1,3},{2,4},{3,5},{4,6},{5,7},{6,0},{7,1},{8,10},{9,11},{10,... | collective-permute-start | bytes 589832 | tf_op jit(solution)/shard_map/ppermute | solution.py:266
  11.5 0.0 copy-start.4
  11.5 0.7 copy-done.4
  12.2 0.6 shard_map.95
  12.8 0.0 collective-permute-done.refs_1_
  12.8 1.5 %collective-permute-done.3.refs_4_ = bf16[64,1536]{1,0:T(8,128)(2,1)S(1)} collective-permute-done((bf16[64,1536]{1,0:T(8,128)(2,1)S(1)}, bf16[64,1536]{1,0:T(8,128)(2,1)S(1)}, u32[]{:S(2)}, u32[]{:S(2)}) %collective-permute-start.3) | collective-permute-done | bytes 196640 | tf_op jit(solution)/shard_map/ppermute | solution.py:266
  14.3 0.1 collective-permute-start.6
  14.4 3.0 %collective-permute-start.5 = (bf16[64,1536]{1,0:T(8,128)(2,1)S(1)}, bf16[64,1536]{1,0:T(8,128)(2,1)S(1)}, u32[]{:S(2)}, u32[]{:S(2)}) collective-permute-start(bf16[64,1536]{1,0:T(8,128)(2,1)S(1)} %collective-permute-done.refs_1_), channel_id=1, source_target_pairs={{0,6},{1,7},{2,0},{3,1},{4,2},{5,3},{6,4},{7,5},{8,14},{9,15},{10,... | collective-permute-start | bytes 589832 | tf_op jit(solution)/shard_map/ppermute | solution.py:266
  17.4 0.0 collective-permute-start.4
  17.4 8.9 %all-to-all-start = ((bf16[16,16,128]{2,1,0:T(8,128)(2,1)}), bf16[16,16,128]{2,1,0:T(8,128)(2,1)S(1)}, u32[]{:S(2)}, u32[]{:S(2)}) async-start(bf16[16,16,128]{2,1,0:T(8,128)(2,1)} %shard_map.95), calls=%async_computation | async-start | bytes 131072 | tf_op jit(solution)/shard_map/all_to_all | solution.py:283
  27.7 0.0 collective-permute-done.2.refs_3_
  27.7 0.0 collective-permute-done.1.refs_2_
  27.7 0.0 collective-permute-done.6.refs_7_
  27.7 0.0 collective-permute-done.5.refs_6_
  27.7 0.0 collective-permute-done.4.refs_5_
  27.7 0.0 copy-start
  27.8 1.1 %copy-done = bf16[192,1536]{1,0:T(8,128)(2,1)S(1)} copy-done((bf16[192,1536]{1,0:T(8,128)(2,1)S(1)}, bf16[192,1536]{1,0:T(8,128)(2,1)}, u32[]{:S(2)}) %copy-start) | copy-done | bytes 589848
  28.8 0.0 copy-start.2
  28.8 1.5 %copy-done.2 = bf16[3,192,1536]{2,1,0:T(8,128)(2,1)S(1)} copy-done((bf16[3,192,1536]{2,1,0:T(8,128)(2,1)S(1)}, bf16[3,192,1536]{2,1,0:T(8,128)(2,1)}, u32[]{:S(2)}) %copy-start.2) | copy-done | bytes 1769496
  30.3 2.1 %shard_map.96 = (bf16[8,1536]{1,0:T(8,128)(2,1)S(1)}, bf16[3,512,192]{2,1,0:T(8,128)(2,1)S(1)}, bf16[16,64,64]{2,1,0:T(8,128)(2,1)S(1)}, f32[8,192]{1,0:T(8,128)S(1)}, f32[2,128]{1,0:T(2,128)S(1)}) custom-call(bf16[64,1536]{1,0:T(8,128)(2,1)S(1)} %get-tuple-element.17.refs_0_, bf16[64,1536]{1,0:T(8,128)(2,1)S(1)} %collective-permute-done.refs_1_, ...), custom_call_target="tpu_custom_call" | custom-call | tf_op jit(solution)/shard_map/pallas_call | solution.py:254
  32.4 0.0 copy-start.1
  32.4 0.0 all-to-all-done.text_ref
  32.4 0.1 shard_map.97
  32.5 18.3 %all_to_all.15.refs_8_ = bf16[8,24,1536]{2,1,0:T(8,128)(2,1)S(1)} all-to-all(bf16[8,24,1536]{2,1,0:T(8,128)(2,1)S(1)} %shard_map.97), channel_id=1, replica_groups=mesh['dp'=16,'mp'=8] {'mp'}, dimensions={0} | all-to-all | bytes 1179648 | tf_op jit(solution)/shard_map/all_to_all | solution.py:300
  50.8 0.0 copy-done.1
  50.8 3.7 %shard_map.98 = (bf16[8,400,128]{2,1,0:T(8,128)(2,1)S(1)}, bf16[8,400,128]{2,1,0:T(8,128)(2,1)S(1)}) custom-call(bf16[64,1536]{1,0:T(8,128)(2,1)S(1)} %get-tuple-element.17.refs_0_, bf16[64,1536]{1,0:T(8,128)(2,1)S(1)} %collective-permute-done.refs_1_, bf16[64,1536]{1,0:T(8,128)(2,1)S(1)} %collective-permute-done.1.refs_2_, ...), custom_call_target="tpu_custom_call" | custom-call | tf_op jit(solution)/shard_map/pallas_call | solution.py:254
  54.5 1.6 %collective-permute-start.7 = (bf16[8,400,128]{2,1,0:T(8,128)(2,1)S(1)}, bf16[8,400,128]{2,1,0:T(8,128)(2,1)S(1)}, u32[]{:S(2)}, u32[]{:S(2)}) collective-permute-start(bf16[8,400,128]{2,1,0:T(8,128)(2,1)S(1)} %get-tuple-element.28), channel_id=1, source_target_pairs={{0,8},{8,0},{16,24},{24,16},{32,40},{40,32},{48,56},{56,48},{64,72... | collective-permute-start | bytes 2457608 | tf_op jit(solution)/shard_map/ppermute | solution.py:309
  56.1 2.0 %collective-permute-done.7 = bf16[8,400,128]{2,1,0:T(8,128)(2,1)S(1)} collective-permute-done((bf16[8,400,128]{2,1,0:T(8,128)(2,1)S(1)}, bf16[8,400,128]{2,1,0:T(8,128)(2,1)S(1)}, u32[]{:S(2)}, u32[]{:S(2)}) %collective-permute-start.7) | collective-permute-done | bytes 819232 | tf_op jit(solution)/shard_map/ppermute | solution.py:309
  58.1 0.0 copy-start.5
  58.1 0.2 add_convert_fusion
  58.3 17.5 %all_to_all.16.r_ref = bf16[8,400,128]{2,1,0:T(8,128)(2,1)S(1)} all-to-all(bf16[8,400,128]{2,1,0:T(8,128)(2,1)S(1)} %add_convert_fusion), channel_id=1, replica_groups={{0,16,32,48,64,80,96,112},{8,24,40,56,72,88,104,120},{1,17,33,49,65,81,..., dimensions={0} | all-to-all | bytes 1638400 | tf_op jit(solution)/shard_map/all_to_all | solution.py:311
  75.8 0.0 copy-done.5
  75.8 1.6 %shard_map.99 = (f32[1,1536]{1,0:T(1,128)}, f32[3,192,96]{2,1,0:T(8,128)}, f32[192,96]{1,0:T(8,128)}) custom-call(bf16[8,400,128]{2,1,0:T(8,128)(2,1)S(1)} %all_to_all.16.r_ref, bf16[1,1536]{1,0:T(2,128)(2,1)S(1)} %copy-done.5), custom_call_target="tpu_custom_call" | custom-call | tf_op jit(solution)/shard_map/pallas_call | solution.py:254
Async XLA Ops:
  0.6 0.9 %copy-start.3 = (bf16[8,12288]{1,0:T(8,128)(2,1)S(1)}, bf16[8,12288]{1,0:T(8,128)(2,1)}, u32[]{:S(2)}) copy-start(bf16[8,12288]{1,0:T(8,128)(2,1)} %tok_ref.1) | copy-start | bytes 589828
  1.6 0.7 copy-start.6
  2.6 10.2 %collective-permute-start = (bf16[64,1536]{1,0:T(8,128)(2,1)S(1)}, bf16[64,1536]{1,0:T(8,128)(2,1)S(1)}, u32[]{:S(2)}, u32[]{:S(2)}) collective-permute-start(bf16[64,1536]{1,0:T(8,128)(2,1)S(1)} %get-tuple-element.17.refs_0_), channel_id=1, source_target_pairs={{0,1},{1,0},{2,3},{3,2},{4,5},{5,4},{6,7},{7,6},{8,9},{9,8},{10,11... | collective-permute-start | bytes 589832 | tf_op jit(solution)/shard_map/ppermute | solution.py:266
  6.4 7.9 %collective-permute-start.3 = (bf16[64,1536]{1,0:T(8,128)(2,1)S(1)}, bf16[64,1536]{1,0:T(8,128)(2,1)S(1)}, u32[]{:S(2)}, u32[]{:S(2)}) collective-permute-start(bf16[64,1536]{1,0:T(8,128)(2,1)S(1)} %get-tuple-element.17.refs_0_), channel_id=1, source_target_pairs={{0,4},{1,5},{2,6},{3,7},{4,0},{5,1},{6,2},{7,3},{8,12},{9,13},{10,... | collective-permute-start | bytes 589832 | tf_op jit(solution)/shard_map/ppermute | solution.py:266
  10.0 17.7 %collective-permute-start.2 = (bf16[64,1536]{1,0:T(8,128)(2,1)S(1)}, bf16[64,1536]{1,0:T(8,128)(2,1)S(1)}, u32[]{:S(2)}, u32[]{:S(2)}) collective-permute-start(bf16[64,1536]{1,0:T(8,128)(2,1)S(1)} %get-tuple-element.17.refs_0_), channel_id=1, source_target_pairs={{0,6},{1,7},{2,0},{3,1},{4,2},{5,3},{6,4},{7,5},{8,14},{9,15},{10,... | collective-permute-start | bytes 589832 | tf_op jit(solution)/shard_map/ppermute | solution.py:266
  10.4 17.3 %collective-permute-start.1 = (bf16[64,1536]{1,0:T(8,128)(2,1)S(1)}, bf16[64,1536]{1,0:T(8,128)(2,1)S(1)}, u32[]{:S(2)}, u32[]{:S(2)}) collective-permute-start(bf16[64,1536]{1,0:T(8,128)(2,1)S(1)} %get-tuple-element.17.refs_0_), channel_id=1, source_target_pairs={{0,2},{1,3},{2,4},{3,5},{4,6},{5,7},{6,0},{7,1},{8,10},{9,11},{10,... | collective-permute-start | bytes 589832 | tf_op jit(solution)/shard_map/ppermute | solution.py:266
  11.5 0.7 copy-start.4
  14.3 13.4 %collective-permute-start.6 = (bf16[64,1536]{1,0:T(8,128)(2,1)S(1)}, bf16[64,1536]{1,0:T(8,128)(2,1)S(1)}, u32[]{:S(2)}, u32[]{:S(2)}) collective-permute-start(bf16[64,1536]{1,0:T(8,128)(2,1)S(1)} %collective-permute-done.3.refs_4_), channel_id=1, source_target_pairs={{0,1},{1,0},{2,3},{3,2},{4,5},{5,4},{6,7},{7,6},{8,9},{9,8},{10,11... | collective-permute-start | bytes 589832 | tf_op jit(solution)/shard_map/ppermute | solution.py:266
  14.4 13.3 %collective-permute-start.5 = (bf16[64,1536]{1,0:T(8,128)(2,1)S(1)}, bf16[64,1536]{1,0:T(8,128)(2,1)S(1)}, u32[]{:S(2)}, u32[]{:S(2)}) collective-permute-start(bf16[64,1536]{1,0:T(8,128)(2,1)S(1)} %collective-permute-done.refs_1_), channel_id=1, source_target_pairs={{0,6},{1,7},{2,0},{3,1},{4,2},{5,3},{6,4},{7,5},{8,14},{9,15},{10,... | collective-permute-start | bytes 589832 | tf_op jit(solution)/shard_map/ppermute | solution.py:266
  17.4 10.3 %collective-permute-start.4 = (bf16[64,1536]{1,0:T(8,128)(2,1)S(1)}, bf16[64,1536]{1,0:T(8,128)(2,1)S(1)}, u32[]{:S(2)}, u32[]{:S(2)}) collective-permute-start(bf16[64,1536]{1,0:T(8,128)(2,1)S(1)} %collective-permute-done.refs_1_), channel_id=1, source_target_pairs={{0,2},{1,3},{2,4},{3,5},{4,6},{5,7},{6,0},{7,1},{8,10},{9,11},{10,... | collective-permute-start | bytes 589832 | tf_op jit(solution)/shard_map/ppermute | solution.py:266
  17.4 14.9 %all-to-all-start = ((bf16[16,16,128]{2,1,0:T(8,128)(2,1)}), bf16[16,16,128]{2,1,0:T(8,128)(2,1)S(1)}, u32[]{:S(2)}, u32[]{:S(2)}) async-start(bf16[16,16,128]{2,1,0:T(8,128)(2,1)} %shard_map.95), calls=%async_computation | async-start | bytes 131072 | tf_op jit(solution)/shard_map/all_to_all | solution.py:283
  27.7 1.1 %copy-start = (bf16[192,1536]{1,0:T(8,128)(2,1)S(1)}, bf16[192,1536]{1,0:T(8,128)(2,1)}, u32[]{:S(2)}) copy-start(bf16[192,1536]{1,0:T(8,128)(2,1)} %refs_13_.1) | copy-start | bytes 1769476
  28.8 1.5 %copy-start.2 = (bf16[3,192,1536]{2,1,0:T(8,128)(2,1)S(1)}, bf16[3,192,1536]{2,1,0:T(8,128)(2,1)}, u32[]{:S(2)}) copy-start(bf16[3,192,1536]{2,1,0:T(8,128)(2,1)} %refs_8_.1) | copy-start | bytes 5308420
  32.4 18.4 %copy-start.1 = (bf16[192,1536]{1,0:T(8,128)(2,1)S(1)}, bf16[192,1536]{1,0:T(8,128)(2,1)}, u32[]{:S(2)}) copy-start(bf16[192,1536]{1,0:T(8,128)(2,1)} %refs_13_.1) | copy-start | bytes 1769476
  54.5 3.6 %collective-permute-start.7 = (bf16[8,400,128]{2,1,0:T(8,128)(2,1)S(1)}, bf16[8,400,128]{2,1,0:T(8,128)(2,1)S(1)}, u32[]{:S(2)}, u32[]{:S(2)}) collective-permute-start(bf16[8,400,128]{2,1,0:T(8,128)(2,1)S(1)} %get-tuple-element.28), channel_id=1, source_target_pairs={{0,8},{8,0},{16,24},{24,16},{32,40},{40,32},{48,56},{56,48},{64,72... | collective-permute-start | bytes 2457608 | tf_op jit(solution)/shard_map/ppermute | solution.py:309
  58.1 17.8 %copy-start.5 = (bf16[1,1536]{1,0:T(2,128)(2,1)S(1)}, bf16[1,1536]{1,0:T(2,128)(2,1)}, u32[]{:S(2)}) copy-start(bf16[1,1536]{1,0:T(2,128)(2,1)} %text_ref.1) | copy-start | bytes 9220

commit v4 on v3

--- a/solution.py
+++ b/solution.py
@@ -22,7 +22,6 @@
 ROWS = 400
 LAST = (((1,), (1,)), ((), ()))
 FIRST = (((0,), (0,)), ((), ()))
-FULL = 48 * 1024 * 1024
 PARAMS = pltpu.CompilerParams(vmem_limit_bytes=48 * 1024 * 1024)
 
 
@@ -43,16 +42,7 @@
     return lax.broadcasted_iota(jnp.int32, shape, len(shape) - 1)
 
 
-def line_kernel(text_ref, out_ref, line_ref):
-    line_ref[...] = jnp.zeros_like(line_ref)
-    for i in range(12):
-        line_ref[i:i + 1, :] = text_ref[:, i * 128:(i + 1) * 128].astype(F32)
-    line = line_ref[...].astype(BF16)
-    for d in range(DP):
-        out_ref[d] = line
-
-
-def norm_kernel(tok_ref, gain_ref, out_ref, sum_ref, rows_ref):
+def norm_kernel(tok_ref, out_ref, sum_ref, rows_ref):
     total = jnp.zeros((IMG, D), F32)
     for t in range(8):
         x = tok_ref[:, t * D:(t + 1) * D].astype(F32)
@@ -60,22 +50,59 @@
         spread = jnp.mean(center * center, axis=-1, keepdims=True)
         row = center * lax.rsqrt(spread + EPS)
         for i in range(12):
-            rows_ref[pl.ds(i * 64 + t, IMG, stride=8), :] = (
-                row[:, i * 128:(i + 1) * 128] * gain_ref[i:i + 1, :]
-            )
+            rows_ref[pl.ds(i * 64 + t, IMG, stride=8), :] = row[:, i * 128:(i + 1) * 128]
         total = total + x
     sum_ref[...] = total
-    out_ref[...] = jnp.concatenate(
+    out_ref[0:64, :] = jnp.concatenate(
         [rows_ref[i * 64:(i + 1) * 64, :] for i in range(12)], axis=1
     ).astype(BF16)
-
-
-def forward_kernel(*refs):
-    shards, (w_ref, wo_ref, sum_ref, temp_ref, bias_ref), refs = refs[:MP], refs[MP:MP + 5], refs[MP + 5:]
-    part_ref, qkv_ref, probs_ref, att_ref, scalar_ref, wide_ref = refs
+    out_ref[64:72, :] = jnp.zeros((8, D), BF16)
+
+
+def load_kernel(
+    w_hbm, wo_hbm, gain_ref, temp_ref, bias_ref, w_ref, wo_ref, scalar_ref, raw_ref, sems
+):
+    copies = [
+        pltpu.make_async_copy(w_hbm, raw_ref, sems.at[0]),
+        pltpu.make_async_copy(wo_hbm, wo_ref, sems.at[1]),
+    ]
+    for copy in copies:
+        copy.start()
     scalar_ref[0:1, :] = jnp.exp(jnp.full((1, 128), temp_ref[0], F32))
     scalar_ref[1:2, :] = jnp.full((1, 128), bias_ref[0], F32)
-    normed = jnp.concatenate([r[...] for r in shards], axis=0)
+    copies[0].wait()
+    for i in range(12):
+        part = slice(i * 128, (i + 1) * 128)
+        for c in range(3):
+            scaled = raw_ref[c, :, part].astype(F32) * gain_ref[i:i + 1, :]
+            w_ref[c, :, part] = scaled.astype(BF16)
+    copies[1].wait()
+
+
+STEPS = ((0, 0), (0, 1), (1, 0), (3, 0), (2, 0), (1, 1), (3, 1), (2, 1))
+
+
+def source(slot, step):
+    dz, dy = STEPS[step]
+    return lax.rem(lax.div(slot, 2) + 4 - dz, 4) * 2 + lax.rem(lax.rem(slot, 2) + dy, 2)
+
+
+def text_kernel(*refs):
+    shards, (out_ref, line_ref) = refs[:MP], refs[MP:]
+    slot = lax.axis_index("mp")
+    core = lax.rem(lax.axis_index("dp"), 2)
+    for s in range(MP):
+        two = shards[s][64:72, :].astype(F32)
+        for i in range(2):
+            at = lax.rem(core + i, 2) * 8 + source(slot, s)
+            line_ref[pl.ds(at, 1), :] = two[i:i + 1, :]
+    out_ref[...] = line_ref[...].astype(BF16)
+
+
+def forward_kernel(*refs):
+    shards, (w_ref, wo_ref, sum_ref), refs = refs[:MP], refs[MP:MP + 3], refs[MP + 3:]
+    part_ref, qkv_ref, probs_ref, att_ref, wide_ref = refs
+    normed = jnp.concatenate([r[0:64, :] for r in shards], axis=0)
     for c in range(3):
         wide_ref[...] = dot(normed, w_ref[c], LAST)
         for b in range(IMG):
@@ -101,22 +128,12 @@
     high, low = pieces(att_ref[...], 2)
     branch = dot(jnp.concatenate([high, low], axis=0), wo_ref[...], (((1,), (0,)), ((), ())))
     part = ((branch[0:8] + branch[8:16] + sum_ref[...]) * (1.0 / TOK)).astype(BF16)
-    part_ref[...] = part
-
-
-def join_kernel(part_ref, text_ref, out_ref, line_ref):
-    line_ref[...] = text_ref[...].astype(F32).reshape(DP * 16, 128)
-    texts = jnp.concatenate(
-        [line_ref[pl.ds(i, DP, stride=16), :] for i in range(12)], axis=1
-    ).astype(BF16)
-    part = part_ref[...]
     for d in range(MP):
-        out_ref[d, 0:16, :] = texts
-        out_ref[d, 16:24, :] = part
+        part_ref[d] = part
 
 
 def backward_kernel(*refs):
-    shards, refs = refs[:MP], refs[MP:]
+    shards, texts, refs = refs[:MP], refs[MP:MP + 2], refs[MP + 2:]
     part_ref, qkv_ref, probs_ref, att_ref, scalar_ref, wo_ref = refs[:6]
     keep_ref, give_ref, grad_ref, turn_ref, text_ref, both_ref = refs[6:]
     me = lax.axis_index("dp")
@@ -124,11 +141,11 @@
     core = lax.rem(me, 2)
     pooled = jnp.zeros((IMG, D), F32)
     for s in range(MP):
-        pooled = pooled + part_ref[s, 16:24, :].astype(F32)
+        pooled = pooled + part_ref[s].astype(F32)
     scale = scalar_ref[0:1, :]
     image_inv = lax.rsqrt(jnp.sum(pooled * pooled, axis=-1, keepdims=True) + EPS)
     unit = pooled * image_inv
-    text = part_ref[:, 0:16, :].reshape(TEXT, D)
+    text = jnp.concatenate([r[...] for r in texts], axis=0)
     wide_text = text.astype(F32)
     square = pieces(wide_text * wide_text, 2)
     ones = jnp.ones((IMG, D), BF16)
@@ -137,7 +154,7 @@
     cosine = (cosine[0:8] + cosine[8:16] + cosine[16:24]) * text_inv
     logits = scale * cosine + scalar_ref[1:2, :]
     image_row = lax.broadcasted_iota(jnp.int32, (IMG, TEXT), 0)
-    own = lanes((IMG, TEXT)) == image_row * DP + me
+    own = lanes((IMG, TEXT)) == core * MP + image_row
     pair = scale * (jax.nn.sigmoid(logits) - jnp.where(own, 1.0, 0.0))
     unit_grad = dot(
         jnp.concatenate(pieces(pair * text_inv, 3), axis=0), text, (((1,), (0,)), ((), ()))
@@ -145,8 +162,14 @@
     unit_grad = unit_grad[0:8] + unit_grad[8:16] + unit_grad[16:24]
     pooled_grad = (unit_grad - unit * jnp.sum(unit * unit_grad, axis=-1, keepdims=True)) * image_inv
     resid = (pooled_grad * (1.0 / TOK)).astype(BF16)
-    mine = pltpu.roll(pair, lax.rem(TEXT - slot * DP, TEXT), axis=1)
-    pair_high, pair_low = pieces(mine, 2)
+    column = lax.broadcasted_iota(jnp.int32, (TEXT, DP), 0)
+    owner = lanes((TEXT, DP))
+    step_x = lax.rem(lax.rem(lax.div(me, 2), 4) - lax.rem(lax.div(owner, 2), 4) + 4, 4)
+    step_y = lax.rem(lax.div(me, 8) + lax.div(owner, 8), 2)
+    place = step_y * 64 + step_x * 16 + lax.rem(owner, 2) * MP + slot
+    chosen = jnp.where(column == place, 1.0, 0.0).astype(BF16)
+    mine = dot(jnp.concatenate(pieces(pair, 3), axis=0), chosen, (((1,), (0,)), ((), ())))
+    pair_high, pair_low = pieces(mine[0:8] + mine[8:16] + mine[16:24], 2)
     unit_high, unit_low = pieces(unit, 2)
     text_grad = dot(
         jnp.concatenate([pair_high, pair_high, pair_low], axis=0),
@@ -190,7 +213,7 @@
     turned = [turn_ref[i * 128:(i + 1) * 128, :].T[0:DH, :] for i in range(2)]
     place = lanes((IMG, 512)) - lax.broadcasted_iota(jnp.int32, (IMG, 512), 0) - core * 256
     spot = jnp.where((place == 208) | (place == 216), 1.0, 0.0).astype(BF16)
-    normed = jnp.concatenate([r[...] for r in shards], axis=0)
+    normed = jnp.concatenate([r[0:64, :] for r in shards], axis=0)
     grads = grad_ref[...].astype(BF16)
     for c in range(4):
         columns = slice(c * 384, (c + 1) * 384)
@@ -207,7 +230,7 @@
     give_ref[...] = both_ref[1 - core]
 
 
-def finish_kernel(r_ref, text_ref, text_out, qkv_out, out_out, stack_ref, line_ref):
+def finish_kernel(r_ref, text_ref, gain_ref, text_out, qkv_out, out_out, stack_ref, line_ref):
     total = r_ref[0].astype(F32)
     for s in range(1, 8):
         total = total + r_ref[s].astype(F32)
@@ -220,13 +243,19 @@
     line_ref[...] = (unit_grad - unit * jnp.sum(unit * unit_grad, keepdims=True)) * inv
     for i in range(12):
         text_out[:, i * 128:(i + 1) * 128] = line_ref[i:i + 1, :]
+    first = lax.axis_index("dp") * 96
+    shift = lax.rem(first, 128)
+    above = gain_ref[pl.ds(lax.div(first, 128), 1), :]
+    below = gain_ref[pl.ds(jnp.minimum(lax.div(first, 128) + 1, 11), 1), :]
+    gain = jnp.where(lanes((1, 128)) < shift, below, above)
+    gain = pltpu.roll(gain, lax.rem(128 - shift, 128), axis=1)[:, 0:96]
     pad = jnp.zeros((32, 128), F32)
     for c in range(2):
         for i in range(2):
             at = (c * 2 + i) * 96
             turned = jnp.concatenate([total[at:at + 96, :], pad], axis=0).T
             rows = 128 if i == 0 else 64
-            qkv_out[c, i * 128:i * 128 + rows, :] = turned[0:rows, 0:96]
+            qkv_out[c, i * 128:i * 128 + rows, :] = turned[0:rows, 0:96] * gain
     lane = lanes((96, 128))
     group = lax.shift_right_logical(lane, 3) - 8
     factors = []
@@ -234,14 +263,14 @@
         for c in range(2):
             block = r_ref[s, (c * 2 + 1) * 96:(c * 2 + 2) * 96, :]
             factors.append(block)
-            rolled = pltpu.roll(block.astype(F32), 96, axis=1)
+            rolled = pltpu.roll(block.astype(F32), 96, axis=1).astype(BF16)
             for g in range(4):
                 at = (s * 2 + c) * 128
                 stack_ref[g * 96:(g + 1) * 96, at:at + 128] = jnp.where(
-                    group == g, rolled, 0.0
-                ).astype(BF16)
+                    group == g, rolled, jnp.zeros_like(rolled)
+                )
     product = dot(stack_ref[...], jnp.concatenate(factors, axis=1), LAST)
-    qkv_out[2] = product[0:192, :]
+    qkv_out[2] = product[0:192, :] * gain
     out_out[...] = product[192:384, :]
 
 
@@ -266,45 +295,68 @@
     return lax.ppermute(block, "mp", route)
 
 
+def over_dp(block, dy, dx, dc):
+    route = [
+        (i, ((i // 8 + dy) % 2 * 4 + (i // 2 + dx) % 4) * 2 + (i + dc) % 2) for i in range(DP)
+    ]
+    return lax.ppermute(block, "dp", route)
+
+
+def first_step(block):
+    far = over_mp(block, 2, 0)
+    across, ahead, behind = [over_mp(block, dz, dy) for dz, dy in STEPS[1:4]]
+    return [block, across, ahead, behind, far]
+
+
+def second_step(blocks):
+    across, far = blocks[1], blocks[4]
+    return [over_mp(across, 1, 0), over_mp(across, 3, 0), over_mp(far, 0, 1)]
+
+
 def body(tokens, norm_gain, qkv_weight, out_weight, text_embed, log_temp, logit_bias):
     own, token_sum = call(
         norm_kernel,
-        [((64, D), BF16), ((IMG, D), F32)],
+        [((72, D), BF16), ((IMG, D), F32)],
         [((12 * 64, 128), F32)],
-        tokens, norm_gain.reshape(12, 128),
-    )
-    across = over_mp(own, 0, 1)
-    far = over_mp(own, 2, 0)
-    ahead = over_mp(own, 1, 0)
-    behind = over_mp(own, 3, 0)
-    own, text_embed = lax.optimization_barrier((own, text_embed))
-    lines, = call(line_kernel, [((DP, 16, 128), BF16)], [((16, 128), F32)], text_embed)
-    across, lines = lax.optimization_barrier((across, lines))
-    texts = lax.all_to_all(lines, "dp", 0, 0)
-    shards = [
-        own, across, ahead, behind, far,
-        over_mp(across, 1, 0), over_mp(across, 3, 0), over_mp(far, 0, 1),
-    ]
-    part, qkv, probs, attended, scalars = call(
+        tokens,
+    )
+    own = lax.dynamic_update_slice(own, text_embed, (64, 0))
+    own = lax.dynamic_update_slice(own, over_dp(text_embed, 0, 0, 1), (65, 0))
+    shards = first_step(own)
+    shards[1], qkv_weight, out_weight, gain = lax.optimization_barrier(
+        (shards[1], qkv_weight, out_weight, norm_gain)
+    )
+    shards += second_step(shards)
+    qkv_weight, out_weight, scalars = call(
+        load_kernel,
+        [((3, WIDTH, D), BF16), ((WIDTH, D), BF16), ((2, 128), F32)],
+        [((3, WIDTH, D), BF16), pltpu.SemaphoreType.DMA((2,))],
+        qkv_weight, out_weight, gain.reshape(12, 128), log_temp, logit_bias,
+        specs=[ANY, ANY, HERE, SMEM, SMEM],
+    )
+    shards[0], qkv_weight, out_weight = lax.optimization_barrier(
+        (shards[0], qkv_weight, out_weight)
+    )
+    texts, = call(text_kernel, [((16, D), BF16)], [((16, D), F32)], *shards)
+    texts = [texts] + [over_dp(texts, 0, dx, 0) for dx in (1, 2, 3)]
+    part, qkv, probs, attended = call(
         forward_kernel,
         [
-            ((IMG, D), BF16), ((3, 512, WIDTH), BF16), ((16, 64, 64), BF16),
-            ((IMG, WIDTH), F32), ((2, 128), F32),
+            ((MP, IMG, D), BF16), ((3, 512, WIDTH), BF16),
+            ((16, 64, 64), BF16), ((IMG, WIDTH), F32),
         ],
         [((512, WIDTH), F32)],
-        *shards, qkv_weight, out_weight, token_sum, log_temp, logit_bias,
-        specs=[HERE] * (MP + 3) + [SMEM] * 2,
-        params=pltpu.CompilerParams(vmem_limit_bytes=FULL),
-    )
-    joined, = call(join_kernel, [((MP, 24, D), BF16)], [((DP * 16, 128), F32)], part, texts)
-    parts = lax.all_to_all(joined, "mp", 0, 0)
+        *shards, qkv_weight, out_weight, token_sum,
+    )
+    part, *texts = lax.optimization_barrier((part, *texts))
+    texts = jnp.concatenate(texts, axis=0)
+    texts = [texts, over_dp(texts, 1, 0, 0)]
+    parts = lax.all_to_all(part, "mp", 0, 0)
     keep, give = call(
         backward_kernel,
         [((8, ROWS, 128), BF16)] * 2,
-        [
-            ((512, 512), F32), ((256, 128), F32), ((256, 128), F32), ((2, 8, ROWS, 128), BF16),
-        ],
-        *shards, parts, qkv, probs, attended, scalars, out_weight,
+        [((512, 512), F32), ((256, 128), F32), ((256, 128), F32), ((2, 8, ROWS, 128), BF16)],
+        *shards, *texts, parts, qkv, probs, attended, scalars, out_weight,
     )
     other = lax.ppermute(give, "dp", [(i, i ^ 1) for i in range(DP)])
     send = (keep.astype(F32) + other.astype(F32)).astype(BF16)
@@ -315,7 +367,7 @@
         finish_kernel,
         [((1, D), F32), ((3, WIDTH, 96), F32), ((WIDTH, 96), F32)],
         [((384, 2048), BF16), ((12, 128), F32)],
-        received, text_embed,
+        received, text_embed, norm_gain.reshape(12, 128),
     )
     return (text_grad, qkv_grad, out_grad)
 

time: 77.9 us -> 76.8 us (0.986)
  blocking collectives: 35.9 us -> 28.7 us
  waiting for transfers between devices: 3.48 us -> 9.2 us
    all_to_all x1 -> x0, starting transfers between devices: 8.95 us -> none  [body(): texts = lax.all_to_all(lines, 'dp', 0, 0)]
    ppermute x0 -> x5, starting transfers between devices: none -> 5.65 us  [over_dp(): return lax.ppermute(block, 'dp', route)]
    all_to_all x1, blocking collectives: 18.3 us -> 13 us  [body(): parts = lax.all_to_all(part, 'mp', 0, 0)]
    ppermute x7, waiting for transfers between devices: 1.51 us -> 5.5 us  [over_mp(): return lax.ppermute(block, 'mp', route)]
    ppermute x1, starting transfers between devices: 1.63 us -> 5.6 us  [body(): other = lax.ppermute(give, 'dp', [(i, i ^ 1) for i in range(DP)])]
    all_to_all x1, blocking collectives: 17.5 us -> 15.7 us  [body(): lax.all_to_all(send, 'dp', 0, 0, axis_index_groups=[list(range(c, DP, 2))...]
    ppermute x0 -> x5, waiting for transfers between devices: none -> 1.74 us  [over_dp(): return lax.ppermute(block, 'dp', route)]
    dynamic_update_slice x0 -> x2, local copies, waits for them, and re-layouts: none -> 0.87 us  [the longest x1 0.78 us: body(): own = lax.dynamic_update_slice(own, text_embed, (64, 0))]
  transfers between devices with their start and end apart: 9 -> 13, of which waited for: 2 -> 6; matrix products, arithmetic and copies ran while one was open for 0% -> 1% of each run, Pallas kernels for 4% -> 4%
where the time goes in v4:
time: 76.8 us; the launch traced here: 76.4 us
  blocking collectives  28.7 us (37%)
  starting transfers between devices  22.5 us (29%)
  waiting for transfers between devices  9.2 us (12%)
  Pallas kernels  8.63 us (11%)
  local copies, waits for them, and re-layouts  5.06 us (7%)
  between operations  2.06 us (3%)
    all_to_all x1, blocking collectives, body(): lax.all_to_all(send, 'dp', 0, 0, axis_index_groups=[list(range(c, DP, 2))...  15.7 us
    all_to_all x1, blocking collectives, body(): parts = lax.all_to_all(part, 'mp', 0, 0)  13 us
    ppermute x7, starting transfers between devices, over_mp(): return lax.ppermute(block, 'mp', route)  11.3 us
    pallas_call x6, Pallas kernels, call(): pl.pallas_call(kernel, out_shape=[jax.ShapeDtypeStruct(*o) for o in outs]...  8.63 us
    ppermute x5, starting transfers between devices, over_dp(): return lax.ppermute(block, 'dp', route)  5.65 us
    ppermute x1, starting transfers between devices, body(): other = lax.ppermute(give, 'dp', [(i, i ^ 1) for i in range(DP)])  5.6 us
    ppermute x7, waiting for transfers between devices, over_mp(): return lax.ppermute(block, 'mp', route)  5.5 us
    unnamed x15, local copies, waits for them, and re-layouts  4.18 us
  transfers between devices with their start and end apart: 13, of which 6 were waited for; matrix products, arithmetic and copies ran while one was open for 1% of the time, Pallas kernels for 4%

profile of v4, /device:TPU:1, one launch (start us, length us, event | category | flops | bytes accessed | tf_op | source)
XLA Modules:
  0.0 76.4 jit_solution(6586006605023827885)
XLA Ops:
  0.6 1.5 %collective-permute-start = (bf16[1,1536]{1,0:T(2,128)(2,1)}, bf16[1,1536]{1,0:T(2,128)(2,1)S(1)}, u32[]{:S(2)}, u32[]{:S(2)}) collective-permute-start(bf16[1,1536]{1,0:T(2,128)(2,1)} %text_ref.1), channel_id=1, source_target_pairs={{0,8},{8,0},{16,24},{24,16},{32,40},{40,32},{48,56},{56,48},{64,72... | collective-permute-start | bytes 9224 | tf_op jit(solution)/shard_map/ppermute | solution.py:302
  2.1 0.0 copy-start.2
  2.1 0.9 %copy-done.2 = bf16[8,12288]{1,0:T(8,128)(2,1)S(1)} copy-done((bf16[8,12288]{1,0:T(8,128)(2,1)S(1)}, bf16[8,12288]{1,0:T(8,128)(2,1)}, u32[]{:S(2)}) %copy-start.2) | copy-done | bytes 196632
  3.1 0.3 shard_map.94
  3.4 0.8 %dynamic_update_slice.6 = bf16[72,1536]{1,0:T(8,128)(2,1)S(1)} dynamic-update-slice(bf16[72,1536]{1,0:T(8,128)(2,1)S(1)} %get-tuple-element.26, bf16[1,1536]{1,0:T(2,128)(2,1)} %text_ref.1, s32[]{:T(128)} %constant.0.clone.1, s32[]{:T(128)} %constant.1.clone.1) | dynamic-update-slice | bytes 6148 | tf_op jit(solution)/shard_map/dynamic_update_slice | solution.py:323
  4.2 0.0 collective-permute-done
  4.2 0.1 dynamic_update_slice.7.refs_0_
  4.3 3.1 %collective-permute-start.1 = (bf16[72,1536]{1,0:T(8,128)(2,1)S(1)}, bf16[72,1536]{1,0:T(8,128)(2,1)S(1)}, u32[]{:S(2)}, u32[]{:S(2)}) collective-permute-start(bf16[72,1536]{1,0:T(8,128)(2,1)S(1)} %dynamic_update_slice.7.refs_0_), channel_id=1, source_target_pairs={{0,1},{1,0},{2,3},{3,2},{4,5},{5,4},{6,7},{7,6},{8,9},{9,8},{10,11... | collective-permute-start | bytes 663560 | tf_op jit(solution)/shard_map/ppermute | solution.py:295
  7.3 3.6 %collective-permute-start.4 = (bf16[72,1536]{1,0:T(8,128)(2,1)S(1)}, bf16[72,1536]{1,0:T(8,128)(2,1)S(1)}, u32[]{:S(2)}, u32[]{:S(2)}) collective-permute-start(bf16[72,1536]{1,0:T(8,128)(2,1)S(1)} %dynamic_update_slice.7.refs_0_), channel_id=1, source_target_pairs={{0,4},{1,5},{2,6},{3,7},{4,0},{5,1},{6,2},{7,3},{8,12},{9,13},{10,... | collective-permute-start | bytes 663560 | tf_op jit(solution)/shard_map/ppermute | solution.py:295
  10.9 0.4 collective-permute-start.3
  11.4 1.0 %collective-permute-start.2 = (bf16[72,1536]{1,0:T(8,128)(2,1)S(1)}, bf16[72,1536]{1,0:T(8,128)(2,1)S(1)}, u32[]{:S(2)}, u32[]{:S(2)}) collective-permute-start(bf16[72,1536]{1,0:T(8,128)(2,1)S(1)} %dynamic_update_slice.7.refs_0_), channel_id=1, source_target_pairs={{0,2},{1,3},{2,4},{3,5},{4,6},{5,7},{6,0},{7,1},{8,10},{9,11},{10,... | collective-permute-start | bytes 663560 | tf_op jit(solution)/shard_map/ppermute | solution.py:295
  12.4 0.6 collective-permute-done.1.refs_1_
  13.0 3.6 %collective-permute-done.4.refs_4_ = bf16[72,1536]{1,0:T(8,128)(2,1)S(1)} collective-permute-done((bf16[72,1536]{1,0:T(8,128)(2,1)S(1)}, bf16[72,1536]{1,0:T(8,128)(2,1)S(1)}, u32[]{:S(2)}, u32[]{:S(2)}) %collective-permute-start.4) | collective-permute-done | bytes 221216 | tf_op jit(solution)/shard_map/ppermute | solution.py:295
  16.5 0.1 collective-permute-start.7
  16.7 3.0 %collective-permute-start.6 = (bf16[72,1536]{1,0:T(8,128)(2,1)S(1)}, bf16[72,1536]{1,0:T(8,128)(2,1)S(1)}, u32[]{:S(2)}, u32[]{:S(2)}) collective-permute-start(bf16[72,1536]{1,0:T(8,128)(2,1)S(1)} %collective-permute-done.1.refs_1_), channel_id=1, source_target_pairs={{0,6},{1,7},{2,0},{3,1},{4,2},{5,3},{6,4},{7,5},{8,14},{9,15},{10,... | collective-permute-start | bytes 663560 | tf_op jit(solution)/shard_map/ppermute | solution.py:295
  19.7 0.0 collective-permute-start.5
  21.0 0.0 copy-start
  21.0 1.5 %copy-done = bf16[3,192,1536]{2,1,0:T(8,128)(2,1)S(1)} copy-done((bf16[3,192,1536]{2,1,0:T(8,128)(2,1)S(1)}, bf16[3,192,1536]{2,1,0:T(8,128)(2,1)}, u32[]{:S(2)}) %copy-start) | copy-done | bytes 1769496
  22.4 0.0 copy-start.1
  22.4 1.1 %copy-done.1 = bf16[192,1536]{1,0:T(8,128)(2,1)S(1)} copy-done((bf16[192,1536]{1,0:T(8,128)(2,1)S(1)}, bf16[192,1536]{1,0:T(8,128)(2,1)}, u32[]{:S(2)}) %copy-start.1) | copy-done | bytes 589848
  23.5 0.0 copy-start.3
  23.5 0.7 copy-done.3
  24.2 0.8 %shard_map.95 = (bf16[3,192,1536]{2,1,0:T(8,128)(2,1)S(1)}, bf16[192,1536]{1,0:T(8,128)(2,1)S(1)}, f32[2,128]{1,0:T(2,128)S(1)}) custom-call(bf16[3,192,1536]{2,1,0:T(8,128)(2,1)S(1)} %copy-done, bf16[192,1536]{1,0:T(8,128)(2,1)S(1)} %copy-done.1, f32[12,128]{1,0:T(8,128)S(1)} %bitcast.2, f32[1]{0:T(128)S(6)} %copy.15.temp_ref, f32[1]{0:T(128)S(6)} %copy.16.bias_ref), custom_call_target="tpu_custom_call" | custom-call | tf_op jit(solution)/shard_map/pallas_call | solution.py:283
  25.1 0.0 collective-permute-done.3.refs_3_
  25.1 0.0 collective-permute-done.2.refs_2_
  25.1 0.0 collective-permute-done.7.refs_7_
  25.1 1.4 %collective-permute-done.6.refs_6_ = bf16[72,1536]{1,0:T(8,128)(2,1)S(1)} collective-permute-done((bf16[72,1536]{1,0:T(8,128)(2,1)S(1)}, bf16[72,1536]{1,0:T(8,128)(2,1)S(1)}, u32[]{:S(2)}, u32[]{:S(2)}) %collective-permute-start.6) | collective-permute-done | bytes 221216 | tf_op jit(solution)/shard_map/ppermute | solution.py:295
  26.5 0.0 collective-permute-done.5.refs_5_
  26.5 0.1 shard_map.97
  26.5 2.5 %collective-permute-start.10 = (bf16[16,1536]{1,0:T(8,128)(2,1)S(1)}, bf16[16,1536]{1,0:T(8,128)(2,1)S(1)}, u32[]{:S(2)}, u32[]{:S(2)}) collective-permute-start(bf16[16,1536]{1,0:T(8,128)(2,1)S(1)} %shard_map.97), channel_id=1, source_target_pairs={{0,48},{8,56},{16,0},{24,8},{32,16},{40,24},{48,32},{56,40},{64,11... | collective-permute-start | bytes 147464 | tf_op jit(solution)/shard_map/ppermute | solution.py:302
  29.1 0.5 collective-permute-start.9
  29.6 0.6 collective-permute-start.8
  30.2 2.1 %shard_map.96 = (bf16[8,8,1536]{2,1,0:T(8,128)(2,1)S(1)}, bf16[3,512,192]{2,1,0:T(8,128)(2,1)S(1)}, bf16[16,64,64]{2,1,0:T(8,128)(2,1)S(1)}, f32[8,192]{1,0:T(8,128)S(1)}) custom-call(bf16[72,1536]{1,0:T(8,128)(2,1)S(1)} %dynamic_update_slice.7.refs_0_, bf16[72,1536]{1,0:T(8,128)(2,1)S(1)} %collective-permute-done.1.refs_1_, ...), custom_call_target="tpu_custom_call" | custom-call | tf_op jit(solution)/shard_map/pallas_call | solution.py:283
  32.3 0.0 collective-permute-done.10
  32.3 1.2 %collective-permute-done.9 = bf16[16,1536]{1,0:T(8,128)(2,1)S(1)} collective-permute-done((bf16[16,1536]{1,0:T(8,128)(2,1)S(1)}, bf16[16,1536]{1,0:T(8,128)(2,1)S(1)}, u32[]{:S(2)}, u32[]{:S(2)}) %collective-permute-start.9) | collective-permute-done | bytes 49184 | tf_op jit(solution)/shard_map/ppermute | solution.py:302
  33.6 0.5 collective-permute-done.8
  34.1 0.5 collective-permute-start.11
  34.6 13.0 %all_to_all.10.refs_10_ = bf16[8,8,1536]{2,1,0:T(8,128)(2,1)S(1)} all-to-all(bf16[8,8,1536]{2,1,0:T(8,128)(2,1)S(1)} %get-tuple-element.42), channel_id=1, replica_groups=mesh['dp'=16,'mp'=8] {'mp'}, dimensions={0} | all-to-all | bytes 393216 | tf_op jit(solution)/shard_map/all_to_all | solution.py:354
  47.6 0.0 collective-permute-done.11.refs_9_
  47.6 3.8 %shard_map.98 = (bf16[8,400,128]{2,1,0:T(8,128)(2,1)S(1)}, bf16[8,400,128]{2,1,0:T(8,128)(2,1)S(1)}) custom-call(bf16[72,1536]{1,0:T(8,128)(2,1)S(1)} %dynamic_update_slice.7.refs_0_, bf16[72,1536]{1,0:T(8,128)(2,1)S(1)} %collective-permute-done.1.refs_1_, bf16[72,1536]{1,0:T(8,128)(2,1)S(1)} %collective-permute-done.2.refs_2_, ...), custom_call_target="tpu_custom_call" | custom-call | tf_op jit(solution)/shard_map/pallas_call | solution.py:283
  51.4 5.6 %collective-permute-start.12 = (bf16[8,400,128]{2,1,0:T(8,128)(2,1)S(1)}, bf16[8,400,128]{2,1,0:T(8,128)(2,1)S(1)}, u32[]{:S(2)}, u32[]{:S(2)}) collective-permute-start(bf16[8,400,128]{2,1,0:T(8,128)(2,1)S(1)} %get-tuple-element.48), channel_id=1, source_target_pairs={{0,8},{8,0},{16,24},{24,16},{32,40},{40,32},{48,56},{56,48},{64,72... | collective-permute-start | bytes 2457608 | tf_op jit(solution)/shard_map/ppermute | solution.py:361
  57.0 2.0 %collective-permute-done.12 = bf16[8,400,128]{2,1,0:T(8,128)(2,1)S(1)} collective-permute-done((bf16[8,400,128]{2,1,0:T(8,128)(2,1)S(1)}, bf16[8,400,128]{2,1,0:T(8,128)(2,1)S(1)}, u32[]{:S(2)}, u32[]{:S(2)}) %collective-permute-start.12) | collective-permute-done | bytes 819232 | tf_op jit(solution)/shard_map/ppermute | solution.py:361
  59.0 0.0 copy-start.4
  59.0 0.2 add_convert_fusion
  59.2 15.7 %all_to_all.11.r_ref = bf16[8,400,128]{2,1,0:T(8,128)(2,1)S(1)} all-to-all(bf16[8,400,128]{2,1,0:T(8,128)(2,1)S(1)} %add_convert_fusion), channel_id=1, replica_groups={{0,16,32,48,64,80,96,112},{8,24,40,56,72,88,104,120},{1,17,33,49,65,81,..., dimensions={0} | all-to-all | bytes 1638400 | tf_op jit(solution)/shard_map/all_to_all | solution.py:363
  74.9 0.0 copy-done.4
  74.9 0.0 copy-done.5
  74.9 1.5 %shard_map.99 = (f32[1,1536]{1,0:T(1,128)}, f32[3,192,96]{2,1,0:T(8,128)}, f32[192,96]{1,0:T(8,128)}) custom-call(bf16[8,400,128]{2,1,0:T(8,128)(2,1)S(1)} %all_to_all.11.r_ref, bf16[1,1536]{1,0:T(2,128)(2,1)S(1)} %copy-done.5, f32[12,128]{1,0:T(8,128)S(1)} %bitcast.3), custom_call_target="tpu_custom_call" | custom-call | tf_op jit(solution)/shard_map/pallas_call | solution.py:283
  (5 shorter events, 0.0 us)
Async XLA Ops:
  0.6 3.5 %collective-permute-start = (bf16[1,1536]{1,0:T(2,128)(2,1)}, bf16[1,1536]{1,0:T(2,128)(2,1)S(1)}, u32[]{:S(2)}, u32[]{:S(2)}) collective-permute-start(bf16[1,1536]{1,0:T(2,128)(2,1)} %text_ref.1), channel_id=1, source_target_pairs={{0,8},{8,0},{16,24},{24,16},{32,40},{40,32},{48,56},{56,48},{64,72... | collective-permute-start | bytes 9224 | tf_op jit(solution)/shard_map/ppermute | solution.py:302
  2.1 0.9 %copy-start.2 = (bf16[8,12288]{1,0:T(8,128)(2,1)S(1)}, bf16[8,12288]{1,0:T(8,128)(2,1)}, u32[]{:S(2)}) copy-start(bf16[8,12288]{1,0:T(8,128)(2,1)} %tok_ref.1) | copy-start | bytes 589828
  4.3 8.7 %collective-permute-start.1 = (bf16[72,1536]{1,0:T(8,128)(2,1)S(1)}, bf16[72,1536]{1,0:T(8,128)(2,1)S(1)}, u32[]{:S(2)}, u32[]{:S(2)}) collective-permute-start(bf16[72,1536]{1,0:T(8,128)(2,1)S(1)} %dynamic_update_slice.7.refs_0_), channel_id=1, source_target_pairs={{0,1},{1,0},{2,3},{3,2},{4,5},{5,4},{6,7},{7,6},{8,9},{9,8},{10,11... | collective-permute-start | bytes 663560 | tf_op jit(solution)/shard_map/ppermute | solution.py:295
  7.3 9.2 %collective-permute-start.4 = (bf16[72,1536]{1,0:T(8,128)(2,1)S(1)}, bf16[72,1536]{1,0:T(8,128)(2,1)S(1)}, u32[]{:S(2)}, u32[]{:S(2)}) collective-permute-start(bf16[72,1536]{1,0:T(8,128)(2,1)S(1)} %dynamic_update_slice.7.refs_0_), channel_id=1, source_target_pairs={{0,4},{1,5},{2,6},{3,7},{4,0},{5,1},{6,2},{7,3},{8,12},{9,13},{10,... | collective-permute-start | bytes 663560 | tf_op jit(solution)/shard_map/ppermute | solution.py:295
  10.9 14.1 %collective-permute-start.3 = (bf16[72,1536]{1,0:T(8,128)(2,1)S(1)}, bf16[72,1536]{1,0:T(8,128)(2,1)S(1)}, u32[]{:S(2)}, u32[]{:S(2)}) collective-permute-start(bf16[72,1536]{1,0:T(8,128)(2,1)S(1)} %dynamic_update_slice.7.refs_0_), channel_id=1, source_target_pairs={{0,6},{1,7},{2,0},{3,1},{4,2},{5,3},{6,4},{7,5},{8,14},{9,15},{10,... | collective-permute-start | bytes 663560 | tf_op jit(solution)/shard_map/ppermute | solution.py:295
  11.4 13.7 %collective-permute-start.2 = (bf16[72,1536]{1,0:T(8,128)(2,1)S(1)}, bf16[72,1536]{1,0:T(8,128)(2,1)S(1)}, u32[]{:S(2)}, u32[]{:S(2)}) collective-permute-start(bf16[72,1536]{1,0:T(8,128)(2,1)S(1)} %dynamic_update_slice.7.refs_0_), channel_id=1, source_target_pairs={{0,2},{1,3},{2,4},{3,5},{4,6},{5,7},{6,0},{7,1},{8,10},{9,11},{10,... | collective-permute-start | bytes 663560 | tf_op jit(solution)/shard_map/ppermute | solution.py:295
  16.5 8.6 %collective-permute-start.7 = (bf16[72,1536]{1,0:T(8,128)(2,1)S(1)}, bf16[72,1536]{1,0:T(8,128)(2,1)S(1)}, u32[]{:S(2)}, u32[]{:S(2)}) collective-permute-start(bf16[72,1536]{1,0:T(8,128)(2,1)S(1)} %collective-permute-done.4.refs_4_), channel_id=1, source_target_pairs={{0,1},{1,0},{2,3},{3,2},{4,5},{5,4},{6,7},{7,6},{8,9},{9,8},{10,11... | collective-permute-start | bytes 663560 | tf_op jit(solution)/shard_map/ppermute | solution.py:295
  16.7 9.8 %collective-permute-start.6 = (bf16[72,1536]{1,0:T(8,128)(2,1)S(1)}, bf16[72,1536]{1,0:T(8,128)(2,1)S(1)}, u32[]{:S(2)}, u32[]{:S(2)}) collective-permute-start(bf16[72,1536]{1,0:T(8,128)(2,1)S(1)} %collective-permute-done.1.refs_1_), channel_id=1, source_target_pairs={{0,6},{1,7},{2,0},{3,1},{4,2},{5,3},{6,4},{7,5},{8,14},{9,15},{10,... | collective-permute-start | bytes 663560 | tf_op jit(solution)/shard_map/ppermute | solution.py:295
  19.7 6.8 %collective-permute-start.5 = (bf16[72,1536]{1,0:T(8,128)(2,1)S(1)}, bf16[72,1536]{1,0:T(8,128)(2,1)S(1)}, u32[]{:S(2)}, u32[]{:S(2)}) collective-permute-start(bf16[72,1536]{1,0:T(8,128)(2,1)S(1)} %collective-permute-done.1.refs_1_), channel_id=1, source_target_pairs={{0,2},{1,3},{2,4},{3,5},{4,6},{5,7},{6,0},{7,1},{8,10},{9,11},{10,... | collective-permute-start | bytes 663560 | tf_op jit(solution)/shard_map/ppermute | solution.py:295
  21.0 1.5 %copy-start = (bf16[3,192,1536]{2,1,0:T(8,128)(2,1)S(1)}, bf16[3,192,1536]{2,1,0:T(8,128)(2,1)}, u32[]{:S(2)}) copy-start(bf16[3,192,1536]{2,1,0:T(8,128)(2,1)} %w_hbm) | copy-start | bytes 5308420
  22.4 1.1 %copy-start.1 = (bf16[192,1536]{1,0:T(8,128)(2,1)S(1)}, bf16[192,1536]{1,0:T(8,128)(2,1)}, u32[]{:S(2)}) copy-start(bf16[192,1536]{1,0:T(8,128)(2,1)} %wo_hbm) | copy-start | bytes 1769476
  23.5 0.7 copy-start.3
  26.5 5.8 %collective-permute-start.10 = (bf16[16,1536]{1,0:T(8,128)(2,1)S(1)}, bf16[16,1536]{1,0:T(8,128)(2,1)S(1)}, u32[]{:S(2)}, u32[]{:S(2)}) collective-permute-start(bf16[16,1536]{1,0:T(8,128)(2,1)S(1)} %shard_map.97), channel_id=1, source_target_pairs={{0,48},{8,56},{16,0},{24,8},{32,16},{40,24},{48,32},{56,40},{64,11... | collective-permute-start | bytes 147464 | tf_op jit(solution)/shard_map/ppermute | solution.py:302
  29.1 4.5 %collective-permute-start.9 = (bf16[16,1536]{1,0:T(8,128)(2,1)S(1)}, bf16[16,1536]{1,0:T(8,128)(2,1)S(1)}, u32[]{:S(2)}, u32[]{:S(2)}) collective-permute-start(bf16[16,1536]{1,0:T(8,128)(2,1)S(1)} %shard_map.97), channel_id=1, source_target_pairs={{0,32},{8,40},{16,48},{24,56},{32,0},{40,8},{48,16},{56,24},{64,96... | collective-permute-start | bytes 147464 | tf_op jit(solution)/shard_map/ppermute | solution.py:302
  29.6 4.5 %collective-permute-start.8 = (bf16[16,1536]{1,0:T(8,128)(2,1)S(1)}, bf16[16,1536]{1,0:T(8,128)(2,1)S(1)}, u32[]{:S(2)}, u32[]{:S(2)}) collective-permute-start(bf16[16,1536]{1,0:T(8,128)(2,1)S(1)} %shard_map.97), channel_id=1, source_target_pairs={{0,16},{8,24},{16,32},{24,40},{32,48},{40,56},{48,0},{56,8},{64,80... | collective-permute-start | bytes 147464 | tf_op jit(solution)/shard_map/ppermute | solution.py:302
  34.1 13.5 %collective-permute-start.11 = (bf16[64,1536]{1,0:T(8,128)(2,1)S(1)}, bf16[64,1536]{1,0:T(8,128)(2,1)S(1)}, u32[]{:S(2)}, u32[]{:S(2)}) collective-permute-start(bf16[64,1536]{1,0:T(8,128)(2,1)S(1)} %constant_dynamic-update-slice_fusion.refs_8_), channel_id=1, source_target_pairs={{0,64},{8,72},{16,80},{24,88},{32,96},{40,104},{48,112},{56,120},{... | collective-permute-start | bytes 589832 | tf_op jit(solution)/shard_map/ppermute | solution.py:302
  51.4 7.6 %collective-permute-start.12 = (bf16[8,400,128]{2,1,0:T(8,128)(2,1)S(1)}, bf16[8,400,128]{2,1,0:T(8,128)(2,1)S(1)}, u32[]{:S(2)}, u32[]{:S(2)}) collective-permute-start(bf16[8,400,128]{2,1,0:T(8,128)(2,1)S(1)} %get-tuple-element.48), channel_id=1, source_target_pairs={{0,8},{8,0},{16,24},{24,16},{32,40},{40,32},{48,56},{56,48},{64,72... | collective-permute-start | bytes 2457608 | tf_op jit(solution)/shard_map/ppermute | solution.py:361
  59.0 15.9 %copy-start.4 = (f32[1536]{0:T(1024)S(1)}, f32[1536]{0:T(1024)}, u32[]{:S(2)}) copy-start(f32[1536]{0:T(1024)} %param.8) | copy-start | bytes 18436
  59.0 15.9 %copy-start.5 = (bf16[1,1536]{1,0:T(2,128)(2,1)S(1)}, bf16[1,1536]{1,0:T(2,128)(2,1)}, u32[]{:S(2)}) copy-start(bf16[1,1536]{1,0:T(2,128)(2,1)} %text_ref.1) | copy-start | bytes 9220

commit v5 on v4

--- a/solution.py
+++ b/solution.py
@@ -59,17 +59,18 @@
     out_ref[64:72, :] = jnp.zeros((8, D), BF16)
 
 
-def load_kernel(
-    w_hbm, wo_hbm, gain_ref, temp_ref, bias_ref, w_ref, wo_ref, scalar_ref, raw_ref, sems
-):
+def scalar_kernel(temp_ref, bias_ref, scalar_ref):
+    scalar_ref[0:1, :] = jnp.exp(jnp.full((1, 128), temp_ref[0], F32))
+    scalar_ref[1:2, :] = jnp.full((1, 128), bias_ref[0], F32)
+
+
+def load_kernel(w_hbm, wo_hbm, gain_ref, w_ref, wo_ref, raw_ref, sems):
     copies = [
         pltpu.make_async_copy(w_hbm, raw_ref, sems.at[0]),
         pltpu.make_async_copy(wo_hbm, wo_ref, sems.at[1]),
     ]
     for copy in copies:
         copy.start()
-    scalar_ref[0:1, :] = jnp.exp(jnp.full((1, 128), temp_ref[0], F32))
-    scalar_ref[1:2, :] = jnp.full((1, 128), bias_ref[0], F32)
     copies[0].wait()
     for i in range(12):
         part = slice(i * 128, (i + 1) * 128)
@@ -99,15 +100,28 @@
     out_ref[...] = line_ref[...].astype(BF16)
 
 
+def early_kernel(*refs):
+    shards, (w_ref, qkv_ref, wide_ref) = refs[:5], refs[5:]
+    normed = jnp.concatenate([r[0:64, :] for r in shards], axis=0)
+    for c in range(3):
+        wide_ref[...] = dot(normed, w_ref[c], LAST)
+        for b in range(IMG):
+            block = jnp.concatenate(
+                [wide_ref[(s * 8 + b) * 8:(s * 8 + b) * 8 + 8, :] for s in range(5)], axis=0
+            )
+            qkv_ref[c, b * 40:(b + 1) * 40, :] = block.astype(BF16)
+
+
 def forward_kernel(*refs):
-    shards, (w_ref, wo_ref, sum_ref), refs = refs[:MP], refs[MP:MP + 3], refs[MP + 3:]
+    shards, (early_ref, w_ref, wo_ref, sum_ref), refs = refs[:3], refs[3:7], refs[7:]
     part_ref, qkv_ref, probs_ref, att_ref, wide_ref = refs
     normed = jnp.concatenate([r[0:64, :] for r in shards], axis=0)
     for c in range(3):
         wide_ref[...] = dot(normed, w_ref[c], LAST)
         for b in range(IMG):
             block = jnp.concatenate(
-                [wide_ref[(s * 8 + b) * 8:(s * 8 + b) * 8 + 8, :] for s in range(MP)], axis=0
+                [early_ref[c, b * 40:(b + 1) * 40, :].astype(F32)]
+                + [wide_ref[(s * 8 + b) * 8:(s * 8 + b) * 8 + 8, :] for s in range(3)], axis=0
             )
             qkv_ref[c, b * 64:(b + 1) * 64, :] = block.astype(BF16)
     lane = lanes((64, WIDTH))
@@ -133,7 +147,7 @@
 
 
 def backward_kernel(*refs):
-    shards, texts, refs = refs[:MP], refs[MP:MP + 2], refs[MP + 2:]
+    shards, texts, refs = refs[:MP], refs[MP:MP + 4], refs[MP + 4:]
     part_ref, qkv_ref, probs_ref, att_ref, scalar_ref, wo_ref = refs[:6]
     keep_ref, give_ref, grad_ref, turn_ref, text_ref, both_ref = refs[6:]
     me = lax.axis_index("dp")
@@ -145,7 +159,7 @@
     scale = scalar_ref[0:1, :]
     image_inv = lax.rsqrt(jnp.sum(pooled * pooled, axis=-1, keepdims=True) + EPS)
     unit = pooled * image_inv
-    text = jnp.concatenate([r[...] for r in texts], axis=0)
+    text = jnp.concatenate([r[0:32, :] for r in texts], axis=0)
     wide_text = text.astype(F32)
     square = pieces(wide_text * wide_text, 2)
     ones = jnp.ones((IMG, D), BF16)
@@ -166,7 +180,7 @@
     owner = lanes((TEXT, DP))
     step_x = lax.rem(lax.rem(lax.div(me, 2), 4) - lax.rem(lax.div(owner, 2), 4) + 4, 4)
     step_y = lax.rem(lax.div(me, 8) + lax.div(owner, 8), 2)
-    place = step_y * 64 + step_x * 16 + lax.rem(owner, 2) * MP + slot
+    place = step_x * 32 + step_y * 16 + lax.rem(owner, 2) * MP + slot
     chosen = jnp.where(column == place, 1.0, 0.0).astype(BF16)
     mine = dot(jnp.concatenate(pieces(pair, 3), axis=0), chosen, (((1,), (0,)), ((), ())))
     pair_high, pair_low = pieces(mine[0:8] + mine[8:16] + mine[16:24], 2)
@@ -323,34 +337,40 @@
     own = lax.dynamic_update_slice(own, text_embed, (64, 0))
     own = lax.dynamic_update_slice(own, over_dp(text_embed, 0, 0, 1), (65, 0))
     shards = first_step(own)
-    shards[1], qkv_weight, out_weight, gain = lax.optimization_barrier(
-        (shards[1], qkv_weight, out_weight, norm_gain)
+    own, qkv_weight, out_weight, gain = lax.optimization_barrier(
+        (own, qkv_weight, out_weight, norm_gain)
+    )
+    qkv_weight, out_weight = call(
+        load_kernel,
+        [((3, WIDTH, D), BF16), ((WIDTH, D), BF16)],
+        [((3, WIDTH, D), BF16), pltpu.SemaphoreType.DMA((2,))],
+        qkv_weight, out_weight, gain.reshape(12, 128), specs=[ANY, ANY, HERE],
+    )
+    shards[1], qkv_weight, out_weight = lax.optimization_barrier(
+        (shards[1], qkv_weight, out_weight)
     )
     shards += second_step(shards)
-    qkv_weight, out_weight, scalars = call(
-        load_kernel,
-        [((3, WIDTH, D), BF16), ((WIDTH, D), BF16), ((2, 128), F32)],
-        [((3, WIDTH, D), BF16), pltpu.SemaphoreType.DMA((2,))],
-        qkv_weight, out_weight, gain.reshape(12, 128), log_temp, logit_bias,
-        specs=[ANY, ANY, HERE, SMEM, SMEM],
-    )
-    shards[0], qkv_weight, out_weight = lax.optimization_barrier(
-        (shards[0], qkv_weight, out_weight)
-    )
+    shards[2], log_temp, logit_bias = lax.optimization_barrier((shards[2], log_temp, logit_bias))
+    scalars, = call(scalar_kernel, [((2, 128), F32)], [], log_temp, logit_bias, specs=[SMEM] * 2)
+    shards[0], scalars = lax.optimization_barrier((shards[0], scalars))
+    early, = call(
+        early_kernel, [((3, 320, WIDTH), BF16)], [((320, WIDTH), F32)], *shards[:5], qkv_weight
+    )
+    shards[0], early = lax.optimization_barrier((shards[0], early))
     texts, = call(text_kernel, [((16, D), BF16)], [((16, D), F32)], *shards)
-    texts = [texts] + [over_dp(texts, 0, dx, 0) for dx in (1, 2, 3)]
+    texts = [texts, over_dp(texts, 1, 0, 0)]
     part, qkv, probs, attended = call(
         forward_kernel,
         [
             ((MP, IMG, D), BF16), ((3, 512, WIDTH), BF16),
             ((16, 64, 64), BF16), ((IMG, WIDTH), F32),
         ],
-        [((512, WIDTH), F32)],
-        *shards, qkv_weight, out_weight, token_sum,
+        [((192, WIDTH), F32)],
+        *shards[5:], early, qkv_weight, out_weight, token_sum,
     )
     part, *texts = lax.optimization_barrier((part, *texts))
-    texts = jnp.concatenate(texts, axis=0)
-    texts = [texts, over_dp(texts, 1, 0, 0)]
+    texts = jnp.concatenate(texts + texts, axis=0)
+    texts = [texts] + [over_dp(texts, 0, dx, 0) for dx in (1, 2, 3)]
     parts = lax.all_to_all(part, "mp", 0, 0)
     keep, give = call(
         backward_kernel,

time: 76.8 us -> 75 us (0.977)
  waiting for transfers between devices: 9.2 us -> 7.78 us
  blocking collectives: 28.7 us -> 27.7 us
    all_to_all x1, blocking collectives: 13 us -> 11.2 us  [body(): parts = lax.all_to_all(part, 'mp', 0, 0)]
    ppermute x7, waiting for transfers between devices: 5.5 us -> 4.51 us  [over_mp(): return lax.ppermute(block, 'mp', route)]
    all_to_all x1, blocking collectives: 15.7 us -> 16.5 us  [body(): lax.all_to_all(send, 'dp', 0, 0, axis_index_groups=[list(range(c, DP, 2))...]
    pallas_call x6 -> x8, Pallas kernels: 8.63 us -> 8.76 us  [call(): pl.pallas_call(kernel, out_shape=[jax.ShapeDtypeStruct(*o) for o in outs]...]
  transfers between devices with their start and end apart: 13 -> 13, of which waited for: 6 -> 6; matrix products, arithmetic and copies ran while one was open for 1% -> 1% of each run, Pallas kernels for 4% -> 5%
where the time goes in v5:
time: 75 us; the launch traced here: 74.6 us
  blocking collectives  27.7 us (37%)
  starting transfers between devices  23 us (31%)
  Pallas kernels  8.76 us (12%)
  waiting for transfers between devices  7.78 us (10%)
  local copies, waits for them, and re-layouts  5.06 us (7%)
  between operations  2.05 us (3%)
    all_to_all x1, blocking collectives, body(): lax.all_to_all(send, 'dp', 0, 0, axis_index_groups=[list(range(c, DP, 2))...  16.5 us
    ppermute x7, starting transfers between devices, over_mp(): return lax.ppermute(block, 'mp', route)  11.3 us
    all_to_all x1, blocking collectives, body(): parts = lax.all_to_all(part, 'mp', 0, 0)  11.2 us
    pallas_call x8, Pallas kernels, call(): pl.pallas_call(kernel, out_shape=[jax.ShapeDtypeStruct(*o) for o in outs]...  8.76 us
    ppermute x1, starting transfers between devices, body(): other = lax.ppermute(give, 'dp', [(i, i ^ 1) for i in range(DP)])  6.1 us
    ppermute x5, starting transfers between devices, over_dp(): return lax.ppermute(block, 'dp', route)  5.65 us
    ppermute x7, waiting for transfers between devices, over_mp(): return lax.ppermute(block, 'mp', route)  4.51 us
    unnamed x15, local copies, waits for them, and re-layouts  4.18 us
  transfers between devices with their start and end apart: 13, of which 6 were waited for; matrix products, arithmetic and copies ran while one was open for 1% of the time, Pallas kernels for 5%

profile of v5, /device:TPU:1, one launch (start us, length us, event | category | flops | bytes accessed | tf_op | source)
XLA Modules:
  0.0 74.6 jit_solution(12735580864169559429)
XLA Ops:
  0.6 1.5 %collective-permute-start = (bf16[1,1536]{1,0:T(2,128)(2,1)}, bf16[1,1536]{1,0:T(2,128)(2,1)S(1)}, u32[]{:S(2)}, u32[]{:S(2)}) collective-permute-start(bf16[1,1536]{1,0:T(2,128)(2,1)} %text_ref.1), channel_id=1, source_target_pairs={{0,8},{8,0},{16,24},{24,16},{32,40},{40,32},{48,56},{56,48},{64,72... | collective-permute-start | bytes 9224 | tf_op jit(solution)/shard_map/ppermute | solution.py:316
  2.1 0.0 copy-start.2
  2.1 0.9 %copy-done.2 = bf16[8,12288]{1,0:T(8,128)(2,1)S(1)} copy-done((bf16[8,12288]{1,0:T(8,128)(2,1)S(1)}, bf16[8,12288]{1,0:T(8,128)(2,1)}, u32[]{:S(2)}) %copy-start.2) | copy-done | bytes 196632
  3.1 0.3 shard_map.94
  3.4 0.8 %dynamic_update_slice.6 = bf16[72,1536]{1,0:T(8,128)(2,1)S(1)} dynamic-update-slice(bf16[72,1536]{1,0:T(8,128)(2,1)S(1)} %get-tuple-element.29, bf16[1,1536]{1,0:T(2,128)(2,1)} %text_ref.1, s32[]{:T(128)} %constant.0.clone.1, s32[]{:T(128)} %constant.1.clone.1) | dynamic-update-slice | bytes 6148 | tf_op jit(solution)/shard_map/dynamic_update_slice | solution.py:337
  4.2 0.0 collective-permute-done
  4.2 0.1 dynamic_update_slice.7.refs_0_
  4.3 3.1 %collective-permute-start.2 = (bf16[72,1536]{1,0:T(8,128)(2,1)S(1)}, bf16[72,1536]{1,0:T(8,128)(2,1)S(1)}, u32[]{:S(2)}, u32[]{:S(2)}) collective-permute-start(bf16[72,1536]{1,0:T(8,128)(2,1)S(1)} %dynamic_update_slice.7.refs_0_), channel_id=1, source_target_pairs={{0,1},{1,0},{2,3},{3,2},{4,5},{5,4},{6,7},{7,6},{8,9},{9,8},{10,11... | collective-permute-start | bytes 663560 | tf_op jit(solution)/shard_map/ppermute | solution.py:309
  7.3 3.6 %collective-permute-start.4 = (bf16[72,1536]{1,0:T(8,128)(2,1)S(1)}, bf16[72,1536]{1,0:T(8,128)(2,1)S(1)}, u32[]{:S(2)}, u32[]{:S(2)}) collective-permute-start(bf16[72,1536]{1,0:T(8,128)(2,1)S(1)} %dynamic_update_slice.7.refs_0_), channel_id=1, source_target_pairs={{0,4},{1,5},{2,6},{3,7},{4,0},{5,1},{6,2},{7,3},{8,12},{9,13},{10,... | collective-permute-start | bytes 663560 | tf_op jit(solution)/shard_map/ppermute | solution.py:309
  10.9 0.4 collective-permute-start.3
  11.4 1.0 %collective-permute-start.1 = (bf16[72,1536]{1,0:T(8,128)(2,1)S(1)}, bf16[72,1536]{1,0:T(8,128)(2,1)S(1)}, u32[]{:S(2)}, u32[]{:S(2)}) collective-permute-start(bf16[72,1536]{1,0:T(8,128)(2,1)S(1)} %dynamic_update_slice.7.refs_0_), channel_id=1, source_target_pairs={{0,2},{1,3},{2,4},{3,5},{4,6},{5,7},{6,0},{7,1},{8,10},{9,11},{10,... | collective-permute-start | bytes 663560 | tf_op jit(solution)/shard_map/ppermute | solution.py:309
  12.4 0.0 copy-start
  12.4 1.5 %copy-done = bf16[3,192,1536]{2,1,0:T(8,128)(2,1)S(1)} copy-done((bf16[3,192,1536]{2,1,0:T(8,128)(2,1)S(1)}, bf16[3,192,1536]{2,1,0:T(8,128)(2,1)}, u32[]{:S(2)}) %copy-start) | copy-done | bytes 1769496
  13.9 0.0 copy-start.1
  13.9 1.1 %copy-done.1 = bf16[192,1536]{1,0:T(8,128)(2,1)S(1)} copy-done((bf16[192,1536]{1,0:T(8,128)(2,1)S(1)}, bf16[192,1536]{1,0:T(8,128)(2,1)}, u32[]{:S(2)}) %copy-start.1) | copy-done | bytes 589848
  15.0 0.0 copy-start.3
  15.0 0.7 copy-done.3
  15.7 0.8 %shard_map.96 = (bf16[3,192,1536]{2,1,0:T(8,128)(2,1)S(1)}, bf16[192,1536]{1,0:T(8,128)(2,1)S(1)}) custom-call(bf16[3,192,1536]{2,1,0:T(8,128)(2,1)S(1)} %copy-done, bf16[192,1536]{1,0:T(8,128)(2,1)S(1)} %copy-done.1, f32[12,128]{1,0:T(8,128)S(1)} %bitcast.2), custom_call_target="tpu_custom_call" | custom-call | tf_op jit(solution)/shard_map/pallas_call | solution.py:297
  16.5 0.0 collective-permute-done.2.refs_1_
  16.5 0.0 collective-permute-done.4.refs_4_
  16.5 0.2 collective-permute-start.7
  16.7 3.0 %collective-permute-start.6 = (bf16[72,1536]{1,0:T(8,128)(2,1)S(1)}, bf16[72,1536]{1,0:T(8,128)(2,1)S(1)}, u32[]{:S(2)}, u32[]{:S(2)}) collective-permute-start(bf16[72,1536]{1,0:T(8,128)(2,1)S(1)} %collective-permute-done.2.refs_1_), channel_id=1, source_target_pairs={{0,6},{1,7},{2,0},{3,1},{4,2},{5,3},{6,4},{7,5},{8,14},{9,15},{10,... | collective-permute-start | bytes 663560 | tf_op jit(solution)/shard_map/ppermute | solution.py:309
  19.7 0.0 collective-permute-start.5
  21.0 0.6 collective-permute-done.1.refs_2_
  21.6 0.2 collective-permute-done.3.refs_3_
  21.7 1.0 %shard_map.97.refs_3_ = bf16[3,320,192]{2,1,0:T(8,128)(2,1)S(1)} custom-call(bf16[72,1536]{1,0:T(8,128)(2,1)S(1)} %dynamic_update_slice.7.refs_0_, bf16[72,1536]{1,0:T(8,128)(2,1)S(1)} %collective-permute-done.2.refs_1_, bf16[72,1536]{1,0:T(8,128)(2,1)S(1)} %collective-permute-done.1.refs_2_, bf16[72,1536]{1,0:T(8,128)(2,1)S(1)} %collective-permute-done.3.refs_3_, ...), custom_call_target="tpu_custom_call" | custom-call | tf_op jit(solution)/shard_map/pallas_call | solution.py:297
  22.7 1.1 %collective-permute-done.7.refs_2_.refs_7_ = bf16[72,1536]{1,0:T(8,128)(2,1)S(1)} collective-permute-done((bf16[72,1536]{1,0:T(8,128)(2,1)S(1)}, bf16[72,1536]{1,0:T(8,128)(2,1)S(1)}, u32[]{:S(2)}, u32[]{:S(2)}) %collective-permute-start.7) | collective-permute-done | bytes 221216 | tf_op jit(solution)/shard_map/ppermute | solution.py:309
  23.9 2.6 %collective-permute-done.6.refs_1_.refs_6_ = bf16[72,1536]{1,0:T(8,128)(2,1)S(1)} collective-permute-done((bf16[72,1536]{1,0:T(8,128)(2,1)S(1)}, bf16[72,1536]{1,0:T(8,128)(2,1)S(1)}, u32[]{:S(2)}, u32[]{:S(2)}) %collective-permute-start.6) | collective-permute-done | bytes 221216 | tf_op jit(solution)/shard_map/ppermute | solution.py:309
  26.5 0.0 collective-permute-done.5.refs_0_.refs_5_
  26.5 0.1 shard_map.99
  26.5 0.5 collective-permute-start.8
  27.0 1.2 %shard_map.98 = (bf16[8,8,1536]{2,1,0:T(8,128)(2,1)S(1)}, bf16[3,512,192]{2,1,0:T(8,128)(2,1)S(1)}, bf16[16,64,64]{2,1,0:T(8,128)(2,1)S(1)}, f32[8,192]{1,0:T(8,128)S(1)}) custom-call(bf16[72,1536]{1,0:T(8,128)(2,1)S(1)} %collective-permute-done.5.refs_0_.refs_5_, bf16[72,1536]{1,0:T(8,128)(2,1)S(1)} %collective-permute-done.6.refs_1_.refs_6_, ...), custom_call_target="tpu_custom_call" | custom-call | tf_op jit(solution)/shard_map/pallas_call | solution.py:297
  28.3 1.3 %collective-permute-done.8 = bf16[16,1536]{1,0:T(8,128)(2,1)S(1)} collective-permute-done((bf16[16,1536]{1,0:T(8,128)(2,1)S(1)}, bf16[16,1536]{1,0:T(8,128)(2,1)S(1)}, u32[]{:S(2)}, u32[]{:S(2)}) %collective-permute-start.8) | collective-permute-done | bytes 49184 | tf_op jit(solution)/shard_map/ppermute | solution.py:316
  29.6 2.5 %collective-permute-start.11 = (bf16[64,1536]{1,0:T(8,128)(2,1)S(1)}, bf16[64,1536]{1,0:T(8,128)(2,1)S(1)}, u32[]{:S(2)}, u32[]{:S(2)}) collective-permute-start(bf16[64,1536]{1,0:T(8,128)(2,1)S(1)} %constant_dynamic-update-slice_fusion.refs_8_), channel_id=1, source_target_pairs={{0,48},{8,56},{16,0},{24,8},{32,16},{40,24},{48,32},{56,40},{64,11... | collective-permute-start | bytes 589832 | tf_op jit(solution)/shard_map/ppermute | solution.py:316
  32.2 0.5 collective-permute-start.10
  32.7 0.6 collective-permute-start.9
  33.3 11.2 %all_to_all.10.refs_12_ = bf16[8,8,1536]{2,1,0:T(8,128)(2,1)S(1)} all-to-all(bf16[8,8,1536]{2,1,0:T(8,128)(2,1)S(1)} %get-tuple-element.48), channel_id=1, replica_groups=mesh['dp'=16,'mp'=8] {'mp'}, dimensions={0} | all-to-all | bytes 393216 | tf_op jit(solution)/shard_map/all_to_all | solution.py:374
  44.5 0.0 collective-permute-done.11.refs_11_
  44.5 0.0 collective-permute-done.10.refs_10_
  44.5 0.0 collective-permute-done.9.refs_9_
  44.5 3.8 %shard_map.100 = (bf16[8,400,128]{2,1,0:T(8,128)(2,1)S(1)}, bf16[8,400,128]{2,1,0:T(8,128)(2,1)S(1)}) custom-call(bf16[72,1536]{1,0:T(8,128)(2,1)S(1)} %dynamic_update_slice.7.refs_0_, bf16[72,1536]{1,0:T(8,128)(2,1)S(1)} %collective-permute-done.2.refs_1_, bf16[72,1536]{1,0:T(8,128)(2,1)S(1)} %collective-permute-done.1.refs_2_, ...), custom_call_target="tpu_custom_call" | custom-call | tf_op jit(solution)/shard_map/pallas_call | solution.py:297
  48.3 6.1 %collective-permute-start.12 = (bf16[8,400,128]{2,1,0:T(8,128)(2,1)S(1)}, bf16[8,400,128]{2,1,0:T(8,128)(2,1)S(1)}, u32[]{:S(2)}, u32[]{:S(2)}) collective-permute-start(bf16[8,400,128]{2,1,0:T(8,128)(2,1)S(1)} %get-tuple-element.54), channel_id=1, source_target_pairs={{0,8},{8,0},{16,24},{24,16},{32,40},{40,32},{48,56},{56,48},{64,72... | collective-permute-start | bytes 2457608 | tf_op jit(solution)/shard_map/ppermute | solution.py:381
  54.4 2.0 %collective-permute-done.12 = bf16[8,400,128]{2,1,0:T(8,128)(2,1)S(1)} collective-permute-done((bf16[8,400,128]{2,1,0:T(8,128)(2,1)S(1)}, bf16[8,400,128]{2,1,0:T(8,128)(2,1)S(1)}, u32[]{:S(2)}, u32[]{:S(2)}) %collective-permute-start.12) | collective-permute-done | bytes 819232 | tf_op jit(solution)/shard_map/ppermute | solution.py:381
  56.4 0.2 add_convert_fusion
  56.6 16.5 %all_to_all.11.r_ref = bf16[8,400,128]{2,1,0:T(8,128)(2,1)S(1)} all-to-all(bf16[8,400,128]{2,1,0:T(8,128)(2,1)S(1)} %add_convert_fusion), channel_id=1, replica_groups={{0,16,32,48,64,80,96,112},{8,24,40,56,72,88,104,120},{1,17,33,49,65,81,..., dimensions={0} | all-to-all | bytes 1638400 | tf_op jit(solution)/shard_map/all_to_all | solution.py:383
  73.1 0.0 copy-done.4
  73.1 0.0 copy-done.5
  73.1 1.5 %shard_map.101 = (f32[1,1536]{1,0:T(1,128)}, f32[3,192,96]{2,1,0:T(8,128)}, f32[192,96]{1,0:T(8,128)}) custom-call(bf16[8,400,128]{2,1,0:T(8,128)(2,1)S(1)} %all_to_all.11.r_ref, bf16[1,1536]{1,0:T(2,128)(2,1)S(1)} %copy-done.5, f32[12,128]{1,0:T(8,128)S(1)} %bitcast.3), custom_call_target="tpu_custom_call" | custom-call | tf_op jit(solution)/shard_map/pallas_call | solution.py:297
  (7 shorter events, 0.0 us)
Async XLA Ops:
  0.6 3.5 %collective-permute-start = (bf16[1,1536]{1,0:T(2,128)(2,1)}, bf16[1,1536]{1,0:T(2,128)(2,1)S(1)}, u32[]{:S(2)}, u32[]{:S(2)}) collective-permute-start(bf16[1,1536]{1,0:T(2,128)(2,1)} %text_ref.1), channel_id=1, source_target_pairs={{0,8},{8,0},{16,24},{24,16},{32,40},{40,32},{48,56},{56,48},{64,72... | collective-permute-start | bytes 9224 | tf_op jit(solution)/shard_map/ppermute | solution.py:316
  2.1 0.9 %copy-start.2 = (bf16[8,12288]{1,0:T(8,128)(2,1)S(1)}, bf16[8,12288]{1,0:T(8,128)(2,1)}, u32[]{:S(2)}) copy-start(bf16[8,12288]{1,0:T(8,128)(2,1)} %tok_ref.1) | copy-start | bytes 589828
  4.3 12.2 %collective-permute-start.2 = (bf16[72,1536]{1,0:T(8,128)(2,1)S(1)}, bf16[72,1536]{1,0:T(8,128)(2,1)S(1)}, u32[]{:S(2)}, u32[]{:S(2)}) collective-permute-start(bf16[72,1536]{1,0:T(8,128)(2,1)S(1)} %dynamic_update_slice.7.refs_0_), channel_id=1, source_target_pairs={{0,1},{1,0},{2,3},{3,2},{4,5},{5,4},{6,7},{7,6},{8,9},{9,8},{10,11... | collective-permute-start | bytes 663560 | tf_op jit(solution)/shard_map/ppermute | solution.py:309
  7.3 9.2 %collective-permute-start.4 = (bf16[72,1536]{1,0:T(8,128)(2,1)S(1)}, bf16[72,1536]{1,0:T(8,128)(2,1)S(1)}, u32[]{:S(2)}, u32[]{:S(2)}) collective-permute-start(bf16[72,1536]{1,0:T(8,128)(2,1)S(1)} %dynamic_update_slice.7.refs_0_), channel_id=1, source_target_pairs={{0,4},{1,5},{2,6},{3,7},{4,0},{5,1},{6,2},{7,3},{8,12},{9,13},{10,... | collective-permute-start | bytes 663560 | tf_op jit(solution)/shard_map/ppermute | solution.py:309
  10.9 10.8 %collective-permute-start.3 = (bf16[72,1536]{1,0:T(8,128)(2,1)S(1)}, bf16[72,1536]{1,0:T(8,128)(2,1)S(1)}, u32[]{:S(2)}, u32[]{:S(2)}) collective-permute-start(bf16[72,1536]{1,0:T(8,128)(2,1)S(1)} %dynamic_update_slice.7.refs_0_), channel_id=1, source_target_pairs={{0,6},{1,7},{2,0},{3,1},{4,2},{5,3},{6,4},{7,5},{8,14},{9,15},{10,... | collective-permute-start | bytes 663560 | tf_op jit(solution)/shard_map/ppermute | solution.py:309
  11.4 10.2 %collective-permute-start.1 = (bf16[72,1536]{1,0:T(8,128)(2,1)S(1)}, bf16[72,1536]{1,0:T(8,128)(2,1)S(1)}, u32[]{:S(2)}, u32[]{:S(2)}) collective-permute-start(bf16[72,1536]{1,0:T(8,128)(2,1)S(1)} %dynamic_update_slice.7.refs_0_), channel_id=1, source_target_pairs={{0,2},{1,3},{2,4},{3,5},{4,6},{5,7},{6,0},{7,1},{8,10},{9,11},{10,... | collective-permute-start | bytes 663560 | tf_op jit(solution)/shard_map/ppermute | solution.py:309
  12.4 1.5 %copy-start = (bf16[3,192,1536]{2,1,0:T(8,128)(2,1)S(1)}, bf16[3,192,1536]{2,1,0:T(8,128)(2,1)}, u32[]{:S(2)}) copy-start(bf16[3,192,1536]{2,1,0:T(8,128)(2,1)} %w_hbm) | copy-start | bytes 5308420
  13.9 1.1 %copy-start.1 = (bf16[192,1536]{1,0:T(8,128)(2,1)S(1)}, bf16[192,1536]{1,0:T(8,128)(2,1)}, u32[]{:S(2)}) copy-start(bf16[192,1536]{1,0:T(8,128)(2,1)} %wo_hbm) | copy-start | bytes 1769476
  15.0 0.7 copy-start.3
  16.5 7.4 %collective-permute-start.7 = (bf16[72,1536]{1,0:T(8,128)(2,1)S(1)}, bf16[72,1536]{1,0:T(8,128)(2,1)S(1)}, u32[]{:S(2)}, u32[]{:S(2)}) collective-permute-start(bf16[72,1536]{1,0:T(8,128)(2,1)S(1)} %collective-permute-done.4.refs_4_), channel_id=1, source_target_pairs={{0,1},{1,0},{2,3},{3,2},{4,5},{5,4},{6,7},{7,6},{8,9},{9,8},{10,11... | collective-permute-start | bytes 663560 | tf_op jit(solution)/shard_map/ppermute | solution.py:309
  16.7 9.8 %collective-permute-start.6 = (bf16[72,1536]{1,0:T(8,128)(2,1)S(1)}, bf16[72,1536]{1,0:T(8,128)(2,1)S(1)}, u32[]{:S(2)}, u32[]{:S(2)}) collective-permute-start(bf16[72,1536]{1,0:T(8,128)(2,1)S(1)} %collective-permute-done.2.refs_1_), channel_id=1, source_target_pairs={{0,6},{1,7},{2,0},{3,1},{4,2},{5,3},{6,4},{7,5},{8,14},{9,15},{10,... | collective-permute-start | bytes 663560 | tf_op jit(solution)/shard_map/ppermute | solution.py:309
  19.7 6.8 %collective-permute-start.5 = (bf16[72,1536]{1,0:T(8,128)(2,1)S(1)}, bf16[72,1536]{1,0:T(8,128)(2,1)S(1)}, u32[]{:S(2)}, u32[]{:S(2)}) collective-permute-start(bf16[72,1536]{1,0:T(8,128)(2,1)S(1)} %collective-permute-done.2.refs_1_), channel_id=1, source_target_pairs={{0,2},{1,3},{2,4},{3,5},{4,6},{5,7},{6,0},{7,1},{8,10},{9,11},{10,... | collective-permute-start | bytes 663560 | tf_op jit(solution)/shard_map/ppermute | solution.py:309
  26.5 3.0 %collective-permute-start.8 = (bf16[16,1536]{1,0:T(8,128)(2,1)S(1)}, bf16[16,1536]{1,0:T(8,128)(2,1)S(1)}, u32[]{:S(2)}, u32[]{:S(2)}) collective-permute-start(bf16[16,1536]{1,0:T(8,128)(2,1)S(1)} %shard_map.99), channel_id=1, source_target_pairs={{0,64},{8,72},{16,80},{24,88},{32,96},{40,104},{48,112},{56,120},{... | collective-permute-start | bytes 147464 | tf_op jit(solution)/shard_map/ppermute | solution.py:316
  29.6 14.9 %collective-permute-start.11 = (bf16[64,1536]{1,0:T(8,128)(2,1)S(1)}, bf16[64,1536]{1,0:T(8,128)(2,1)S(1)}, u32[]{:S(2)}, u32[]{:S(2)}) collective-permute-start(bf16[64,1536]{1,0:T(8,128)(2,1)S(1)} %constant_dynamic-update-slice_fusion.refs_8_), channel_id=1, source_target_pairs={{0,48},{8,56},{16,0},{24,8},{32,16},{40,24},{48,32},{56,40},{64,11... | collective-permute-start | bytes 589832 | tf_op jit(solution)/shard_map/ppermute | solution.py:316
  32.2 12.3 %collective-permute-start.10 = (bf16[64,1536]{1,0:T(8,128)(2,1)S(1)}, bf16[64,1536]{1,0:T(8,128)(2,1)S(1)}, u32[]{:S(2)}, u32[]{:S(2)}) collective-permute-start(bf16[64,1536]{1,0:T(8,128)(2,1)S(1)} %constant_dynamic-update-slice_fusion.refs_8_), channel_id=1, source_target_pairs={{0,32},{8,40},{16,48},{24,56},{32,0},{40,8},{48,16},{56,24},{64,96... | collective-permute-start | bytes 589832 | tf_op jit(solution)/shard_map/ppermute | solution.py:316
  32.7 11.8 %collective-permute-start.9 = (bf16[64,1536]{1,0:T(8,128)(2,1)S(1)}, bf16[64,1536]{1,0:T(8,128)(2,1)S(1)}, u32[]{:S(2)}, u32[]{:S(2)}) collective-permute-start(bf16[64,1536]{1,0:T(8,128)(2,1)S(1)} %constant_dynamic-update-slice_fusion.refs_8_), channel_id=1, source_target_pairs={{0,16},{8,24},{16,32},{24,40},{32,48},{40,56},{48,0},{56,8},{64,80... | collective-permute-start | bytes 589832 | tf_op jit(solution)/shard_map/ppermute | solution.py:316
  48.3 8.1 %collective-permute-start.12 = (bf16[8,400,128]{2,1,0:T(8,128)(2,1)S(1)}, bf16[8,400,128]{2,1,0:T(8,128)(2,1)S(1)}, u32[]{:S(2)}, u32[]{:S(2)}) collective-permute-start(bf16[8,400,128]{2,1,0:T(8,128)(2,1)S(1)} %get-tuple-element.54), channel_id=1, source_target_pairs={{0,8},{8,0},{16,24},{24,16},{32,40},{40,32},{48,56},{56,48},{64,72... | collective-permute-start | bytes 2457608 | tf_op jit(solution)/shard_map/ppermute | solution.py:381
  56.4 16.8 %copy-start.4 = (f32[1536]{0:T(1024)S(1)}, f32[1536]{0:T(1024)}, u32[]{:S(2)}) copy-start(f32[1536]{0:T(1024)} %param.8) | copy-start | bytes 18436
  56.4 16.8 %copy-start.5 = (bf16[1,1536]{1,0:T(2,128)(2,1)S(1)}, bf16[1,1536]{1,0:T(2,128)(2,1)}, u32[]{:S(2)}) copy-start(bf16[1,1536]{1,0:T(2,128)(2,1)} %text_ref.1) | copy-start | bytes 9220

commit v6 on v5

--- a/solution.py
+++ b/solution.py
@@ -1,3 +1,4 @@
+import functools
 import math
 
 import jax
@@ -88,16 +89,18 @@
     return lax.rem(lax.div(slot, 2) + 4 - dz, 4) * 2 + lax.rem(lax.rem(slot, 2) + dy, 2)
 
 
-def text_kernel(*refs):
-    shards, (out_ref, line_ref) = refs[:MP], refs[MP:]
+def text_kernel(first, count, *refs):
+    shards, (kept_ref, out_ref) = refs[:count], refs[count:]
     slot = lax.axis_index("mp")
     core = lax.rem(lax.axis_index("dp"), 2)
-    for s in range(MP):
+    row = lax.broadcasted_iota(jnp.int32, (16, D), 0)
+    total = kept_ref[...]
+    for s in range(count):
         two = shards[s][64:72, :].astype(F32)
         for i in range(2):
-            at = lax.rem(core + i, 2) * 8 + source(slot, s)
-            line_ref[pl.ds(at, 1), :] = two[i:i + 1, :]
-    out_ref[...] = line_ref[...].astype(BF16)
+            at = lax.rem(core + i, 2) * 8 + source(slot, first + s)
+            total = jnp.where(row == at, two[i:i + 1, :], total)
+    out_ref[...] = total.astype(out_ref.dtype)
 
 
 def early_kernel(*refs):
@@ -357,7 +360,11 @@
         early_kernel, [((3, 320, WIDTH), BF16)], [((320, WIDTH), F32)], *shards[:5], qkv_weight
     )
     shards[0], early = lax.optimization_barrier((shards[0], early))
-    texts, = call(text_kernel, [((16, D), BF16)], [((16, D), F32)], *shards)
+    kept, = call(
+        functools.partial(text_kernel, 0, 7), [((16, D), F32)], [], *shards[:7],
+        jnp.zeros((16, D), F32),
+    )
+    texts, = call(functools.partial(text_kernel, 7, 1), [((16, D), BF16)], [], shards[7], kept)
     texts = [texts, over_dp(texts, 1, 0, 0)]
     part, qkv, probs, attended = call(
         forward_kernel,

time: 75 us -> 74.5 us (level)
  starting transfers between devices: 23 us -> 22.1 us
    ppermute x1, starting transfers between devices: 6.1 us -> 5.14 us  [body(): other = lax.ppermute(give, 'dp', [(i, i ^ 1) for i in range(DP)])]
    pallas_call x8 -> x9, Pallas kernels: 8.76 us -> 8.85 us  [call(): pl.pallas_call(kernel, out_shape=[jax.ShapeDtypeStruct(*o) for o in outs]...]
  transfers between devices with their start and end apart: 13 -> 13, of which waited for: 6 -> 5; matrix products, arithmetic and copies ran while one was open for 1% -> 1% of each run, Pallas kernels for 5% -> 5%
where the time goes in v6:
time: 74.5 us; the launch traced here: 74.1 us
  blocking collectives  28.1 us (38%)
  starting transfers between devices  22.1 us (30%)
  Pallas kernels  8.85 us (12%)
  waiting for transfers between devices  7.77 us (10%)
  local copies, waits for them, and re-layouts  5.07 us (7%)
  between operations  2.07 us (3%)
    all_to_all x1, blocking collectives, body(): lax.all_to_all(send, 'dp', 0, 0, axis_index_groups=[list(range(c, DP, 2))...  16.5 us
    all_to_all x1, blocking collectives, body(): parts = lax.all_to_all(part, 'mp', 0, 0)  11.5 us
    ppermute x7, starting transfers between devices, over_mp(): return lax.ppermute(block, 'mp', route)  11.3 us
    pallas_call x9, Pallas kernels, call(): pl.pallas_call(kernel, out_shape=[jax.ShapeDtypeStruct(*o) for o in outs]...  8.85 us
    ppermute x5, starting transfers between devices, over_dp(): return lax.ppermute(block, 'dp', route)  5.65 us
    ppermute x1, starting transfers between devices, body(): other = lax.ppermute(give, 'dp', [(i, i ^ 1) for i in range(DP)])  5.14 us
    ppermute x7, waiting for transfers between devices, over_mp(): return lax.ppermute(block, 'mp', route)  4.49 us
    unnamed x15, local copies, waits for them, and re-layouts  4.18 us
  transfers between devices with their start and end apart: 13, of which 5 were waited for; matrix products, arithmetic and copies ran while one was open for 1% of the time, Pallas kernels for 5%

profile of v6, /device:TPU:1, one launch (start us, length us, event | category | flops | bytes accessed | tf_op | source)
XLA Modules:
  0.0 74.1 jit_solution(2943221387723596536)
XLA Ops:
  0.6 1.5 %collective-permute-start = (bf16[1,1536]{1,0:T(2,128)(2,1)}, bf16[1,1536]{1,0:T(2,128)(2,1)S(1)}, u32[]{:S(2)}, u32[]{:S(2)}) collective-permute-start(bf16[1,1536]{1,0:T(2,128)(2,1)} %text_ref.1), channel_id=1, source_target_pairs={{0,8},{8,0},{16,24},{24,16},{32,40},{40,32},{48,56},{56,48},{64,72... | collective-permute-start | bytes 9224 | tf_op jit(solution)/shard_map/ppermute | solution.py:319
  2.1 0.0 copy-start.2
  2.1 0.9 %copy-done.2 = bf16[8,12288]{1,0:T(8,128)(2,1)S(1)} copy-done((bf16[8,12288]{1,0:T(8,128)(2,1)S(1)}, bf16[8,12288]{1,0:T(8,128)(2,1)}, u32[]{:S(2)}) %copy-start.2) | copy-done | bytes 196632
  3.1 0.3 shard_map.94
  3.4 0.8 %dynamic_update_slice.6 = bf16[72,1536]{1,0:T(8,128)(2,1)S(1)} dynamic-update-slice(bf16[72,1536]{1,0:T(8,128)(2,1)S(1)} %get-tuple-element.29, bf16[1,1536]{1,0:T(2,128)(2,1)} %text_ref.1, s32[]{:T(128)} %constant.0.clone.1, s32[]{:T(128)} %constant.1.clone.1) | dynamic-update-slice | bytes 6148 | tf_op jit(solution)/shard_map/dynamic_update_slice | solution.py:340
  4.2 0.0 collective-permute-done
  4.2 0.1 dynamic_update_slice.7.refs_0_
  4.3 3.1 %collective-permute-start.2 = (bf16[72,1536]{1,0:T(8,128)(2,1)S(1)}, bf16[72,1536]{1,0:T(8,128)(2,1)S(1)}, u32[]{:S(2)}, u32[]{:S(2)}) collective-permute-start(bf16[72,1536]{1,0:T(8,128)(2,1)S(1)} %dynamic_update_slice.7.refs_0_), channel_id=1, source_target_pairs={{0,1},{1,0},{2,3},{3,2},{4,5},{5,4},{6,7},{7,6},{8,9},{9,8},{10,11... | collective-permute-start | bytes 663560 | tf_op jit(solution)/shard_map/ppermute | solution.py:312
  7.3 3.6 %collective-permute-start.4 = (bf16[72,1536]{1,0:T(8,128)(2,1)S(1)}, bf16[72,1536]{1,0:T(8,128)(2,1)S(1)}, u32[]{:S(2)}, u32[]{:S(2)}) collective-permute-start(bf16[72,1536]{1,0:T(8,128)(2,1)S(1)} %dynamic_update_slice.7.refs_0_), channel_id=1, source_target_pairs={{0,4},{1,5},{2,6},{3,7},{4,0},{5,1},{6,2},{7,3},{8,12},{9,13},{10,... | collective-permute-start | bytes 663560 | tf_op jit(solution)/shard_map/ppermute | solution.py:312
  10.9 0.4 collective-permute-start.3
  11.4 1.0 %collective-permute-start.1 = (bf16[72,1536]{1,0:T(8,128)(2,1)S(1)}, bf16[72,1536]{1,0:T(8,128)(2,1)S(1)}, u32[]{:S(2)}, u32[]{:S(2)}) collective-permute-start(bf16[72,1536]{1,0:T(8,128)(2,1)S(1)} %dynamic_update_slice.7.refs_0_), channel_id=1, source_target_pairs={{0,2},{1,3},{2,4},{3,5},{4,6},{5,7},{6,0},{7,1},{8,10},{9,11},{10,... | collective-permute-start | bytes 663560 | tf_op jit(solution)/shard_map/ppermute | solution.py:312
  12.4 0.0 copy-start
  12.4 1.5 %copy-done = bf16[3,192,1536]{2,1,0:T(8,128)(2,1)S(1)} copy-done((bf16[3,192,1536]{2,1,0:T(8,128)(2,1)S(1)}, bf16[3,192,1536]{2,1,0:T(8,128)(2,1)}, u32[]{:S(2)}) %copy-start) | copy-done | bytes 1769496
  13.9 0.0 copy-start.1
  13.9 1.1 %copy-done.1 = bf16[192,1536]{1,0:T(8,128)(2,1)S(1)} copy-done((bf16[192,1536]{1,0:T(8,128)(2,1)S(1)}, bf16[192,1536]{1,0:T(8,128)(2,1)}, u32[]{:S(2)}) %copy-start.1) | copy-done | bytes 589848
  15.0 0.0 copy-start.3
  15.0 0.7 copy-done.3
  15.7 0.8 %shard_map.96 = (bf16[3,192,1536]{2,1,0:T(8,128)(2,1)S(1)}, bf16[192,1536]{1,0:T(8,128)(2,1)S(1)}) custom-call(bf16[3,192,1536]{2,1,0:T(8,128)(2,1)S(1)} %copy-done, bf16[192,1536]{1,0:T(8,128)(2,1)S(1)} %copy-done.1, f32[12,128]{1,0:T(8,128)S(1)} %bitcast.2), custom_call_target="tpu_custom_call" | custom-call | tf_op jit(solution)/shard_map/pallas_call | solution.py:300
  16.5 0.0 collective-permute-done.2.refs_1_
  16.5 1.7 %collective-permute-start.6 = (bf16[72,1536]{1,0:T(8,128)(2,1)S(1)}, bf16[72,1536]{1,0:T(8,128)(2,1)S(1)}, u32[]{:S(2)}, u32[]{:S(2)}) collective-permute-start(bf16[72,1536]{1,0:T(8,128)(2,1)S(1)} %collective-permute-done.2.refs_1_), channel_id=1, source_target_pairs={{0,6},{1,7},{2,0},{3,1},{4,2},{5,3},{6,4},{7,5},{8,14},{9,15},{10,... | collective-permute-start | bytes 663560 | tf_op jit(solution)/shard_map/ppermute | solution.py:312
  18.2 0.0 collective-permute-start.5
  18.2 0.0 collective-permute-done.4.refs_4_
  18.2 1.4 %collective-permute-start.7 = (bf16[72,1536]{1,0:T(8,128)(2,1)S(1)}, bf16[72,1536]{1,0:T(8,128)(2,1)S(1)}, u32[]{:S(2)}, u32[]{:S(2)}) collective-permute-start(bf16[72,1536]{1,0:T(8,128)(2,1)S(1)} %collective-permute-done.4.refs_4_), channel_id=1, source_target_pairs={{0,1},{1,0},{2,3},{3,2},{4,5},{5,4},{6,7},{7,6},{8,9},{9,8},{10,11... | collective-permute-start | bytes 663560 | tf_op jit(solution)/shard_map/ppermute | solution.py:312
  21.0 0.6 collective-permute-done.1.refs_2_
  21.6 0.2 collective-permute-done.3.refs_3_
  21.7 1.0 %shard_map.97.refs_3_ = bf16[3,320,192]{2,1,0:T(8,128)(2,1)S(1)} custom-call(bf16[72,1536]{1,0:T(8,128)(2,1)S(1)} %dynamic_update_slice.7.refs_0_, bf16[72,1536]{1,0:T(8,128)(2,1)S(1)} %collective-permute-done.2.refs_1_, bf16[72,1536]{1,0:T(8,128)(2,1)S(1)} %collective-permute-done.1.refs_2_, bf16[72,1536]{1,0:T(8,128)(2,1)S(1)} %collective-permute-done.3.refs_3_, ...), custom_call_target="tpu_custom_call" | custom-call | tf_op jit(solution)/shard_map/pallas_call | solution.py:300
  22.7 3.7 %collective-permute-done.6.refs_1_.refs_6_ = bf16[72,1536]{1,0:T(8,128)(2,1)S(1)} collective-permute-done((bf16[72,1536]{1,0:T(8,128)(2,1)S(1)}, bf16[72,1536]{1,0:T(8,128)(2,1)S(1)}, u32[]{:S(2)}, u32[]{:S(2)}) %collective-permute-start.6) | collective-permute-done | bytes 221216 | tf_op jit(solution)/shard_map/ppermute | solution.py:312
  26.5 0.0 collective-permute-done.5.refs_0_.refs_5_
  26.5 0.1 shard_map.99.refs_1_
  26.6 0.0 collective-permute-done.7.refs_2_.refs_0_.refs_7_
  26.7 0.5 collective-permute-start.8
  27.1 1.2 %shard_map.98 = (bf16[8,8,1536]{2,1,0:T(8,128)(2,1)S(1)}, bf16[3,512,192]{2,1,0:T(8,128)(2,1)S(1)}, bf16[16,64,64]{2,1,0:T(8,128)(2,1)S(1)}, f32[8,192]{1,0:T(8,128)S(1)}) custom-call(bf16[72,1536]{1,0:T(8,128)(2,1)S(1)} %collective-permute-done.5.refs_0_.refs_5_, bf16[72,1536]{1,0:T(8,128)(2,1)S(1)} %collective-permute-done.6.refs_1_.refs_6_, ...), custom_call_target="tpu_custom_call" | custom-call | tf_op jit(solution)/shard_map/pallas_call | solution.py:300
  28.4 1.3 %collective-permute-done.8 = bf16[16,1536]{1,0:T(8,128)(2,1)S(1)} collective-permute-done((bf16[16,1536]{1,0:T(8,128)(2,1)S(1)}, bf16[16,1536]{1,0:T(8,128)(2,1)S(1)}, u32[]{:S(2)}, u32[]{:S(2)}) %collective-permute-start.8) | collective-permute-done | bytes 49184 | tf_op jit(solution)/shard_map/ppermute | solution.py:319
  29.7 2.5 %collective-permute-start.11 = (bf16[64,1536]{1,0:T(8,128)(2,1)S(1)}, bf16[64,1536]{1,0:T(8,128)(2,1)S(1)}, u32[]{:S(2)}, u32[]{:S(2)}) collective-permute-start(bf16[64,1536]{1,0:T(8,128)(2,1)S(1)} %constant_dynamic-update-slice_fusion.refs_8_), channel_id=1, source_target_pairs={{0,48},{8,56},{16,0},{24,8},{32,16},{40,24},{48,32},{56,40},{64,11... | collective-permute-start | bytes 589832 | tf_op jit(solution)/shard_map/ppermute | solution.py:319
  32.3 0.5 collective-permute-start.10
  32.8 0.6 collective-permute-start.9
  33.4 11.5 %all_to_all.10.refs_12_ = bf16[8,8,1536]{2,1,0:T(8,128)(2,1)S(1)} all-to-all(bf16[8,8,1536]{2,1,0:T(8,128)(2,1)S(1)} %get-tuple-element.48), channel_id=1, replica_groups=mesh['dp'=16,'mp'=8] {'mp'}, dimensions={0} | all-to-all | bytes 393216 | tf_op jit(solution)/shard_map/all_to_all | solution.py:381
  44.9 0.0 collective-permute-done.11.refs_11_
  44.9 0.0 collective-permute-done.10.refs_10_
  44.9 0.0 collective-permute-done.9.refs_9_
  44.9 3.8 %shard_map.101 = (bf16[8,400,128]{2,1,0:T(8,128)(2,1)S(1)}, bf16[8,400,128]{2,1,0:T(8,128)(2,1)S(1)}) custom-call(bf16[72,1536]{1,0:T(8,128)(2,1)S(1)} %dynamic_update_slice.7.refs_0_, bf16[72,1536]{1,0:T(8,128)(2,1)S(1)} %collective-permute-done.2.refs_1_, bf16[72,1536]{1,0:T(8,128)(2,1)S(1)} %collective-permute-done.1.refs_2_, ...), custom_call_target="tpu_custom_call" | custom-call | tf_op jit(solution)/shard_map/pallas_call | solution.py:300
  48.8 5.1 %collective-permute-start.12 = (bf16[8,400,128]{2,1,0:T(8,128)(2,1)S(1)}, bf16[8,400,128]{2,1,0:T(8,128)(2,1)S(1)}, u32[]{:S(2)}, u32[]{:S(2)}) collective-permute-start(bf16[8,400,128]{2,1,0:T(8,128)(2,1)S(1)} %get-tuple-element.54), channel_id=1, source_target_pairs={{0,8},{8,0},{16,24},{24,16},{32,40},{40,32},{48,56},{56,48},{64,72... | collective-permute-start | bytes 2457608 | tf_op jit(solution)/shard_map/ppermute | solution.py:388
  53.9 2.0 %collective-permute-done.12 = bf16[8,400,128]{2,1,0:T(8,128)(2,1)S(1)} collective-permute-done((bf16[8,400,128]{2,1,0:T(8,128)(2,1)S(1)}, bf16[8,400,128]{2,1,0:T(8,128)(2,1)S(1)}, u32[]{:S(2)}, u32[]{:S(2)}) %collective-permute-start.12) | collective-permute-done | bytes 819232 | tf_op jit(solution)/shard_map/ppermute | solution.py:388
  55.9 0.2 add_convert_fusion
  56.1 16.5 %all_to_all.11.r_ref = bf16[8,400,128]{2,1,0:T(8,128)(2,1)S(1)} all-to-all(bf16[8,400,128]{2,1,0:T(8,128)(2,1)S(1)} %add_convert_fusion), channel_id=1, replica_groups={{0,16,32,48,64,80,96,112},{8,24,40,56,72,88,104,120},{1,17,33,49,65,81,..., dimensions={0} | all-to-all | bytes 1638400 | tf_op jit(solution)/shard_map/all_to_all | solution.py:390
  72.6 0.0 copy-done.4
  72.6 0.0 copy-done.5
  72.6 1.5 %shard_map.102 = (f32[1,1536]{1,0:T(1,128)}, f32[3,192,96]{2,1,0:T(8,128)}, f32[192,96]{1,0:T(8,128)}) custom-call(bf16[8,400,128]{2,1,0:T(8,128)(2,1)S(1)} %all_to_all.11.r_ref, bf16[1,1536]{1,0:T(2,128)(2,1)S(1)} %copy-done.5, f32[12,128]{1,0:T(8,128)S(1)} %bitcast.3), custom_call_target="tpu_custom_call" | custom-call | tf_op jit(solution)/shard_map/pallas_call | solution.py:300
  (9 shorter events, 0.1 us)
Async XLA Ops:
  0.6 3.5 %collective-permute-start = (bf16[1,1536]{1,0:T(2,128)(2,1)}, bf16[1,1536]{1,0:T(2,128)(2,1)S(1)}, u32[]{:S(2)}, u32[]{:S(2)}) collective-permute-start(bf16[1,1536]{1,0:T(2,128)(2,1)} %text_ref.1), channel_id=1, source_target_pairs={{0,8},{8,0},{16,24},{24,16},{32,40},{40,32},{48,56},{56,48},{64,72... | collective-permute-start | bytes 9224 | tf_op jit(solution)/shard_map/ppermute | solution.py:319
  2.1 0.9 %copy-start.2 = (bf16[8,12288]{1,0:T(8,128)(2,1)S(1)}, bf16[8,12288]{1,0:T(8,128)(2,1)}, u32[]{:S(2)}) copy-start(bf16[8,12288]{1,0:T(8,128)(2,1)} %tok_ref.1) | copy-start | bytes 589828
  4.3 12.2 %collective-permute-start.2 = (bf16[72,1536]{1,0:T(8,128)(2,1)S(1)}, bf16[72,1536]{1,0:T(8,128)(2,1)S(1)}, u32[]{:S(2)}, u32[]{:S(2)}) collective-permute-start(bf16[72,1536]{1,0:T(8,128)(2,1)S(1)} %dynamic_update_slice.7.refs_0_), channel_id=1, source_target_pairs={{0,1},{1,0},{2,3},{3,2},{4,5},{5,4},{6,7},{7,6},{8,9},{9,8},{10,11... | collective-permute-start | bytes 663560 | tf_op jit(solution)/shard_map/ppermute | solution.py:312
  7.3 10.9 %collective-permute-start.4 = (bf16[72,1536]{1,0:T(8,128)(2,1)S(1)}, bf16[72,1536]{1,0:T(8,128)(2,1)S(1)}, u32[]{:S(2)}, u32[]{:S(2)}) collective-permute-start(bf16[72,1536]{1,0:T(8,128)(2,1)S(1)} %dynamic_update_slice.7.refs_0_), channel_id=1, source_target_pairs={{0,4},{1,5},{2,6},{3,7},{4,0},{5,1},{6,2},{7,3},{8,12},{9,13},{10,... | collective-permute-start | bytes 663560 | tf_op jit(solution)/shard_map/ppermute | solution.py:312
  10.9 10.8 %collective-permute-start.3 = (bf16[72,1536]{1,0:T(8,128)(2,1)S(1)}, bf16[72,1536]{1,0:T(8,128)(2,1)S(1)}, u32[]{:S(2)}, u32[]{:S(2)}) collective-permute-start(bf16[72,1536]{1,0:T(8,128)(2,1)S(1)} %dynamic_update_slice.7.refs_0_), channel_id=1, source_target_pairs={{0,6},{1,7},{2,0},{3,1},{4,2},{5,3},{6,4},{7,5},{8,14},{9,15},{10,... | collective-permute-start | bytes 663560 | tf_op jit(solution)/shard_map/ppermute | solution.py:312
  11.4 10.2 %collective-permute-start.1 = (bf16[72,1536]{1,0:T(8,128)(2,1)S(1)}, bf16[72,1536]{1,0:T(8,128)(2,1)S(1)}, u32[]{:S(2)}, u32[]{:S(2)}) collective-permute-start(bf16[72,1536]{1,0:T(8,128)(2,1)S(1)} %dynamic_update_slice.7.refs_0_), channel_id=1, source_target_pairs={{0,2},{1,3},{2,4},{3,5},{4,6},{5,7},{6,0},{7,1},{8,10},{9,11},{10,... | collective-permute-start | bytes 663560 | tf_op jit(solution)/shard_map/ppermute | solution.py:312
  12.4 1.5 %copy-start = (bf16[3,192,1536]{2,1,0:T(8,128)(2,1)S(1)}, bf16[3,192,1536]{2,1,0:T(8,128)(2,1)}, u32[]{:S(2)}) copy-start(bf16[3,192,1536]{2,1,0:T(8,128)(2,1)} %w_hbm) | copy-start | bytes 5308420
  13.9 1.1 %copy-start.1 = (bf16[192,1536]{1,0:T(8,128)(2,1)S(1)}, bf16[192,1536]{1,0:T(8,128)(2,1)}, u32[]{:S(2)}) copy-start(bf16[192,1536]{1,0:T(8,128)(2,1)} %wo_hbm) | copy-start | bytes 1769476
  15.0 0.7 copy-start.3
  16.5 10.0 %collective-permute-start.6 = (bf16[72,1536]{1,0:T(8,128)(2,1)S(1)}, bf16[72,1536]{1,0:T(8,128)(2,1)S(1)}, u32[]{:S(2)}, u32[]{:S(2)}) collective-permute-start(bf16[72,1536]{1,0:T(8,128)(2,1)S(1)} %collective-permute-done.2.refs_1_), channel_id=1, source_target_pairs={{0,6},{1,7},{2,0},{3,1},{4,2},{5,3},{6,4},{7,5},{8,14},{9,15},{10,... | collective-permute-start | bytes 663560 | tf_op jit(solution)/shard_map/ppermute | solution.py:312
  18.2 8.3 %collective-permute-start.5 = (bf16[72,1536]{1,0:T(8,128)(2,1)S(1)}, bf16[72,1536]{1,0:T(8,128)(2,1)S(1)}, u32[]{:S(2)}, u32[]{:S(2)}) collective-permute-start(bf16[72,1536]{1,0:T(8,128)(2,1)S(1)} %collective-permute-done.2.refs_1_), channel_id=1, source_target_pairs={{0,2},{1,3},{2,4},{3,5},{4,6},{5,7},{6,0},{7,1},{8,10},{9,11},{10,... | collective-permute-start | bytes 663560 | tf_op jit(solution)/shard_map/ppermute | solution.py:312
  18.2 8.4 %collective-permute-start.7 = (bf16[72,1536]{1,0:T(8,128)(2,1)S(1)}, bf16[72,1536]{1,0:T(8,128)(2,1)S(1)}, u32[]{:S(2)}, u32[]{:S(2)}) collective-permute-start(bf16[72,1536]{1,0:T(8,128)(2,1)S(1)} %collective-permute-done.4.refs_4_), channel_id=1, source_target_pairs={{0,1},{1,0},{2,3},{3,2},{4,5},{5,4},{6,7},{7,6},{8,9},{9,8},{10,11... | collective-permute-start | bytes 663560 | tf_op jit(solution)/shard_map/ppermute | solution.py:312
  26.7 3.0 %collective-permute-start.8 = (bf16[16,1536]{1,0:T(8,128)(2,1)S(1)}, bf16[16,1536]{1,0:T(8,128)(2,1)S(1)}, u32[]{:S(2)}, u32[]{:S(2)}) collective-permute-start(bf16[16,1536]{1,0:T(8,128)(2,1)S(1)} %shard_map.100), channel_id=1, source_target_pairs={{0,64},{8,72},{16,80},{24,88},{32,96},{40,104},{48,112},{56,120},{... | collective-permute-start | bytes 147464 | tf_op jit(solution)/shard_map/ppermute | solution.py:319
  29.7 15.2 %collective-permute-start.11 = (bf16[64,1536]{1,0:T(8,128)(2,1)S(1)}, bf16[64,1536]{1,0:T(8,128)(2,1)S(1)}, u32[]{:S(2)}, u32[]{:S(2)}) collective-permute-start(bf16[64,1536]{1,0:T(8,128)(2,1)S(1)} %constant_dynamic-update-slice_fusion.refs_8_), channel_id=1, source_target_pairs={{0,48},{8,56},{16,0},{24,8},{32,16},{40,24},{48,32},{56,40},{64,11... | collective-permute-start | bytes 589832 | tf_op jit(solution)/shard_map/ppermute | solution.py:319
  32.3 12.6 %collective-permute-start.10 = (bf16[64,1536]{1,0:T(8,128)(2,1)S(1)}, bf16[64,1536]{1,0:T(8,128)(2,1)S(1)}, u32[]{:S(2)}, u32[]{:S(2)}) collective-permute-start(bf16[64,1536]{1,0:T(8,128)(2,1)S(1)} %constant_dynamic-update-slice_fusion.refs_8_), channel_id=1, source_target_pairs={{0,32},{8,40},{16,48},{24,56},{32,0},{40,8},{48,16},{56,24},{64,96... | collective-permute-start | bytes 589832 | tf_op jit(solution)/shard_map/ppermute | solution.py:319
  32.8 12.1 %collective-permute-start.9 = (bf16[64,1536]{1,0:T(8,128)(2,1)S(1)}, bf16[64,1536]{1,0:T(8,128)(2,1)S(1)}, u32[]{:S(2)}, u32[]{:S(2)}) collective-permute-start(bf16[64,1536]{1,0:T(8,128)(2,1)S(1)} %constant_dynamic-update-slice_fusion.refs_8_), channel_id=1, source_target_pairs={{0,16},{8,24},{16,32},{24,40},{32,48},{40,56},{48,0},{56,8},{64,80... | collective-permute-start | bytes 589832 | tf_op jit(solution)/shard_map/ppermute | solution.py:319
  48.8 7.1 %collective-permute-start.12 = (bf16[8,400,128]{2,1,0:T(8,128)(2,1)S(1)}, bf16[8,400,128]{2,1,0:T(8,128)(2,1)S(1)}, u32[]{:S(2)}, u32[]{:S(2)}) collective-permute-start(bf16[8,400,128]{2,1,0:T(8,128)(2,1)S(1)} %get-tuple-element.54), channel_id=1, source_target_pairs={{0,8},{8,0},{16,24},{24,16},{32,40},{40,32},{48,56},{56,48},{64,72... | collective-permute-start | bytes 2457608 | tf_op jit(solution)/shard_map/ppermute | solution.py:388
  55.9 16.8 %copy-start.4 = (f32[1536]{0:T(1024)S(1)}, f32[1536]{0:T(1024)}, u32[]{:S(2)}) copy-start(f32[1536]{0:T(1024)} %param.8) | copy-start | bytes 18436
  55.9 16.8 %copy-start.5 = (bf16[1,1536]{1,0:T(2,128)(2,1)S(1)}, bf16[1,1536]{1,0:T(2,128)(2,1)}, u32[]{:S(2)}) copy-start(bf16[1,1536]{1,0:T(2,128)(2,1)} %text_ref.1) | copy-start | bytes 9220

commit v7 on v6

--- a/solution.py
+++ b/solution.py
@@ -65,22 +65,6 @@
     scalar_ref[1:2, :] = jnp.full((1, 128), bias_ref[0], F32)
 
 
-def load_kernel(w_hbm, wo_hbm, gain_ref, w_ref, wo_ref, raw_ref, sems):
-    copies = [
-        pltpu.make_async_copy(w_hbm, raw_ref, sems.at[0]),
-        pltpu.make_async_copy(wo_hbm, wo_ref, sems.at[1]),
-    ]
-    for copy in copies:
-        copy.start()
-    copies[0].wait()
-    for i in range(12):
-        part = slice(i * 128, (i + 1) * 128)
-        for c in range(3):
-            scaled = raw_ref[c, :, part].astype(F32) * gain_ref[i:i + 1, :]
-            w_ref[c, :, part] = scaled.astype(BF16)
-    copies[1].wait()
-
-
 STEPS = ((0, 0), (0, 1), (1, 0), (3, 0), (2, 0), (1, 1), (3, 1), (2, 1))
 
 
@@ -104,7 +88,12 @@
 
 
 def early_kernel(*refs):
-    shards, (w_ref, qkv_ref, wide_ref) = refs[:5], refs[5:]
+    shards, (raw_ref, gain_ref, qkv_ref, w_ref, wide_ref) = refs[:5], refs[5:]
+    for i in range(12):
+        part = slice(i * 128, (i + 1) * 128)
+        for c in range(3):
+            scaled = raw_ref[c, :, part].astype(F32) * gain_ref[i:i + 1, :]
+            w_ref[c, :, part] = scaled.astype(BF16)
     normed = jnp.concatenate([r[0:64, :] for r in shards], axis=0)
     for c in range(3):
         wide_ref[...] = dot(normed, w_ref[c], LAST)
@@ -117,7 +106,7 @@
 
 def forward_kernel(*refs):
     shards, (early_ref, w_ref, wo_ref, sum_ref), refs = refs[:3], refs[3:7], refs[7:]
-    part_ref, qkv_ref, probs_ref, att_ref, wide_ref = refs
+    part_ref, qkv_ref, att_ref, wide_ref = refs
     normed = jnp.concatenate([r[0:64, :] for r in shards], axis=0)
     for c in range(3):
         wide_ref[...] = dot(normed, w_ref[c], LAST)
@@ -126,19 +115,19 @@
                 [early_ref[c, b * 40:(b + 1) * 40, :].astype(F32)]
                 + [wide_ref[(s * 8 + b) * 8:(s * 8 + b) * 8 + 8, :] for s in range(3)], axis=0
             )
-            qkv_ref[c, b * 64:(b + 1) * 64, :] = block.astype(BF16)
+            qkv_ref[c, b * 64:(b + 1) * 64, 0:WIDTH] = block.astype(BF16)
     lane = lanes((64, WIDTH))
     for b in range(IMG):
         rows = slice(b * 64, (b + 1) * 64)
-        q, k = qkv_ref[0, rows, :], qkv_ref[1, rows, :]
-        v = qkv_ref[2, rows, :].astype(F32)
+        q, k = qkv_ref[0, rows, 0:WIDTH], qkv_ref[1, rows, 0:WIDTH]
+        v = qkv_ref[2, rows, 0:WIDTH].astype(F32)
         columns = []
         for h in range(2):
             inside = lane < DH if h == 0 else lane >= DH
             score = dot(k, jnp.where(inside, q, jnp.zeros_like(q)), LAST) * SCALE
             weights = jnp.exp(score)
             probs = (weights / jnp.sum(weights, axis=0, keepdims=True)).astype(BF16)
-            probs_ref[b * 2 + h] = probs
+            qkv_ref[h, rows, WIDTH:256] = probs
             columns.append(jnp.sum(probs.astype(F32), axis=1, keepdims=True))
         attended = jnp.sum(jnp.where(lane < DH, columns[0], columns[1]) * v, axis=0, keepdims=True)
         att_ref[b:b + 1, :] = attended
@@ -149,10 +138,14 @@
         part_ref[d] = part
 
 
+def join_kernel(*refs):
+    refs[-1][...] = jnp.concatenate([r[...] for r in refs[:-1]], axis=0)
+
+
 def backward_kernel(*refs):
-    shards, texts, refs = refs[:MP], refs[MP:MP + 4], refs[MP + 4:]
-    part_ref, qkv_ref, probs_ref, att_ref, scalar_ref, wo_ref = refs[:6]
-    keep_ref, give_ref, grad_ref, turn_ref, text_ref, both_ref = refs[6:]
+    shards, t_ref, refs = refs[:MP], refs[MP], refs[MP + 1:]
+    part_ref, qkv_ref, att_ref, scalar_ref, wo_ref = refs[:5]
+    keep_ref, give_ref, grad_ref, turn_ref, text_ref, both_ref = refs[5:]
     me = lax.axis_index("dp")
     slot = lax.axis_index("mp")
     core = lax.rem(me, 2)
@@ -162,7 +155,7 @@
     scale = scalar_ref[0:1, :]
     image_inv = lax.rsqrt(jnp.sum(pooled * pooled, axis=-1, keepdims=True) + EPS)
     unit = pooled * image_inv
-    text = jnp.concatenate([r[0:32, :] for r in texts], axis=0)
+    text = t_ref[...]
     wide_text = text.astype(F32)
     square = pieces(wide_text * wide_text, 2)
     ones = jnp.ones((IMG, D), BF16)
@@ -202,13 +195,13 @@
     slim = lanes((64, 64))
     for b in range(IMG):
         rows = slice(b * 64, (b + 1) * 64)
-        q, k = qkv_ref[0, rows, :], qkv_ref[1, rows, :]
-        product = qkv_ref[2, rows, :].astype(F32) * wide_attend[b:b + 1, :]
+        q, k = qkv_ref[0, rows, 0:WIDTH], qkv_ref[1, rows, 0:WIDTH]
+        product = qkv_ref[2, rows, 0:WIDTH].astype(F32) * wide_attend[b:b + 1, :]
         query_grad, key_grad, factor = [], [], jnp.zeros((64, 64), F32)
         for h in range(2):
             inside = lane < DH if h == 0 else lane >= DH
             prob_grad = jnp.sum(jnp.where(inside, product, 0.0), axis=1, keepdims=True)
-            probs = probs_ref[b * 2 + h].astype(F32)
+            probs = qkv_ref[h, rows, WIDTH:256].astype(F32)
             mean = jnp.sum(probs * prob_grad, axis=0, keepdims=True)
             score_grad = (probs * (prob_grad - mean) * SCALE).astype(BF16)
             query_grad.append(dot(score_grad, k, FIRST))
@@ -340,24 +333,15 @@
     own = lax.dynamic_update_slice(own, text_embed, (64, 0))
     own = lax.dynamic_update_slice(own, over_dp(text_embed, 0, 0, 1), (65, 0))
     shards = first_step(own)
-    own, qkv_weight, out_weight, gain = lax.optimization_barrier(
-        (own, qkv_weight, out_weight, norm_gain)
-    )
-    qkv_weight, out_weight = call(
-        load_kernel,
-        [((3, WIDTH, D), BF16), ((WIDTH, D), BF16)],
-        [((3, WIDTH, D), BF16), pltpu.SemaphoreType.DMA((2,))],
-        qkv_weight, out_weight, gain.reshape(12, 128), specs=[ANY, ANY, HERE],
-    )
-    shards[1], qkv_weight, out_weight = lax.optimization_barrier(
-        (shards[1], qkv_weight, out_weight)
-    )
     shards += second_step(shards)
     shards[2], log_temp, logit_bias = lax.optimization_barrier((shards[2], log_temp, logit_bias))
     scalars, = call(scalar_kernel, [((2, 128), F32)], [], log_temp, logit_bias, specs=[SMEM] * 2)
     shards[0], scalars = lax.optimization_barrier((shards[0], scalars))
-    early, = call(
-        early_kernel, [((3, 320, WIDTH), BF16)], [((320, WIDTH), F32)], *shards[:5], qkv_weight
+    early, scaled = call(
+        early_kernel,
+        [((3, 320, WIDTH), BF16), ((3, WIDTH, D), BF16)],
+        [((320, WIDTH), F32)],
+        *shards[:5], qkv_weight, norm_gain.reshape(12, 128),
     )
     shards[0], early = lax.optimization_barrier((shards[0], early))
     kept, = call(
@@ -366,24 +350,23 @@
     )
     texts, = call(functools.partial(text_kernel, 7, 1), [((16, D), BF16)], [], shards[7], kept)
     texts = [texts, over_dp(texts, 1, 0, 0)]
-    part, qkv, probs, attended = call(
+    part, qkv, attended = call(
         forward_kernel,
         [
-            ((MP, IMG, D), BF16), ((3, 512, WIDTH), BF16),
-            ((16, 64, 64), BF16), ((IMG, WIDTH), F32),
+            ((MP, IMG, D), BF16), ((3, 512, 256), BF16), ((IMG, WIDTH), F32),
         ],
         [((192, WIDTH), F32)],
-        *shards[5:], early, qkv_weight, out_weight, token_sum,
-    )
-    part, *texts = lax.optimization_barrier((part, *texts))
-    texts = jnp.concatenate(texts + texts, axis=0)
+        *shards[5:], early, scaled, out_weight, token_sum,
+    )
+    texts = jnp.concatenate(texts, axis=0)
     texts = [texts] + [over_dp(texts, 0, dx, 0) for dx in (1, 2, 3)]
     parts = lax.all_to_all(part, "mp", 0, 0)
+    texts, = call(join_kernel, [((TEXT, D), BF16)], [], *texts)
     keep, give = call(
         backward_kernel,
         [((8, ROWS, 128), BF16)] * 2,
         [((512, 512), F32), ((256, 128), F32), ((256, 128), F32), ((2, 8, ROWS, 128), BF16)],
-        *shards, *texts, parts, qkv, probs, attended, scalars, out_weight,
+        *shards, texts, parts, qkv, attended, scalars, out_weight,
     )
     other = lax.ppermute(give, "dp", [(i, i ^ 1) for i in range(DP)])
     send = (keep.astype(F32) + other.astype(F32)).astype(BF16)

time: 74.5 us -> 71.9 us (0.965)
  blocking collectives: 28.1 us -> 15.7 us
  starting transfers between devices: 22.1 us -> 29.7 us
  local copies, waits for them, and re-layouts: 5.07 us -> 6.01 us
  waiting for transfers between devices: 7.77 us -> 8.6 us
    all_to_all x1 -> x0, blocking collectives: 11.5 us -> none  [body(): parts = lax.all_to_all(part, 'mp', 0, 0)]
    all_to_all x0 -> x1, starting transfers between devices: none -> 5.53 us  [body(): parts = lax.all_to_all(part, 'mp', 0, 0)]
    ppermute x7, starting transfers between devices: 11.3 us -> 15.4 us  [over_mp(): return lax.ppermute(block, 'mp', route)]
    ppermute x5, waiting for transfers between devices: 1.31 us -> 4.39 us  [over_dp(): return lax.ppermute(block, 'dp', route)]
    ppermute x1, starting transfers between devices: 5.14 us -> 2.52 us  [body(): other = lax.ppermute(give, 'dp', [(i, i ^ 1) for i in range(DP)])]
    ppermute x7, waiting for transfers between devices: 4.49 us -> 2.25 us  [over_mp(): return lax.ppermute(block, 'mp', route)]
    unnamed x15 -> x16, local copies, waits for them, and re-layouts: 4.18 us -> 5.13 us
    all_to_all x1, blocking collectives: 16.5 us -> 15.7 us  [body(): lax.all_to_all(send, 'dp', 0, 0, axis_index_groups=[list(range(c, DP, 2))...]
  transfers between devices with their start and end apart: 13 -> 14, of which waited for: 5 -> 8; matrix products, arithmetic and copies ran while one was open for 1% -> 1% of each run, Pallas kernels for 5% -> 5%
where the time goes in v7:
time: 71.9 us; the launch traced here: 71.4 us
  starting transfers between devices  29.7 us (41%)
  blocking collectives  15.7 us (22%)
  Pallas kernels  9.08 us (13%)
  waiting for transfers between devices  8.6 us (12%)
  local copies, waits for them, and re-layouts  6.01 us (8%)
  between operations  2.06 us (3%)
    all_to_all x1, blocking collectives, body(): lax.all_to_all(send, 'dp', 0, 0, axis_index_groups=[list(range(c, DP, 2))...  15.7 us
    ppermute x7, starting transfers between devices, over_mp(): return lax.ppermute(block, 'mp', route)  15.4 us
    pallas_call x9, Pallas kernels, call(): pl.pallas_call(kernel, out_shape=[jax.ShapeDtypeStruct(*o) for o in outs]...  9.08 us
    ppermute x5, starting transfers between devices, over_dp(): return lax.ppermute(block, 'dp', route)  6.27 us
    all_to_all x1, starting transfers between devices, body(): parts = lax.all_to_all(part, 'mp', 0, 0)  5.53 us
    unnamed x16, local copies, waits for them, and re-layouts  5.13 us
    ppermute x5, waiting for transfers between devices, over_dp(): return lax.ppermute(block, 'dp', route)  4.39 us
    ppermute x1, starting transfers between devices, body(): other = lax.ppermute(give, 'dp', [(i, i ^ 1) for i in range(DP)])  2.52 us
  transfers between devices with their start and end apart: 14, of which 8 were waited for; matrix products, arithmetic and copies ran while one was open for 1% of the time, Pallas kernels for 5%

profile of v7, /device:TPU:1, one launch (start us, length us, event | category | flops | bytes accessed | tf_op | source)
XLA Modules:
  0.0 71.4 jit_solution(13131654443649880386)
XLA Ops:
  0.6 1.5 %collective-permute-start = (bf16[1,1536]{1,0:T(2,128)(2,1)}, bf16[1,1536]{1,0:T(2,128)(2,1)S(1)}, u32[]{:S(2)}, u32[]{:S(2)}) collective-permute-start(bf16[1,1536]{1,0:T(2,128)(2,1)} %text_ref.1), channel_id=1, source_target_pairs={{0,8},{8,0},{16,24},{24,16},{32,40},{40,32},{48,56},{56,48},{64,72... | collective-permute-start | bytes 9224 | tf_op jit(solution)/shard_map/ppermute | solution.py:312
  2.1 0.9 %copy-done.4 = bf16[8,12288]{1,0:T(8,128)(2,1)S(1)} copy-done((bf16[8,12288]{1,0:T(8,128)(2,1)S(1)}, bf16[8,12288]{1,0:T(8,128)(2,1)}, u32[]{:S(2)}) %copy-start.4) | copy-done | bytes 196632
  3.1 0.3 shard_map.94
  3.4 0.8 %dynamic_update_slice.6 = bf16[72,1536]{1,0:T(8,128)(2,1)S(1)} dynamic-update-slice(bf16[72,1536]{1,0:T(8,128)(2,1)S(1)} %get-tuple-element.19, bf16[1,1536]{1,0:T(2,128)(2,1)} %text_ref.1, s32[]{:T(128)} %constant.0.clone.1, s32[]{:T(128)} %constant.1.clone.1) | dynamic-update-slice | bytes 6148 | tf_op jit(solution)/shard_map/dynamic_update_slice | solution.py:333
  4.2 0.0 collective-permute-done
  4.2 0.1 dynamic_update_slice.7.refs_0_
  4.3 3.1 %collective-permute-start.2 = (bf16[72,1536]{1,0:T(8,128)(2,1)S(1)}, bf16[72,1536]{1,0:T(8,128)(2,1)S(1)}, u32[]{:S(2)}, u32[]{:S(2)}) collective-permute-start(bf16[72,1536]{1,0:T(8,128)(2,1)S(1)} %dynamic_update_slice.7.refs_0_), channel_id=1, source_target_pairs={{0,1},{1,0},{2,3},{3,2},{4,5},{5,4},{6,7},{7,6},{8,9},{9,8},{10,11... | collective-permute-start | bytes 663560 | tf_op jit(solution)/shard_map/ppermute | solution.py:305
  7.3 3.6 %collective-permute-start.4 = (bf16[72,1536]{1,0:T(8,128)(2,1)S(1)}, bf16[72,1536]{1,0:T(8,128)(2,1)S(1)}, u32[]{:S(2)}, u32[]{:S(2)}) collective-permute-start(bf16[72,1536]{1,0:T(8,128)(2,1)S(1)} %dynamic_update_slice.7.refs_0_), channel_id=1, source_target_pairs={{0,4},{1,5},{2,6},{3,7},{4,0},{5,1},{6,2},{7,3},{8,12},{9,13},{10,... | collective-permute-start | bytes 663560 | tf_op jit(solution)/shard_map/ppermute | solution.py:305
  10.9 0.7 %collective-permute-start.1 = (bf16[72,1536]{1,0:T(8,128)(2,1)S(1)}, bf16[72,1536]{1,0:T(8,128)(2,1)S(1)}, u32[]{:S(2)}, u32[]{:S(2)}) collective-permute-start(bf16[72,1536]{1,0:T(8,128)(2,1)S(1)} %dynamic_update_slice.7.refs_0_), channel_id=1, source_target_pairs={{0,2},{1,3},{2,4},{3,5},{4,6},{5,7},{6,0},{7,1},{8,10},{9,11},{10,... | collective-permute-start | bytes 663560 | tf_op jit(solution)/shard_map/ppermute | solution.py:305
  11.7 1.9 %collective-permute-start.3 = (bf16[72,1536]{1,0:T(8,128)(2,1)S(1)}, bf16[72,1536]{1,0:T(8,128)(2,1)S(1)}, u32[]{:S(2)}, u32[]{:S(2)}) collective-permute-start(bf16[72,1536]{1,0:T(8,128)(2,1)S(1)} %dynamic_update_slice.7.refs_0_), channel_id=1, source_target_pairs={{0,6},{1,7},{2,0},{3,1},{4,2},{5,3},{6,4},{7,5},{8,14},{9,15},{10,... | collective-permute-start | bytes 663560 | tf_op jit(solution)/shard_map/ppermute | solution.py:305
  13.6 0.0 collective-permute-done.2.refs_1_
  13.6 1.0 %collective-permute-start.5 = (bf16[72,1536]{1,0:T(8,128)(2,1)S(1)}, bf16[72,1536]{1,0:T(8,128)(2,1)S(1)}, u32[]{:S(2)}, u32[]{:S(2)}) collective-permute-start(bf16[72,1536]{1,0:T(8,128)(2,1)S(1)} %collective-permute-done.2.refs_1_), channel_id=1, source_target_pairs={{0,2},{1,3},{2,4},{3,5},{4,6},{5,7},{6,0},{7,1},{8,10},{9,11},{10,... | collective-permute-start | bytes 663560 | tf_op jit(solution)/shard_map/ppermute | solution.py:305
  14.6 2.1 %collective-permute-start.6 = (bf16[72,1536]{1,0:T(8,128)(2,1)S(1)}, bf16[72,1536]{1,0:T(8,128)(2,1)S(1)}, u32[]{:S(2)}, u32[]{:S(2)}) collective-permute-start(bf16[72,1536]{1,0:T(8,128)(2,1)S(1)} %collective-permute-done.2.refs_1_), channel_id=1, source_target_pairs={{0,6},{1,7},{2,0},{3,1},{4,2},{5,3},{6,4},{7,5},{8,14},{9,15},{10,... | collective-permute-start | bytes 663560 | tf_op jit(solution)/shard_map/ppermute | solution.py:305
  16.7 0.0 collective-permute-done.4.refs_4_
  16.8 2.9 %collective-permute-start.7 = (bf16[72,1536]{1,0:T(8,128)(2,1)S(1)}, bf16[72,1536]{1,0:T(8,128)(2,1)S(1)}, u32[]{:S(2)}, u32[]{:S(2)}) collective-permute-start(bf16[72,1536]{1,0:T(8,128)(2,1)S(1)} %collective-permute-done.4.refs_4_), channel_id=1, source_target_pairs={{0,1},{1,0},{2,3},{3,2},{4,5},{5,4},{6,7},{7,6},{8,9},{9,8},{10,11... | collective-permute-start | bytes 663560 | tf_op jit(solution)/shard_map/ppermute | solution.py:305
  21.0 0.6 collective-permute-done.1.refs_2_
  21.6 0.1 collective-permute-done.3.refs_3_
  21.7 1.5 %copy-done.1 = bf16[3,192,1536]{2,1,0:T(8,128)(2,1)S(1)} copy-done((bf16[3,192,1536]{2,1,0:T(8,128)(2,1)S(1)}, bf16[3,192,1536]{2,1,0:T(8,128)(2,1)}, u32[]{:S(2)}) %copy-start.1) | copy-done | bytes 1769496
  23.2 0.7 copy-done.5
  23.9 1.1 %shard_map.96 = (bf16[3,320,192]{2,1,0:T(8,128)(2,1)S(1)}, bf16[3,192,1536]{2,1,0:T(8,128)(2,1)S(1)}) custom-call(bf16[72,1536]{1,0:T(8,128)(2,1)S(1)} %dynamic_update_slice.7.refs_0_, bf16[72,1536]{1,0:T(8,128)(2,1)S(1)} %collective-permute-done.2.refs_1_, bf16[72,1536]{1,0:T(8,128)(2,1)S(1)} %collective-permute-done.1.refs_2_, ...), custom_call_target="tpu_custom_call" | custom-call | tf_op jit(solution)/shard_map/pallas_call | solution.py:293
  25.0 0.0 copy-start
  25.0 1.3 %collective-permute-done.5.refs_5_.refs_0_ = bf16[72,1536]{1,0:T(8,128)(2,1)S(1)} collective-permute-done((bf16[72,1536]{1,0:T(8,128)(2,1)S(1)}, bf16[72,1536]{1,0:T(8,128)(2,1)S(1)}, u32[]{:S(2)}, u32[]{:S(2)}) %collective-permute-start.5) | collective-permute-done | bytes 221216 | tf_op jit(solution)/shard_map/ppermute | solution.py:305
  26.3 0.1 collective-permute-done.6.refs_6_.refs_1_
  26.5 0.1 shard_map.97.refs_1_
  26.6 0.0 collective-permute-done.7.refs_0_.refs_2_.refs_7_
  26.6 0.5 collective-permute-start.8
  27.1 0.0 copy-done
  27.1 2.0 %shard_map.100 = (bf16[8,8,1536]{2,1,0:T(8,128)(2,1)}, bf16[3,512,256]{2,1,0:T(8,128)(2,1)S(1)}, f32[8,192]{1,0:T(8,128)S(1)}) custom-call(bf16[72,1536]{1,0:T(8,128)(2,1)S(1)} %collective-permute-done.5.refs_5_.refs_0_, bf16[72,1536]{1,0:T(8,128)(2,1)S(1)} %collective-permute-done.6.refs_6_.refs_1_, ...), custom_call_target="tpu_custom_call" | custom-call | tf_op jit(solution)/shard_map/pallas_call | solution.py:293
  29.1 0.9 %copy-done.2 = bf16[3,512,256]{2,1,0:T(8,128)(2,1)} copy-done((bf16[3,512,256]{2,1,0:T(8,128)(2,1)}, bf16[3,512,256]{2,1,0:T(8,128)(2,1)S(1)}, u32[]{:S(2)}) %copy-start.2) | copy-done | bytes 786456
  30.0 5.5 %all-to-all-start = ((bf16[8,8,1536]{2,1,0:T(8,128)(2,1)}), bf16[8,8,1536]{2,1,0:T(8,128)(2,1)S(1)}, u32[]{:S(2)}, u32[]{:S(2)}) async-start(bf16[8,8,1536]{2,1,0:T(8,128)(2,1)} %get-tuple-element.29), calls=%async_computation | async-start | bytes 393216 | tf_op jit(solution)/shard_map/all_to_all | solution.py:363
  35.6 0.0 collective-permute-done.8
  35.6 2.8 %collective-permute-start.10 = (bf16[32,1536]{1,0:T(8,128)(2,1)S(1)}, bf16[32,1536]{1,0:T(8,128)(2,1)S(1)}, u32[]{:S(2)}, u32[]{:S(2)}) collective-permute-start(bf16[32,1536]{1,0:T(8,128)(2,1)S(1)} %pad_maximum_fusion.refs_0_), channel_id=1, source_target_pairs={{0,32},{8,40},{16,48},{24,56},{32,0},{40,8},{48,16},{56,24},{64,96... | collective-permute-start | bytes 294920 | tf_op jit(solution)/shard_map/ppermute | solution.py:312
  38.4 0.9 %collective-permute-start.11 = (bf16[32,1536]{1,0:T(8,128)(2,1)S(1)}, bf16[32,1536]{1,0:T(8,128)(2,1)S(1)}, u32[]{:S(2)}, u32[]{:S(2)}) collective-permute-start(bf16[32,1536]{1,0:T(8,128)(2,1)S(1)} %pad_maximum_fusion.refs_0_), channel_id=1, source_target_pairs={{0,48},{8,56},{16,0},{24,8},{32,16},{40,24},{48,32},{56,40},{64,11... | collective-permute-start | bytes 294920 | tf_op jit(solution)/shard_map/ppermute | solution.py:312
  39.3 0.6 collective-permute-start.9
  39.9 0.8 %collective-permute-done.10.refs_2_ = bf16[32,1536]{1,0:T(8,128)(2,1)S(1)} collective-permute-done((bf16[32,1536]{1,0:T(8,128)(2,1)S(1)}, bf16[32,1536]{1,0:T(8,128)(2,1)S(1)}, u32[]{:S(2)}, u32[]{:S(2)}) %collective-permute-start.10) | collective-permute-done | bytes 98336 | tf_op jit(solution)/shard_map/ppermute | solution.py:312
  40.6 2.3 %collective-permute-done.11.refs_3_ = bf16[32,1536]{1,0:T(8,128)(2,1)S(1)} collective-permute-done((bf16[32,1536]{1,0:T(8,128)(2,1)S(1)}, bf16[32,1536]{1,0:T(8,128)(2,1)S(1)}, u32[]{:S(2)}, u32[]{:S(2)}) %collective-permute-start.11) | collective-permute-done | bytes 98336 | tf_op jit(solution)/shard_map/ppermute | solution.py:312
  43.0 1.3 %collective-permute-done.9.refs_1_ = bf16[32,1536]{1,0:T(8,128)(2,1)S(1)} collective-permute-done((bf16[32,1536]{1,0:T(8,128)(2,1)S(1)}, bf16[32,1536]{1,0:T(8,128)(2,1)S(1)}, u32[]{:S(2)}, u32[]{:S(2)}) %collective-permute-start.9) | collective-permute-done | bytes 98336 | tf_op jit(solution)/shard_map/ppermute | solution.py:312
  44.3 0.0 all-to-all-done.refs_9_
  44.3 0.0 copy-start.3
  44.3 1.1 %copy-done.3 = bf16[3,512,256]{2,1,0:T(8,128)(2,1)S(1)} copy-done((bf16[3,512,256]{2,1,0:T(8,128)(2,1)S(1)}, bf16[3,512,256]{2,1,0:T(8,128)(2,1)}, u32[]{:S(2)}) %copy-start.3) | copy-done | bytes 786456
  45.4 4.0 %shard_map.101 = (bf16[8,400,128]{2,1,0:T(8,128)(2,1)S(1)}, bf16[8,400,128]{2,1,0:T(8,128)(2,1)S(1)}) custom-call(bf16[72,1536]{1,0:T(8,128)(2,1)S(1)} %dynamic_update_slice.7.refs_0_, bf16[72,1536]{1,0:T(8,128)(2,1)S(1)} %collective-permute-done.2.refs_1_, bf16[72,1536]{1,0:T(8,128)(2,1)S(1)} %collective-permute-done.1.refs_2_, ...), custom_call_target="tpu_custom_call" | custom-call | tf_op jit(solution)/shard_map/pallas_call | solution.py:293
  49.5 2.5 %collective-permute-start.12 = (bf16[8,400,128]{2,1,0:T(8,128)(2,1)S(1)}, bf16[8,400,128]{2,1,0:T(8,128)(2,1)S(1)}, u32[]{:S(2)}, u32[]{:S(2)}) collective-permute-start(bf16[8,400,128]{2,1,0:T(8,128)(2,1)S(1)} %get-tuple-element.34), channel_id=1, source_target_pairs={{0,8},{8,0},{16,24},{24,16},{32,40},{40,32},{48,56},{56,48},{64,72... | collective-permute-start | bytes 2457608 | tf_op jit(solution)/shard_map/ppermute | solution.py:371
  52.0 2.0 %collective-permute-done.12 = bf16[8,400,128]{2,1,0:T(8,128)(2,1)S(1)} collective-permute-done((bf16[8,400,128]{2,1,0:T(8,128)(2,1)S(1)}, bf16[8,400,128]{2,1,0:T(8,128)(2,1)S(1)}, u32[]{:S(2)}, u32[]{:S(2)}) %collective-permute-start.12) | collective-permute-done | bytes 819232 | tf_op jit(solution)/shard_map/ppermute | solution.py:371
  54.0 0.2 add_convert_fusion
  54.2 15.7 %all_to_all.10.r_ref = bf16[8,400,128]{2,1,0:T(8,128)(2,1)S(1)} all-to-all(bf16[8,400,128]{2,1,0:T(8,128)(2,1)S(1)} %add_convert_fusion), channel_id=1, replica_groups={{0,16,32,48,64,80,96,112},{8,24,40,56,72,88,104,120},{1,17,33,49,65,81,..., dimensions={0} | all-to-all | bytes 1638400 | tf_op jit(solution)/shard_map/all_to_all | solution.py:373
  70.0 0.0 copy-done.6
  70.0 0.0 copy-done.7
  70.0 1.5 %shard_map.102 = (f32[1,1536]{1,0:T(1,128)}, f32[3,192,96]{2,1,0:T(8,128)}, f32[192,96]{1,0:T(8,128)}) custom-call(bf16[8,400,128]{2,1,0:T(8,128)(2,1)S(1)} %all_to_all.10.r_ref, bf16[1,1536]{1,0:T(2,128)(2,1)S(1)} %copy-done.7, f32[12,128]{1,0:T(8,128)S(1)} %bitcast.2), custom_call_target="tpu_custom_call" | custom-call | tf_op jit(solution)/shard_map/pallas_call | solution.py:293
  (11 shorter events, 0.1 us)
Async XLA Ops:
  0.6 3.5 %collective-permute-start = (bf16[1,1536]{1,0:T(2,128)(2,1)}, bf16[1,1536]{1,0:T(2,128)(2,1)S(1)}, u32[]{:S(2)}, u32[]{:S(2)}) collective-permute-start(bf16[1,1536]{1,0:T(2,128)(2,1)} %text_ref.1), channel_id=1, source_target_pairs={{0,8},{8,0},{16,24},{24,16},{32,40},{40,32},{48,56},{56,48},{64,72... | collective-permute-start | bytes 9224 | tf_op jit(solution)/shard_map/ppermute | solution.py:312
  2.1 0.9 %copy-start.4 = (bf16[8,12288]{1,0:T(8,128)(2,1)S(1)}, bf16[8,12288]{1,0:T(8,128)(2,1)}, u32[]{:S(2)}) copy-start(bf16[8,12288]{1,0:T(8,128)(2,1)} %tok_ref.1) | copy-start | bytes 589828
  4.3 9.4 %collective-permute-start.2 = (bf16[72,1536]{1,0:T(8,128)(2,1)S(1)}, bf16[72,1536]{1,0:T(8,128)(2,1)S(1)}, u32[]{:S(2)}, u32[]{:S(2)}) collective-permute-start(bf16[72,1536]{1,0:T(8,128)(2,1)S(1)} %dynamic_update_slice.7.refs_0_), channel_id=1, source_target_pairs={{0,1},{1,0},{2,3},{3,2},{4,5},{5,4},{6,7},{7,6},{8,9},{9,8},{10,11... | collective-permute-start | bytes 663560 | tf_op jit(solution)/shard_map/ppermute | solution.py:305
  7.3 9.4 %collective-permute-start.4 = (bf16[72,1536]{1,0:T(8,128)(2,1)S(1)}, bf16[72,1536]{1,0:T(8,128)(2,1)S(1)}, u32[]{:S(2)}, u32[]{:S(2)}) collective-permute-start(bf16[72,1536]{1,0:T(8,128)(2,1)S(1)} %dynamic_update_slice.7.refs_0_), channel_id=1, source_target_pairs={{0,4},{1,5},{2,6},{3,7},{4,0},{5,1},{6,2},{7,3},{8,12},{9,13},{10,... | collective-permute-start | bytes 663560 | tf_op jit(solution)/shard_map/ppermute | solution.py:305
  10.9 10.6 %collective-permute-start.1 = (bf16[72,1536]{1,0:T(8,128)(2,1)S(1)}, bf16[72,1536]{1,0:T(8,128)(2,1)S(1)}, u32[]{:S(2)}, u32[]{:S(2)}) collective-permute-start(bf16[72,1536]{1,0:T(8,128)(2,1)S(1)} %dynamic_update_slice.7.refs_0_), channel_id=1, source_target_pairs={{0,2},{1,3},{2,4},{3,5},{4,6},{5,7},{6,0},{7,1},{8,10},{9,11},{10,... | collective-permute-start | bytes 663560 | tf_op jit(solution)/shard_map/ppermute | solution.py:305
  11.7 10.0 %collective-permute-start.3 = (bf16[72,1536]{1,0:T(8,128)(2,1)S(1)}, bf16[72,1536]{1,0:T(8,128)(2,1)S(1)}, u32[]{:S(2)}, u32[]{:S(2)}) collective-permute-start(bf16[72,1536]{1,0:T(8,128)(2,1)S(1)} %dynamic_update_slice.7.refs_0_), channel_id=1, source_target_pairs={{0,6},{1,7},{2,0},{3,1},{4,2},{5,3},{6,4},{7,5},{8,14},{9,15},{10,... | collective-permute-start | bytes 663560 | tf_op jit(solution)/shard_map/ppermute | solution.py:305
  13.6 12.7 %collective-permute-start.5 = (bf16[72,1536]{1,0:T(8,128)(2,1)S(1)}, bf16[72,1536]{1,0:T(8,128)(2,1)S(1)}, u32[]{:S(2)}, u32[]{:S(2)}) collective-permute-start(bf16[72,1536]{1,0:T(8,128)(2,1)S(1)} %collective-permute-done.2.refs_1_), channel_id=1, source_target_pairs={{0,2},{1,3},{2,4},{3,5},{4,6},{5,7},{6,0},{7,1},{8,10},{9,11},{10,... | collective-permute-start | bytes 663560 | tf_op jit(solution)/shard_map/ppermute | solution.py:305
  14.6 11.8 %collective-permute-start.6 = (bf16[72,1536]{1,0:T(8,128)(2,1)S(1)}, bf16[72,1536]{1,0:T(8,128)(2,1)S(1)}, u32[]{:S(2)}, u32[]{:S(2)}) collective-permute-start(bf16[72,1536]{1,0:T(8,128)(2,1)S(1)} %collective-permute-done.2.refs_1_), channel_id=1, source_target_pairs={{0,6},{1,7},{2,0},{3,1},{4,2},{5,3},{6,4},{7,5},{8,14},{9,15},{10,... | collective-permute-start | bytes 663560 | tf_op jit(solution)/shard_map/ppermute | solution.py:305
  16.8 9.8 %collective-permute-start.7 = (bf16[72,1536]{1,0:T(8,128)(2,1)S(1)}, bf16[72,1536]{1,0:T(8,128)(2,1)S(1)}, u32[]{:S(2)}, u32[]{:S(2)}) collective-permute-start(bf16[72,1536]{1,0:T(8,128)(2,1)S(1)} %collective-permute-done.4.refs_4_), channel_id=1, source_target_pairs={{0,1},{1,0},{2,3},{3,2},{4,5},{5,4},{6,7},{7,6},{8,9},{9,8},{10,11... | collective-permute-start | bytes 663560 | tf_op jit(solution)/shard_map/ppermute | solution.py:305
  21.7 1.5 %copy-start.1 = (bf16[3,192,1536]{2,1,0:T(8,128)(2,1)S(1)}, bf16[3,192,1536]{2,1,0:T(8,128)(2,1)}, u32[]{:S(2)}) copy-start(bf16[3,192,1536]{2,1,0:T(8,128)(2,1)} %refs_5_.2) | copy-start | bytes 5308420
  23.2 0.7 copy-start.5
  25.0 2.2 %copy-start = (bf16[192,1536]{1,0:T(8,128)(2,1)S(1)}, bf16[192,1536]{1,0:T(8,128)(2,1)}, u32[]{:S(2)}) copy-start(bf16[192,1536]{1,0:T(8,128)(2,1)} %refs_13_.1) | copy-start | bytes 1769476
  26.6 8.9 %collective-permute-start.8 = (bf16[16,1536]{1,0:T(8,128)(2,1)S(1)}, bf16[16,1536]{1,0:T(8,128)(2,1)S(1)}, u32[]{:S(2)}, u32[]{:S(2)}) collective-permute-start(bf16[16,1536]{1,0:T(8,128)(2,1)S(1)} %shard_map.98), channel_id=1, source_target_pairs={{0,64},{8,72},{16,80},{24,88},{32,96},{40,104},{48,112},{56,120},{... | collective-permute-start | bytes 147464 | tf_op jit(solution)/shard_map/ppermute | solution.py:312
  29.1 0.9 %copy-start.2 = (bf16[3,512,256]{2,1,0:T(8,128)(2,1)}, bf16[3,512,256]{2,1,0:T(8,128)(2,1)S(1)}, u32[]{:S(2)}) copy-start(bf16[3,512,256]{2,1,0:T(8,128)(2,1)S(1)} %get-tuple-element.30.refs_10_) | copy-start | bytes 2359300
  30.0 14.3 %all-to-all-start = ((bf16[8,8,1536]{2,1,0:T(8,128)(2,1)}), bf16[8,8,1536]{2,1,0:T(8,128)(2,1)S(1)}, u32[]{:S(2)}, u32[]{:S(2)}) async-start(bf16[8,8,1536]{2,1,0:T(8,128)(2,1)} %get-tuple-element.29), calls=%async_computation | async-start | bytes 393216 | tf_op jit(solution)/shard_map/all_to_all | solution.py:363
  35.6 5.1 %collective-permute-start.10 = (bf16[32,1536]{1,0:T(8,128)(2,1)S(1)}, bf16[32,1536]{1,0:T(8,128)(2,1)S(1)}, u32[]{:S(2)}, u32[]{:S(2)}) collective-permute-start(bf16[32,1536]{1,0:T(8,128)(2,1)S(1)} %pad_maximum_fusion.refs_0_), channel_id=1, source_target_pairs={{0,32},{8,40},{16,48},{24,56},{32,0},{40,8},{48,16},{56,24},{64,96... | collective-permute-start | bytes 294920 | tf_op jit(solution)/shard_map/ppermute | solution.py:312
  38.4 4.5 %collective-permute-start.11 = (bf16[32,1536]{1,0:T(8,128)(2,1)S(1)}, bf16[32,1536]{1,0:T(8,128)(2,1)S(1)}, u32[]{:S(2)}, u32[]{:S(2)}) collective-permute-start(bf16[32,1536]{1,0:T(8,128)(2,1)S(1)} %pad_maximum_fusion.refs_0_), channel_id=1, source_target_pairs={{0,48},{8,56},{16,0},{24,8},{32,16},{40,24},{48,32},{56,40},{64,11... | collective-permute-start | bytes 294920 | tf_op jit(solution)/shard_map/ppermute | solution.py:312
  39.3 5.0 %collective-permute-start.9 = (bf16[32,1536]{1,0:T(8,128)(2,1)S(1)}, bf16[32,1536]{1,0:T(8,128)(2,1)S(1)}, u32[]{:S(2)}, u32[]{:S(2)}) collective-permute-start(bf16[32,1536]{1,0:T(8,128)(2,1)S(1)} %pad_maximum_fusion.refs_0_), channel_id=1, source_target_pairs={{0,16},{8,24},{16,32},{24,40},{32,48},{40,56},{48,0},{56,8},{64,80... | collective-permute-start | bytes 294920 | tf_op jit(solution)/shard_map/ppermute | solution.py:312
  44.3 1.1 %copy-start.3 = (bf16[3,512,256]{2,1,0:T(8,128)(2,1)S(1)}, bf16[3,512,256]{2,1,0:T(8,128)(2,1)}, u32[]{:S(2)}) copy-start(bf16[3,512,256]{2,1,0:T(8,128)(2,1)} %copy-done.2) | copy-start | bytes 2359300
  49.5 4.5 %collective-permute-start.12 = (bf16[8,400,128]{2,1,0:T(8,128)(2,1)S(1)}, bf16[8,400,128]{2,1,0:T(8,128)(2,1)S(1)}, u32[]{:S(2)}, u32[]{:S(2)}) collective-permute-start(bf16[8,400,128]{2,1,0:T(8,128)(2,1)S(1)} %get-tuple-element.34), channel_id=1, source_target_pairs={{0,8},{8,0},{16,24},{24,16},{32,40},{40,32},{48,56},{56,48},{64,72... | collective-permute-start | bytes 2457608 | tf_op jit(solution)/shard_map/ppermute | solution.py:371
  54.0 16.0 %copy-start.6 = (f32[1536]{0:T(1024)S(1)}, f32[1536]{0:T(1024)}, u32[]{:S(2)}) copy-start(f32[1536]{0:T(1024)} %param.8) | copy-start | bytes 18436
  54.0 16.0 %copy-start.7 = (bf16[1,1536]{1,0:T(2,128)(2,1)S(1)}, bf16[1,1536]{1,0:T(2,128)(2,1)}, u32[]{:S(2)}) copy-start(bf16[1,1536]{1,0:T(2,128)(2,1)} %text_ref.1) | copy-start | bytes 9220

commit v8 on v7

--- a/solution.py
+++ b/solution.py
@@ -106,7 +106,7 @@
 
 def forward_kernel(*refs):
     shards, (early_ref, w_ref, wo_ref, sum_ref), refs = refs[:3], refs[3:7], refs[7:]
-    part_ref, qkv_ref, att_ref, wide_ref = refs
+    part_ref, *qkv_ref, att_ref, wide_ref = refs
     normed = jnp.concatenate([r[0:64, :] for r in shards], axis=0)
     for c in range(3):
         wide_ref[...] = dot(normed, w_ref[c], LAST)
@@ -115,19 +115,19 @@
                 [early_ref[c, b * 40:(b + 1) * 40, :].astype(F32)]
                 + [wide_ref[(s * 8 + b) * 8:(s * 8 + b) * 8 + 8, :] for s in range(3)], axis=0
             )
-            qkv_ref[c, b * 64:(b + 1) * 64, 0:WIDTH] = block.astype(BF16)
+            qkv_ref[c][b * 64:(b + 1) * 64, 0:WIDTH] = block.astype(BF16)
     lane = lanes((64, WIDTH))
     for b in range(IMG):
         rows = slice(b * 64, (b + 1) * 64)
-        q, k = qkv_ref[0, rows, 0:WIDTH], qkv_ref[1, rows, 0:WIDTH]
-        v = qkv_ref[2, rows, 0:WIDTH].astype(F32)
+        q, k = qkv_ref[0][rows, 0:WIDTH], qkv_ref[1][rows, 0:WIDTH]
+        v = qkv_ref[2][rows, 0:WIDTH].astype(F32)
         columns = []
         for h in range(2):
             inside = lane < DH if h == 0 else lane >= DH
             score = dot(k, jnp.where(inside, q, jnp.zeros_like(q)), LAST) * SCALE
             weights = jnp.exp(score)
             probs = (weights / jnp.sum(weights, axis=0, keepdims=True)).astype(BF16)
-            qkv_ref[h, rows, WIDTH:256] = probs
+            qkv_ref[h][rows, WIDTH:256] = probs
             columns.append(jnp.sum(probs.astype(F32), axis=1, keepdims=True))
         attended = jnp.sum(jnp.where(lane < DH, columns[0], columns[1]) * v, axis=0, keepdims=True)
         att_ref[b:b + 1, :] = attended
@@ -144,8 +144,8 @@
 
 def backward_kernel(*refs):
     shards, t_ref, refs = refs[:MP], refs[MP], refs[MP + 1:]
-    part_ref, qkv_ref, att_ref, scalar_ref, wo_ref = refs[:5]
-    keep_ref, give_ref, grad_ref, turn_ref, text_ref, both_ref = refs[5:]
+    part_ref, *qkv_ref, att_ref, scalar_ref, wo_ref = refs[:7]
+    keep_ref, give_ref, grad_ref, turn_ref, text_ref, both_ref = refs[7:]
     me = lax.axis_index("dp")
     slot = lax.axis_index("mp")
     core = lax.rem(me, 2)
@@ -195,13 +195,13 @@
     slim = lanes((64, 64))
     for b in range(IMG):
         rows = slice(b * 64, (b + 1) * 64)
-        q, k = qkv_ref[0, rows, 0:WIDTH], qkv_ref[1, rows, 0:WIDTH]
-        product = qkv_ref[2, rows, 0:WIDTH].astype(F32) * wide_attend[b:b + 1, :]
+        q, k = qkv_ref[0][rows, 0:WIDTH], qkv_ref[1][rows, 0:WIDTH]
+        product = qkv_ref[2][rows, 0:WIDTH].astype(F32) * wide_attend[b:b + 1, :]
         query_grad, key_grad, factor = [], [], jnp.zeros((64, 64), F32)
         for h in range(2):
             inside = lane < DH if h == 0 else lane >= DH
             prob_grad = jnp.sum(jnp.where(inside, product, 0.0), axis=1, keepdims=True)
-            probs = qkv_ref[h, rows, WIDTH:256].astype(F32)
+            probs = qkv_ref[h][rows, WIDTH:256].astype(F32)
             mean = jnp.sum(probs * prob_grad, axis=0, keepdims=True)
             score_grad = (probs * (prob_grad - mean) * SCALE).astype(BF16)
             query_grad.append(dot(score_grad, k, FIRST))
@@ -350,10 +350,11 @@
     )
     texts, = call(functools.partial(text_kernel, 7, 1), [((16, D), BF16)], [], shards[7], kept)
     texts = [texts, over_dp(texts, 1, 0, 0)]
-    part, qkv, attended = call(
+    part, *qkv, attended = call(
         forward_kernel,
         [
-            ((MP, IMG, D), BF16), ((3, 512, 256), BF16), ((IMG, WIDTH), F32),
+            ((MP, IMG, D), BF16), ((512, 256), BF16), ((512, 256), BF16),
+            ((512, WIDTH), BF16), ((IMG, WIDTH), F32),
         ],
         [((192, WIDTH), F32)],
         *shards[5:], early, scaled, out_weight, token_sum,
@@ -366,7 +367,7 @@
         backward_kernel,
         [((8, ROWS, 128), BF16)] * 2,
         [((512, 512), F32), ((256, 128), F32), ((256, 128), F32), ((2, 8, ROWS, 128), BF16)],
-        *shards, texts, parts, qkv, attended, scalars, out_weight,
+        *shards, texts, parts, *qkv, attended, scalars, out_weight,
     )
     other = lax.ppermute(give, "dp", [(i, i ^ 1) for i in range(DP)])
     send = (keep.astype(F32) + other.astype(F32)).astype(BF16)

time: 71.9 us -> 70.8 us (0.985)
  local copies, waits for them, and re-layouts: 6.01 us -> 4.94 us
    unnamed x16, local copies, waits for them, and re-layouts: 5.13 us -> 4.06 us
where the time goes in v8:
time: 70.8 us; the launch traced here: 70.3 us
  starting transfers between devices  29.7 us (42%)
  blocking collectives  15.7 us (22%)
  Pallas kernels  9.05 us (13%)
  waiting for transfers between devices  8.6 us (12%)
  local copies, waits for them, and re-layouts  4.94 us (7%)
  between operations  2.06 us (3%)
    all_to_all x1, blocking collectives, body(): lax.all_to_all(send, 'dp', 0, 0, axis_index_groups=[list(range(c, DP, 2))...  15.7 us
    ppermute x7, starting transfers between devices, over_mp(): return lax.ppermute(block, 'mp', route)  15.4 us
    pallas_call x9, Pallas kernels, call(): pl.pallas_call(kernel, out_shape=[jax.ShapeDtypeStruct(*o) for o in outs]...  9.05 us
    ppermute x5, starting transfers between devices, over_dp(): return lax.ppermute(block, 'dp', route)  6.27 us
    all_to_all x1, starting transfers between devices, body(): parts = lax.all_to_all(part, 'mp', 0, 0)  5.53 us
    ppermute x5, waiting for transfers between devices, over_dp(): return lax.ppermute(block, 'dp', route)  4.39 us
    unnamed x16, local copies, waits for them, and re-layouts  4.06 us
    ppermute x1, starting transfers between devices, body(): other = lax.ppermute(give, 'dp', [(i, i ^ 1) for i in range(DP)])  2.53 us
  transfers between devices with their start and end apart: 14, of which 8 were waited for; matrix products, arithmetic and copies ran while one was open for 1% of the time, Pallas kernels for 5%

profile of v8, /device:TPU:1, one launch (start us, length us, event | category | flops | bytes accessed | tf_op | source)
XLA Modules:
  0.0 70.3 jit_solution(1770417518808708231)
XLA Ops:
  0.6 1.5 %collective-permute-start = (bf16[1,1536]{1,0:T(2,128)(2,1)}, bf16[1,1536]{1,0:T(2,128)(2,1)S(1)}, u32[]{:S(2)}, u32[]{:S(2)}) collective-permute-start(bf16[1,1536]{1,0:T(2,128)(2,1)} %text_ref.1), channel_id=1, source_target_pairs={{0,8},{8,0},{16,24},{24,16},{32,40},{40,32},{48,56},{56,48},{64,72... | collective-permute-start | bytes 9224 | tf_op jit(solution)/shard_map/ppermute | solution.py:312
  2.1 0.9 %copy-done.4 = bf16[8,12288]{1,0:T(8,128)(2,1)S(1)} copy-done((bf16[8,12288]{1,0:T(8,128)(2,1)S(1)}, bf16[8,12288]{1,0:T(8,128)(2,1)}, u32[]{:S(2)}) %copy-start.4) | copy-done | bytes 196632
  3.1 0.3 shard_map.94
  3.4 0.8 %dynamic_update_slice.6 = bf16[72,1536]{1,0:T(8,128)(2,1)S(1)} dynamic-update-slice(bf16[72,1536]{1,0:T(8,128)(2,1)S(1)} %get-tuple-element.21, bf16[1,1536]{1,0:T(2,128)(2,1)} %text_ref.1, s32[]{:T(128)} %constant.0.clone.1, s32[]{:T(128)} %constant.1.clone.1) | dynamic-update-slice | bytes 6148 | tf_op jit(solution)/shard_map/dynamic_update_slice | solution.py:333
  4.2 0.0 collective-permute-done
  4.2 0.1 dynamic_update_slice.7.refs_0_
  4.3 3.1 %collective-permute-start.2 = (bf16[72,1536]{1,0:T(8,128)(2,1)S(1)}, bf16[72,1536]{1,0:T(8,128)(2,1)S(1)}, u32[]{:S(2)}, u32[]{:S(2)}) collective-permute-start(bf16[72,1536]{1,0:T(8,128)(2,1)S(1)} %dynamic_update_slice.7.refs_0_), channel_id=1, source_target_pairs={{0,1},{1,0},{2,3},{3,2},{4,5},{5,4},{6,7},{7,6},{8,9},{9,8},{10,11... | collective-permute-start | bytes 663560 | tf_op jit(solution)/shard_map/ppermute | solution.py:305
  7.3 3.6 %collective-permute-start.4 = (bf16[72,1536]{1,0:T(8,128)(2,1)S(1)}, bf16[72,1536]{1,0:T(8,128)(2,1)S(1)}, u32[]{:S(2)}, u32[]{:S(2)}) collective-permute-start(bf16[72,1536]{1,0:T(8,128)(2,1)S(1)} %dynamic_update_slice.7.refs_0_), channel_id=1, source_target_pairs={{0,4},{1,5},{2,6},{3,7},{4,0},{5,1},{6,2},{7,3},{8,12},{9,13},{10,... | collective-permute-start | bytes 663560 | tf_op jit(solution)/shard_map/ppermute | solution.py:305
  10.9 0.7 %collective-permute-start.1 = (bf16[72,1536]{1,0:T(8,128)(2,1)S(1)}, bf16[72,1536]{1,0:T(8,128)(2,1)S(1)}, u32[]{:S(2)}, u32[]{:S(2)}) collective-permute-start(bf16[72,1536]{1,0:T(8,128)(2,1)S(1)} %dynamic_update_slice.7.refs_0_), channel_id=1, source_target_pairs={{0,2},{1,3},{2,4},{3,5},{4,6},{5,7},{6,0},{7,1},{8,10},{9,11},{10,... | collective-permute-start | bytes 663560 | tf_op jit(solution)/shard_map/ppermute | solution.py:305
  11.7 1.9 %collective-permute-start.3 = (bf16[72,1536]{1,0:T(8,128)(2,1)S(1)}, bf16[72,1536]{1,0:T(8,128)(2,1)S(1)}, u32[]{:S(2)}, u32[]{:S(2)}) collective-permute-start(bf16[72,1536]{1,0:T(8,128)(2,1)S(1)} %dynamic_update_slice.7.refs_0_), channel_id=1, source_target_pairs={{0,6},{1,7},{2,0},{3,1},{4,2},{5,3},{6,4},{7,5},{8,14},{9,15},{10,... | collective-permute-start | bytes 663560 | tf_op jit(solution)/shard_map/ppermute | solution.py:305
  13.6 0.0 collective-permute-done.2.refs_1_
  13.6 1.0 %collective-permute-start.5 = (bf16[72,1536]{1,0:T(8,128)(2,1)S(1)}, bf16[72,1536]{1,0:T(8,128)(2,1)S(1)}, u32[]{:S(2)}, u32[]{:S(2)}) collective-permute-start(bf16[72,1536]{1,0:T(8,128)(2,1)S(1)} %collective-permute-done.2.refs_1_), channel_id=1, source_target_pairs={{0,2},{1,3},{2,4},{3,5},{4,6},{5,7},{6,0},{7,1},{8,10},{9,11},{10,... | collective-permute-start | bytes 663560 | tf_op jit(solution)/shard_map/ppermute | solution.py:305
  14.6 2.1 %collective-permute-start.6 = (bf16[72,1536]{1,0:T(8,128)(2,1)S(1)}, bf16[72,1536]{1,0:T(8,128)(2,1)S(1)}, u32[]{:S(2)}, u32[]{:S(2)}) collective-permute-start(bf16[72,1536]{1,0:T(8,128)(2,1)S(1)} %collective-permute-done.2.refs_1_), channel_id=1, source_target_pairs={{0,6},{1,7},{2,0},{3,1},{4,2},{5,3},{6,4},{7,5},{8,14},{9,15},{10,... | collective-permute-start | bytes 663560 | tf_op jit(solution)/shard_map/ppermute | solution.py:305
  16.7 0.0 collective-permute-done.4.refs_4_
  16.8 2.9 %collective-permute-start.7 = (bf16[72,1536]{1,0:T(8,128)(2,1)S(1)}, bf16[72,1536]{1,0:T(8,128)(2,1)S(1)}, u32[]{:S(2)}, u32[]{:S(2)}) collective-permute-start(bf16[72,1536]{1,0:T(8,128)(2,1)S(1)} %collective-permute-done.4.refs_4_), channel_id=1, source_target_pairs={{0,1},{1,0},{2,3},{3,2},{4,5},{5,4},{6,7},{7,6},{8,9},{9,8},{10,11... | collective-permute-start | bytes 663560 | tf_op jit(solution)/shard_map/ppermute | solution.py:305
  21.0 0.6 collective-permute-done.1.refs_2_
  21.6 0.1 collective-permute-done.3.refs_3_
  21.7 1.5 %copy-done.1 = bf16[3,192,1536]{2,1,0:T(8,128)(2,1)S(1)} copy-done((bf16[3,192,1536]{2,1,0:T(8,128)(2,1)S(1)}, bf16[3,192,1536]{2,1,0:T(8,128)(2,1)}, u32[]{:S(2)}) %copy-start.1) | copy-done | bytes 1769496
  23.2 0.7 copy-done.5
  23.9 1.0 %shard_map.96 = (bf16[3,320,192]{2,1,0:T(8,128)(2,1)S(1)}, bf16[3,192,1536]{2,1,0:T(8,128)(2,1)S(1)}) custom-call(bf16[72,1536]{1,0:T(8,128)(2,1)S(1)} %dynamic_update_slice.7.refs_0_, bf16[72,1536]{1,0:T(8,128)(2,1)S(1)} %collective-permute-done.2.refs_1_, bf16[72,1536]{1,0:T(8,128)(2,1)S(1)} %collective-permute-done.1.refs_2_, ...), custom_call_target="tpu_custom_call" | custom-call | tf_op jit(solution)/shard_map/pallas_call | solution.py:293
  25.0 0.0 copy-start
  25.0 1.3 %collective-permute-done.5.refs_5_.refs_0_ = bf16[72,1536]{1,0:T(8,128)(2,1)S(1)} collective-permute-done((bf16[72,1536]{1,0:T(8,128)(2,1)S(1)}, bf16[72,1536]{1,0:T(8,128)(2,1)S(1)}, u32[]{:S(2)}, u32[]{:S(2)}) %collective-permute-start.5) | collective-permute-done | bytes 221216 | tf_op jit(solution)/shard_map/ppermute | solution.py:305
  26.3 0.1 collective-permute-done.6.refs_6_.refs_1_
  26.5 0.1 shard_map.97.refs_1_
  26.6 0.0 collective-permute-done.7.refs_0_.refs_2_.refs_7_
  26.6 0.5 collective-permute-start.8
  27.1 0.0 copy-done
  27.1 2.0 %shard_map.100 = (bf16[8,8,1536]{2,1,0:T(8,128)(2,1)}, bf16[512,256]{1,0:T(8,128)(2,1)S(1)}, bf16[512,256]{1,0:T(8,128)(2,1)S(1)}, bf16[512,192]{1,0:T(8,128)(2,1)S(1)}, f32[8,192]{1,0:T(8,128)S(1)}) custom-call(bf16[72,1536]{1,0:T(8,128)(2,1)S(1)} %collective-permute-done.5.refs_5_.refs_0_, bf16[72,1536]{1,0:T(8,128)(2,1)S(1)} %collective-permute-done.6.refs_6_.refs_1_, ...), custom_call_target="tpu_custom_call" | custom-call | tf_op jit(solution)/shard_map/pallas_call | solution.py:293
  29.1 5.5 %all-to-all-start = ((bf16[8,8,1536]{2,1,0:T(8,128)(2,1)}), bf16[8,8,1536]{2,1,0:T(8,128)(2,1)S(1)}, u32[]{:S(2)}, u32[]{:S(2)}) async-start(bf16[8,8,1536]{2,1,0:T(8,128)(2,1)} %get-tuple-element.31), calls=%async_computation | async-start | bytes 393216 | tf_op jit(solution)/shard_map/all_to_all | solution.py:364
  34.7 0.0 collective-permute-done.8
  34.7 2.8 %collective-permute-start.10 = (bf16[32,1536]{1,0:T(8,128)(2,1)S(1)}, bf16[32,1536]{1,0:T(8,128)(2,1)S(1)}, u32[]{:S(2)}, u32[]{:S(2)}) collective-permute-start(bf16[32,1536]{1,0:T(8,128)(2,1)S(1)} %pad_maximum_fusion.refs_0_), channel_id=1, source_target_pairs={{0,32},{8,40},{16,48},{24,56},{32,0},{40,8},{48,16},{56,24},{64,96... | collective-permute-start | bytes 294920 | tf_op jit(solution)/shard_map/ppermute | solution.py:312
  37.5 0.9 %collective-permute-start.11 = (bf16[32,1536]{1,0:T(8,128)(2,1)S(1)}, bf16[32,1536]{1,0:T(8,128)(2,1)S(1)}, u32[]{:S(2)}, u32[]{:S(2)}) collective-permute-start(bf16[32,1536]{1,0:T(8,128)(2,1)S(1)} %pad_maximum_fusion.refs_0_), channel_id=1, source_target_pairs={{0,48},{8,56},{16,0},{24,8},{32,16},{40,24},{48,32},{56,40},{64,11... | collective-permute-start | bytes 294920 | tf_op jit(solution)/shard_map/ppermute | solution.py:312
  38.4 0.6 collective-permute-start.9
  39.0 0.8 %collective-permute-done.10.refs_2_ = bf16[32,1536]{1,0:T(8,128)(2,1)S(1)} collective-permute-done((bf16[32,1536]{1,0:T(8,128)(2,1)S(1)}, bf16[32,1536]{1,0:T(8,128)(2,1)S(1)}, u32[]{:S(2)}, u32[]{:S(2)}) %collective-permute-start.10) | collective-permute-done | bytes 98336 | tf_op jit(solution)/shard_map/ppermute | solution.py:312
  39.8 2.3 %collective-permute-done.11.refs_3_ = bf16[32,1536]{1,0:T(8,128)(2,1)S(1)} collective-permute-done((bf16[32,1536]{1,0:T(8,128)(2,1)S(1)}, bf16[32,1536]{1,0:T(8,128)(2,1)S(1)}, u32[]{:S(2)}, u32[]{:S(2)}) %collective-permute-start.11) | collective-permute-done | bytes 98336 | tf_op jit(solution)/shard_map/ppermute | solution.py:312
  42.1 0.0 copy-done.2
  42.1 1.3 %collective-permute-done.9.refs_1_ = bf16[32,1536]{1,0:T(8,128)(2,1)S(1)} collective-permute-done((bf16[32,1536]{1,0:T(8,128)(2,1)S(1)}, bf16[32,1536]{1,0:T(8,128)(2,1)S(1)}, u32[]{:S(2)}, u32[]{:S(2)}) %collective-permute-start.9) | collective-permute-done | bytes 98336 | tf_op jit(solution)/shard_map/ppermute | solution.py:312
  43.4 0.0 all-to-all-done.refs_9_
  43.4 0.0 copy-start.3
  43.4 0.9 %copy-done.3 = bf16[512,192]{1,0:T(8,128)(2,1)S(1)} copy-done((bf16[512,192]{1,0:T(8,128)(2,1)S(1)}, bf16[512,192]{1,0:T(8,128)(2,1)}, u32[]{:S(2)}) %copy-start.3) | copy-done | bytes 196632
  44.4 4.0 %shard_map.101 = (bf16[8,400,128]{2,1,0:T(8,128)(2,1)S(1)}, bf16[8,400,128]{2,1,0:T(8,128)(2,1)S(1)}) custom-call(bf16[72,1536]{1,0:T(8,128)(2,1)S(1)} %dynamic_update_slice.7.refs_0_, bf16[72,1536]{1,0:T(8,128)(2,1)S(1)} %collective-permute-done.2.refs_1_, bf16[72,1536]{1,0:T(8,128)(2,1)S(1)} %collective-permute-done.1.refs_2_, ...), custom_call_target="tpu_custom_call" | custom-call | tf_op jit(solution)/shard_map/pallas_call | solution.py:293
  48.4 2.5 %collective-permute-start.12 = (bf16[8,400,128]{2,1,0:T(8,128)(2,1)S(1)}, bf16[8,400,128]{2,1,0:T(8,128)(2,1)S(1)}, u32[]{:S(2)}, u32[]{:S(2)}) collective-permute-start(bf16[8,400,128]{2,1,0:T(8,128)(2,1)S(1)} %get-tuple-element.38), channel_id=1, source_target_pairs={{0,8},{8,0},{16,24},{24,16},{32,40},{40,32},{48,56},{56,48},{64,72... | collective-permute-start | bytes 2457608 | tf_op jit(solution)/shard_map/ppermute | solution.py:372
  50.9 2.0 %collective-permute-done.12 = bf16[8,400,128]{2,1,0:T(8,128)(2,1)S(1)} collective-permute-done((bf16[8,400,128]{2,1,0:T(8,128)(2,1)S(1)}, bf16[8,400,128]{2,1,0:T(8,128)(2,1)S(1)}, u32[]{:S(2)}, u32[]{:S(2)}) %collective-permute-start.12) | collective-permute-done | bytes 819232 | tf_op jit(solution)/shard_map/ppermute | solution.py:372
  52.9 0.2 add_convert_fusion
  53.1 15.7 %all_to_all.10.r_ref = bf16[8,400,128]{2,1,0:T(8,128)(2,1)S(1)} all-to-all(bf16[8,400,128]{2,1,0:T(8,128)(2,1)S(1)} %add_convert_fusion), channel_id=1, replica_groups={{0,16,32,48,64,80,96,112},{8,24,40,56,72,88,104,120},{1,17,33,49,65,81,..., dimensions={0} | all-to-all | bytes 1638400 | tf_op jit(solution)/shard_map/all_to_all | solution.py:374
  68.9 0.0 copy-done.6
  68.9 0.0 copy-done.7
  68.9 1.5 %shard_map.102 = (f32[1,1536]{1,0:T(1,128)}, f32[3,192,96]{2,1,0:T(8,128)}, f32[192,96]{1,0:T(8,128)}) custom-call(bf16[8,400,128]{2,1,0:T(8,128)(2,1)S(1)} %all_to_all.10.r_ref, bf16[1,1536]{1,0:T(2,128)(2,1)S(1)} %copy-done.7, f32[12,128]{1,0:T(8,128)S(1)} %bitcast.2), custom_call_target="tpu_custom_call" | custom-call | tf_op jit(solution)/shard_map/pallas_call | solution.py:293
  (11 shorter events, 0.1 us)
Async XLA Ops:
  0.6 3.5 %collective-permute-start = (bf16[1,1536]{1,0:T(2,128)(2,1)}, bf16[1,1536]{1,0:T(2,128)(2,1)S(1)}, u32[]{:S(2)}, u32[]{:S(2)}) collective-permute-start(bf16[1,1536]{1,0:T(2,128)(2,1)} %text_ref.1), channel_id=1, source_target_pairs={{0,8},{8,0},{16,24},{24,16},{32,40},{40,32},{48,56},{56,48},{64,72... | collective-permute-start | bytes 9224 | tf_op jit(solution)/shard_map/ppermute | solution.py:312
  2.1 0.9 %copy-start.4 = (bf16[8,12288]{1,0:T(8,128)(2,1)S(1)}, bf16[8,12288]{1,0:T(8,128)(2,1)}, u32[]{:S(2)}) copy-start(bf16[8,12288]{1,0:T(8,128)(2,1)} %tok_ref.1) | copy-start | bytes 589828
  4.3 9.4 %collective-permute-start.2 = (bf16[72,1536]{1,0:T(8,128)(2,1)S(1)}, bf16[72,1536]{1,0:T(8,128)(2,1)S(1)}, u32[]{:S(2)}, u32[]{:S(2)}) collective-permute-start(bf16[72,1536]{1,0:T(8,128)(2,1)S(1)} %dynamic_update_slice.7.refs_0_), channel_id=1, source_target_pairs={{0,1},{1,0},{2,3},{3,2},{4,5},{5,4},{6,7},{7,6},{8,9},{9,8},{10,11... | collective-permute-start | bytes 663560 | tf_op jit(solution)/shard_map/ppermute | solution.py:305
  7.3 9.4 %collective-permute-start.4 = (bf16[72,1536]{1,0:T(8,128)(2,1)S(1)}, bf16[72,1536]{1,0:T(8,128)(2,1)S(1)}, u32[]{:S(2)}, u32[]{:S(2)}) collective-permute-start(bf16[72,1536]{1,0:T(8,128)(2,1)S(1)} %dynamic_update_slice.7.refs_0_), channel_id=1, source_target_pairs={{0,4},{1,5},{2,6},{3,7},{4,0},{5,1},{6,2},{7,3},{8,12},{9,13},{10,... | collective-permute-start | bytes 663560 | tf_op jit(solution)/shard_map/ppermute | solution.py:305
  10.9 10.6 %collective-permute-start.1 = (bf16[72,1536]{1,0:T(8,128)(2,1)S(1)}, bf16[72,1536]{1,0:T(8,128)(2,1)S(1)}, u32[]{:S(2)}, u32[]{:S(2)}) collective-permute-start(bf16[72,1536]{1,0:T(8,128)(2,1)S(1)} %dynamic_update_slice.7.refs_0_), channel_id=1, source_target_pairs={{0,2},{1,3},{2,4},{3,5},{4,6},{5,7},{6,0},{7,1},{8,10},{9,11},{10,... | collective-permute-start | bytes 663560 | tf_op jit(solution)/shard_map/ppermute | solution.py:305
  11.7 10.0 %collective-permute-start.3 = (bf16[72,1536]{1,0:T(8,128)(2,1)S(1)}, bf16[72,1536]{1,0:T(8,128)(2,1)S(1)}, u32[]{:S(2)}, u32[]{:S(2)}) collective-permute-start(bf16[72,1536]{1,0:T(8,128)(2,1)S(1)} %dynamic_update_slice.7.refs_0_), channel_id=1, source_target_pairs={{0,6},{1,7},{2,0},{3,1},{4,2},{5,3},{6,4},{7,5},{8,14},{9,15},{10,... | collective-permute-start | bytes 663560 | tf_op jit(solution)/shard_map/ppermute | solution.py:305
  13.6 12.7 %collective-permute-start.5 = (bf16[72,1536]{1,0:T(8,128)(2,1)S(1)}, bf16[72,1536]{1,0:T(8,128)(2,1)S(1)}, u32[]{:S(2)}, u32[]{:S(2)}) collective-permute-start(bf16[72,1536]{1,0:T(8,128)(2,1)S(1)} %collective-permute-done.2.refs_1_), channel_id=1, source_target_pairs={{0,2},{1,3},{2,4},{3,5},{4,6},{5,7},{6,0},{7,1},{8,10},{9,11},{10,... | collective-permute-start | bytes 663560 | tf_op jit(solution)/shard_map/ppermute | solution.py:305
  14.6 11.8 %collective-permute-start.6 = (bf16[72,1536]{1,0:T(8,128)(2,1)S(1)}, bf16[72,1536]{1,0:T(8,128)(2,1)S(1)}, u32[]{:S(2)}, u32[]{:S(2)}) collective-permute-start(bf16[72,1536]{1,0:T(8,128)(2,1)S(1)} %collective-permute-done.2.refs_1_), channel_id=1, source_target_pairs={{0,6},{1,7},{2,0},{3,1},{4,2},{5,3},{6,4},{7,5},{8,14},{9,15},{10,... | collective-permute-start | bytes 663560 | tf_op jit(solution)/shard_map/ppermute | solution.py:305
  16.8 9.8 %collective-permute-start.7 = (bf16[72,1536]{1,0:T(8,128)(2,1)S(1)}, bf16[72,1536]{1,0:T(8,128)(2,1)S(1)}, u32[]{:S(2)}, u32[]{:S(2)}) collective-permute-start(bf16[72,1536]{1,0:T(8,128)(2,1)S(1)} %collective-permute-done.4.refs_4_), channel_id=1, source_target_pairs={{0,1},{1,0},{2,3},{3,2},{4,5},{5,4},{6,7},{7,6},{8,9},{9,8},{10,11... | collective-permute-start | bytes 663560 | tf_op jit(solution)/shard_map/ppermute | solution.py:305
  21.7 1.5 %copy-start.1 = (bf16[3,192,1536]{2,1,0:T(8,128)(2,1)S(1)}, bf16[3,192,1536]{2,1,0:T(8,128)(2,1)}, u32[]{:S(2)}) copy-start(bf16[3,192,1536]{2,1,0:T(8,128)(2,1)} %refs_5_.2) | copy-start | bytes 5308420
  23.2 0.7 copy-start.5
  25.0 2.2 %copy-start = (bf16[192,1536]{1,0:T(8,128)(2,1)S(1)}, bf16[192,1536]{1,0:T(8,128)(2,1)}, u32[]{:S(2)}) copy-start(bf16[192,1536]{1,0:T(8,128)(2,1)} %refs_15_.1) | copy-start | bytes 1769476
  26.6 8.0 %collective-permute-start.8 = (bf16[16,1536]{1,0:T(8,128)(2,1)S(1)}, bf16[16,1536]{1,0:T(8,128)(2,1)S(1)}, u32[]{:S(2)}, u32[]{:S(2)}) collective-permute-start(bf16[16,1536]{1,0:T(8,128)(2,1)S(1)} %shard_map.98), channel_id=1, source_target_pairs={{0,64},{8,72},{16,80},{24,88},{32,96},{40,104},{48,112},{56,120},{... | collective-permute-start | bytes 147464 | tf_op jit(solution)/shard_map/ppermute | solution.py:312
  29.1 12.9 %copy-start.2 = (bf16[512,192]{1,0:T(8,128)(2,1)}, bf16[512,192]{1,0:T(8,128)(2,1)S(1)}, u32[]{:S(2)}) copy-start(bf16[512,192]{1,0:T(8,128)(2,1)S(1)} %get-tuple-element.34.refs_12_) | copy-start | bytes 589828
  29.1 14.3 %all-to-all-start = ((bf16[8,8,1536]{2,1,0:T(8,128)(2,1)}), bf16[8,8,1536]{2,1,0:T(8,128)(2,1)S(1)}, u32[]{:S(2)}, u32[]{:S(2)}) async-start(bf16[8,8,1536]{2,1,0:T(8,128)(2,1)} %get-tuple-element.31), calls=%async_computation | async-start | bytes 393216 | tf_op jit(solution)/shard_map/all_to_all | solution.py:364
  34.7 5.1 %collective-permute-start.10 = (bf16[32,1536]{1,0:T(8,128)(2,1)S(1)}, bf16[32,1536]{1,0:T(8,128)(2,1)S(1)}, u32[]{:S(2)}, u32[]{:S(2)}) collective-permute-start(bf16[32,1536]{1,0:T(8,128)(2,1)S(1)} %pad_maximum_fusion.refs_0_), channel_id=1, source_target_pairs={{0,32},{8,40},{16,48},{24,56},{32,0},{40,8},{48,16},{56,24},{64,96... | collective-permute-start | bytes 294920 | tf_op jit(solution)/shard_map/ppermute | solution.py:312
  37.5 4.5 %collective-permute-start.11 = (bf16[32,1536]{1,0:T(8,128)(2,1)S(1)}, bf16[32,1536]{1,0:T(8,128)(2,1)S(1)}, u32[]{:S(2)}, u32[]{:S(2)}) collective-permute-start(bf16[32,1536]{1,0:T(8,128)(2,1)S(1)} %pad_maximum_fusion.refs_0_), channel_id=1, source_target_pairs={{0,48},{8,56},{16,0},{24,8},{32,16},{40,24},{48,32},{56,40},{64,11... | collective-permute-start | bytes 294920 | tf_op jit(solution)/shard_map/ppermute | solution.py:312
  38.4 5.0 %collective-permute-start.9 = (bf16[32,1536]{1,0:T(8,128)(2,1)S(1)}, bf16[32,1536]{1,0:T(8,128)(2,1)S(1)}, u32[]{:S(2)}, u32[]{:S(2)}) collective-permute-start(bf16[32,1536]{1,0:T(8,128)(2,1)S(1)} %pad_maximum_fusion.refs_0_), channel_id=1, source_target_pairs={{0,16},{8,24},{16,32},{24,40},{32,48},{40,56},{48,0},{56,8},{64,80... | collective-permute-start | bytes 294920 | tf_op jit(solution)/shard_map/ppermute | solution.py:312
  43.4 1.0 %copy-start.3 = (bf16[512,192]{1,0:T(8,128)(2,1)S(1)}, bf16[512,192]{1,0:T(8,128)(2,1)}, u32[]{:S(2)}) copy-start(bf16[512,192]{1,0:T(8,128)(2,1)} %copy-done.2) | copy-start | bytes 589828
  48.4 4.5 %collective-permute-start.12 = (bf16[8,400,128]{2,1,0:T(8,128)(2,1)S(1)}, bf16[8,400,128]{2,1,0:T(8,128)(2,1)S(1)}, u32[]{:S(2)}, u32[]{:S(2)}) collective-permute-start(bf16[8,400,128]{2,1,0:T(8,128)(2,1)S(1)} %get-tuple-element.38), channel_id=1, source_target_pairs={{0,8},{8,0},{16,24},{24,16},{32,40},{40,32},{48,56},{56,48},{64,72... | collective-permute-start | bytes 2457608 | tf_op jit(solution)/shard_map/ppermute | solution.py:372
  52.9 16.0 %copy-start.6 = (f32[1536]{0:T(1024)S(1)}, f32[1536]{0:T(1024)}, u32[]{:S(2)}) copy-start(f32[1536]{0:T(1024)} %param.8) | copy-start | bytes 18436
  52.9 16.0 %copy-start.7 = (bf16[1,1536]{1,0:T(2,128)(2,1)S(1)}, bf16[1,1536]{1,0:T(2,128)(2,1)}, u32[]{:S(2)}) copy-start(bf16[1,1536]{1,0:T(2,128)(2,1)} %text_ref.1) | copy-start | bytes 9220

commit v9 on v8

--- a/solution.py
+++ b/solution.py
@@ -143,7 +143,7 @@
 
 
 def backward_kernel(*refs):
-    shards, t_ref, refs = refs[:MP], refs[MP], refs[MP + 1:]
+    shards, own_ref, t_ref, refs = refs[:MP], refs[MP], refs[MP + 1], refs[MP + 2:]
     part_ref, *qkv_ref, att_ref, scalar_ref, wo_ref = refs[:7]
     keep_ref, give_ref, grad_ref, turn_ref, text_ref, both_ref = refs[7:]
     me = lax.axis_index("dp")
@@ -155,7 +155,7 @@
     scale = scalar_ref[0:1, :]
     image_inv = lax.rsqrt(jnp.sum(pooled * pooled, axis=-1, keepdims=True) + EPS)
     unit = pooled * image_inv
-    text = t_ref[...]
+    text = jnp.concatenate([own_ref[...], t_ref[...]], axis=0)
     wide_text = text.astype(F32)
     square = pieces(wide_text * wide_text, 2)
     ones = jnp.ones((IMG, D), BF16)
@@ -362,12 +362,13 @@
     texts = jnp.concatenate(texts, axis=0)
     texts = [texts] + [over_dp(texts, 0, dx, 0) for dx in (1, 2, 3)]
     parts = lax.all_to_all(part, "mp", 0, 0)
-    texts, = call(join_kernel, [((TEXT, D), BF16)], [], *texts)
+    own_texts = texts[0]
+    texts, = call(join_kernel, [((96, D), BF16)], [], *texts[1:])
     keep, give = call(
         backward_kernel,
         [((8, ROWS, 128), BF16)] * 2,
         [((512, 512), F32), ((256, 128), F32), ((256, 128), F32), ((2, 8, ROWS, 128), BF16)],
-        *shards, texts, parts, *qkv, attended, scalars, out_weight,
+        *shards, own_texts, texts, parts, *qkv, attended, scalars, out_weight,
     )
     other = lax.ppermute(give, "dp", [(i, i ^ 1) for i in range(DP)])
     send = (keep.astype(F32) + other.astype(F32)).astype(BF16)

time: 70.8 us -> 70.8 us (level)
    unnamed x16 -> x18, local copies, waits for them, and re-layouts: 4.06 us -> 4.73 us
  transfers between devices with their start and end apart: 14 -> 14, of which waited for: 8 -> 8; matrix products, arithmetic and copies ran while one was open for 1% -> 1% of each run, Pallas kernels for 5% -> 4%
where the time goes in v9:
time: 70.8 us; the launch traced here: 70.3 us
  starting transfers between devices  29.7 us (42%)
  blocking collectives  15.7 us (22%)
  waiting for transfers between devices  8.6 us (12%)
  Pallas kernels  8.4 us (12%)
  local copies, waits for them, and re-layouts  5.61 us (8%)
  between operations  2.08 us (3%)
    all_to_all x1, blocking collectives, body(): lax.all_to_all(send, 'dp', 0, 0, axis_index_groups=[list(range(c, DP, 2))...  15.7 us
    ppermute x7, starting transfers between devices, over_mp(): return lax.ppermute(block, 'mp', route)  15.4 us
    pallas_call x9, Pallas kernels, call(): pl.pallas_call(kernel, out_shape=[jax.ShapeDtypeStruct(*o) for o in outs]...  8.4 us
    ppermute x5, starting transfers between devices, over_dp(): return lax.ppermute(block, 'dp', route)  6.27 us
    all_to_all x1, starting transfers between devices, body(): parts = lax.all_to_all(part, 'mp', 0, 0)  5.53 us
    unnamed x18, local copies, waits for them, and re-layouts  4.73 us
    ppermute x5, waiting for transfers between devices, over_dp(): return lax.ppermute(block, 'dp', route)  4.39 us
    ppermute x1, starting transfers between devices, body(): other = lax.ppermute(give, 'dp', [(i, i ^ 1) for i in range(DP)])  2.5 us
  transfers between devices with their start and end apart: 14, of which 8 were waited for; matrix products, arithmetic and copies ran while one was open for 1% of the time, Pallas kernels for 4%

profile of v9, /device:TPU:1, one launch (start us, length us, event | category | flops | bytes accessed | tf_op | source)
XLA Modules:
  0.0 70.3 jit_solution(12869700398563475466)
XLA Ops:
  0.6 1.5 %collective-permute-start = (bf16[1,1536]{1,0:T(2,128)(2,1)}, bf16[1,1536]{1,0:T(2,128)(2,1)S(1)}, u32[]{:S(2)}, u32[]{:S(2)}) collective-permute-start(bf16[1,1536]{1,0:T(2,128)(2,1)} %text_ref.1), channel_id=1, source_target_pairs={{0,8},{8,0},{16,24},{24,16},{32,40},{40,32},{48,56},{56,48},{64,72... | collective-permute-start | bytes 9224 | tf_op jit(solution)/shard_map/ppermute | solution.py:312
  2.1 0.9 %copy-done.4 = bf16[8,12288]{1,0:T(8,128)(2,1)S(1)} copy-done((bf16[8,12288]{1,0:T(8,128)(2,1)S(1)}, bf16[8,12288]{1,0:T(8,128)(2,1)}, u32[]{:S(2)}) %copy-start.4) | copy-done | bytes 196632
  3.1 0.3 shard_map.94
  3.4 0.8 %dynamic_update_slice.6 = bf16[72,1536]{1,0:T(8,128)(2,1)S(1)} dynamic-update-slice(bf16[72,1536]{1,0:T(8,128)(2,1)S(1)} %get-tuple-element.21, bf16[1,1536]{1,0:T(2,128)(2,1)} %text_ref.1, s32[]{:T(128)} %constant.0.clone.1, s32[]{:T(128)} %constant.1.clone.1) | dynamic-update-slice | bytes 6148 | tf_op jit(solution)/shard_map/dynamic_update_slice | solution.py:333
  4.2 0.0 collective-permute-done
  4.2 0.1 dynamic_update_slice.7.refs_0_
  4.3 3.1 %collective-permute-start.2 = (bf16[72,1536]{1,0:T(8,128)(2,1)S(1)}, bf16[72,1536]{1,0:T(8,128)(2,1)S(1)}, u32[]{:S(2)}, u32[]{:S(2)}) collective-permute-start(bf16[72,1536]{1,0:T(8,128)(2,1)S(1)} %dynamic_update_slice.7.refs_0_), channel_id=1, source_target_pairs={{0,1},{1,0},{2,3},{3,2},{4,5},{5,4},{6,7},{7,6},{8,9},{9,8},{10,11... | collective-permute-start | bytes 663560 | tf_op jit(solution)/shard_map/ppermute | solution.py:305
  7.3 3.6 %collective-permute-start.4 = (bf16[72,1536]{1,0:T(8,128)(2,1)S(1)}, bf16[72,1536]{1,0:T(8,128)(2,1)S(1)}, u32[]{:S(2)}, u32[]{:S(2)}) collective-permute-start(bf16[72,1536]{1,0:T(8,128)(2,1)S(1)} %dynamic_update_slice.7.refs_0_), channel_id=1, source_target_pairs={{0,4},{1,5},{2,6},{3,7},{4,0},{5,1},{6,2},{7,3},{8,12},{9,13},{10,... | collective-permute-start | bytes 663560 | tf_op jit(solution)/shard_map/ppermute | solution.py:305
  10.9 0.7 %collective-permute-start.1 = (bf16[72,1536]{1,0:T(8,128)(2,1)S(1)}, bf16[72,1536]{1,0:T(8,128)(2,1)S(1)}, u32[]{:S(2)}, u32[]{:S(2)}) collective-permute-start(bf16[72,1536]{1,0:T(8,128)(2,1)S(1)} %dynamic_update_slice.7.refs_0_), channel_id=1, source_target_pairs={{0,2},{1,3},{2,4},{3,5},{4,6},{5,7},{6,0},{7,1},{8,10},{9,11},{10,... | collective-permute-start | bytes 663560 | tf_op jit(solution)/shard_map/ppermute | solution.py:305
  11.7 1.9 %collective-permute-start.3 = (bf16[72,1536]{1,0:T(8,128)(2,1)S(1)}, bf16[72,1536]{1,0:T(8,128)(2,1)S(1)}, u32[]{:S(2)}, u32[]{:S(2)}) collective-permute-start(bf16[72,1536]{1,0:T(8,128)(2,1)S(1)} %dynamic_update_slice.7.refs_0_), channel_id=1, source_target_pairs={{0,6},{1,7},{2,0},{3,1},{4,2},{5,3},{6,4},{7,5},{8,14},{9,15},{10,... | collective-permute-start | bytes 663560 | tf_op jit(solution)/shard_map/ppermute | solution.py:305
  13.6 0.0 collective-permute-done.2.refs_1_
  13.6 1.0 %collective-permute-start.5 = (bf16[72,1536]{1,0:T(8,128)(2,1)S(1)}, bf16[72,1536]{1,0:T(8,128)(2,1)S(1)}, u32[]{:S(2)}, u32[]{:S(2)}) collective-permute-start(bf16[72,1536]{1,0:T(8,128)(2,1)S(1)} %collective-permute-done.2.refs_1_), channel_id=1, source_target_pairs={{0,2},{1,3},{2,4},{3,5},{4,6},{5,7},{6,0},{7,1},{8,10},{9,11},{10,... | collective-permute-start | bytes 663560 | tf_op jit(solution)/shard_map/ppermute | solution.py:305
  14.6 2.1 %collective-permute-start.6 = (bf16[72,1536]{1,0:T(8,128)(2,1)S(1)}, bf16[72,1536]{1,0:T(8,128)(2,1)S(1)}, u32[]{:S(2)}, u32[]{:S(2)}) collective-permute-start(bf16[72,1536]{1,0:T(8,128)(2,1)S(1)} %collective-permute-done.2.refs_1_), channel_id=1, source_target_pairs={{0,6},{1,7},{2,0},{3,1},{4,2},{5,3},{6,4},{7,5},{8,14},{9,15},{10,... | collective-permute-start | bytes 663560 | tf_op jit(solution)/shard_map/ppermute | solution.py:305
  16.7 0.0 collective-permute-done.4.refs_4_
  16.8 2.9 %collective-permute-start.7 = (bf16[72,1536]{1,0:T(8,128)(2,1)S(1)}, bf16[72,1536]{1,0:T(8,128)(2,1)S(1)}, u32[]{:S(2)}, u32[]{:S(2)}) collective-permute-start(bf16[72,1536]{1,0:T(8,128)(2,1)S(1)} %collective-permute-done.4.refs_4_), channel_id=1, source_target_pairs={{0,1},{1,0},{2,3},{3,2},{4,5},{5,4},{6,7},{7,6},{8,9},{9,8},{10,11... | collective-permute-start | bytes 663560 | tf_op jit(solution)/shard_map/ppermute | solution.py:305
  21.0 0.6 collective-permute-done.1.refs_2_
  21.6 0.1 collective-permute-done.3.refs_3_
  21.7 1.5 %copy-done.1 = bf16[3,192,1536]{2,1,0:T(8,128)(2,1)S(1)} copy-done((bf16[3,192,1536]{2,1,0:T(8,128)(2,1)S(1)}, bf16[3,192,1536]{2,1,0:T(8,128)(2,1)}, u32[]{:S(2)}) %copy-start.1) | copy-done | bytes 1769496
  23.2 0.7 copy-done.6
  23.9 1.0 %shard_map.96 = (bf16[3,320,192]{2,1,0:T(8,128)(2,1)S(1)}, bf16[3,192,1536]{2,1,0:T(8,128)(2,1)S(1)}) custom-call(bf16[72,1536]{1,0:T(8,128)(2,1)S(1)} %dynamic_update_slice.7.refs_0_, bf16[72,1536]{1,0:T(8,128)(2,1)S(1)} %collective-permute-done.2.refs_1_, bf16[72,1536]{1,0:T(8,128)(2,1)S(1)} %collective-permute-done.1.refs_2_, ...), custom_call_target="tpu_custom_call" | custom-call | tf_op jit(solution)/shard_map/pallas_call | solution.py:293
  25.0 0.0 copy-start
  25.0 1.3 %collective-permute-done.5.refs_5_.refs_0_ = bf16[72,1536]{1,0:T(8,128)(2,1)S(1)} collective-permute-done((bf16[72,1536]{1,0:T(8,128)(2,1)S(1)}, bf16[72,1536]{1,0:T(8,128)(2,1)S(1)}, u32[]{:S(2)}, u32[]{:S(2)}) %collective-permute-start.5) | collective-permute-done | bytes 221216 | tf_op jit(solution)/shard_map/ppermute | solution.py:305
  26.3 0.1 collective-permute-done.6.refs_6_.refs_1_
  26.5 0.1 shard_map.97.refs_1_
  26.6 0.0 collective-permute-done.7.refs_0_.refs_2_.refs_7_
  26.6 0.5 collective-permute-start.8
  27.1 0.0 copy-done
  27.1 1.3 %shard_map.100 = (bf16[8,8,1536]{2,1,0:T(8,128)(2,1)S(1)}, bf16[512,256]{1,0:T(8,128)(2,1)S(1)}, bf16[512,256]{1,0:T(8,128)(2,1)S(1)}, bf16[512,192]{1,0:T(8,128)(2,1)S(1)}, f32[8,192]{1,0:T(8,128)S(1)}) custom-call(bf16[72,1536]{1,0:T(8,128)(2,1)S(1)} %collective-permute-done.5.refs_5_.refs_0_, bf16[72,1536]{1,0:T(8,128)(2,1)S(1)} %collective-permute-done.6.refs_6_.refs_1_, ...), custom_call_target="tpu_custom_call" | custom-call | tf_op jit(solution)/shard_map/pallas_call | solution.py:293
  28.5 0.7 copy-done.5
  29.1 5.5 %all-to-all-start = ((bf16[8,8,1536]{2,1,0:T(8,128)(2,1)}), bf16[8,8,1536]{2,1,0:T(8,128)(2,1)S(1)}, u32[]{:S(2)}, u32[]{:S(2)}) async-start(bf16[8,8,1536]{2,1,0:T(8,128)(2,1)} %copy-done.5), calls=%async_computation | async-start | bytes 393216 | tf_op jit(solution)/shard_map/all_to_all | solution.py:364
  34.7 0.0 collective-permute-done.8
  34.7 2.8 %collective-permute-start.10 = (bf16[32,1536]{1,0:T(8,128)(2,1)S(1)}, bf16[32,1536]{1,0:T(8,128)(2,1)S(1)}, u32[]{:S(2)}, u32[]{:S(2)}) collective-permute-start(bf16[32,1536]{1,0:T(8,128)(2,1)S(1)} %pad_maximum_fusion.refs_8_), channel_id=1, source_target_pairs={{0,32},{8,40},{16,48},{24,56},{32,0},{40,8},{48,16},{56,24},{64,96... | collective-permute-start | bytes 294920 | tf_op jit(solution)/shard_map/ppermute | solution.py:312
  37.5 0.9 %collective-permute-start.11 = (bf16[32,1536]{1,0:T(8,128)(2,1)S(1)}, bf16[32,1536]{1,0:T(8,128)(2,1)S(1)}, u32[]{:S(2)}, u32[]{:S(2)}) collective-permute-start(bf16[32,1536]{1,0:T(8,128)(2,1)S(1)} %pad_maximum_fusion.refs_8_), channel_id=1, source_target_pairs={{0,48},{8,56},{16,0},{24,8},{32,16},{40,24},{48,32},{56,40},{64,11... | collective-permute-start | bytes 294920 | tf_op jit(solution)/shard_map/ppermute | solution.py:312
  38.4 0.6 collective-permute-start.9
  39.0 0.8 %collective-permute-done.10.refs_1_ = bf16[32,1536]{1,0:T(8,128)(2,1)S(1)} collective-permute-done((bf16[32,1536]{1,0:T(8,128)(2,1)S(1)}, bf16[32,1536]{1,0:T(8,128)(2,1)S(1)}, u32[]{:S(2)}, u32[]{:S(2)}) %collective-permute-start.10) | collective-permute-done | bytes 98336 | tf_op jit(solution)/shard_map/ppermute | solution.py:312
  39.8 2.3 %collective-permute-done.11.refs_2_ = bf16[32,1536]{1,0:T(8,128)(2,1)S(1)} collective-permute-done((bf16[32,1536]{1,0:T(8,128)(2,1)S(1)}, bf16[32,1536]{1,0:T(8,128)(2,1)S(1)}, u32[]{:S(2)}, u32[]{:S(2)}) %collective-permute-start.11) | collective-permute-done | bytes 98336 | tf_op jit(solution)/shard_map/ppermute | solution.py:312
  42.1 0.0 copy-done.2
  42.1 1.3 %collective-permute-done.9.refs_0_ = bf16[32,1536]{1,0:T(8,128)(2,1)S(1)} collective-permute-done((bf16[32,1536]{1,0:T(8,128)(2,1)S(1)}, bf16[32,1536]{1,0:T(8,128)(2,1)S(1)}, u32[]{:S(2)}, u32[]{:S(2)}) %collective-permute-start.9) | collective-permute-done | bytes 98336 | tf_op jit(solution)/shard_map/ppermute | solution.py:312
  43.4 0.0 all-to-all-done.refs_10_
  43.4 0.0 copy-start.3
  43.4 0.9 %copy-done.3 = bf16[512,192]{1,0:T(8,128)(2,1)S(1)} copy-done((bf16[512,192]{1,0:T(8,128)(2,1)S(1)}, bf16[512,192]{1,0:T(8,128)(2,1)}, u32[]{:S(2)}) %copy-start.3) | copy-done | bytes 196632
  44.4 4.1 %shard_map.101 = (bf16[8,400,128]{2,1,0:T(8,128)(2,1)S(1)}, bf16[8,400,128]{2,1,0:T(8,128)(2,1)S(1)}) custom-call(bf16[72,1536]{1,0:T(8,128)(2,1)S(1)} %dynamic_update_slice.7.refs_0_, bf16[72,1536]{1,0:T(8,128)(2,1)S(1)} %collective-permute-done.2.refs_1_, bf16[72,1536]{1,0:T(8,128)(2,1)S(1)} %collective-permute-done.1.refs_2_, ...), custom_call_target="tpu_custom_call" | custom-call | tf_op jit(solution)/shard_map/pallas_call | solution.py:293
  48.4 2.5 %collective-permute-start.12 = (bf16[8,400,128]{2,1,0:T(8,128)(2,1)S(1)}, bf16[8,400,128]{2,1,0:T(8,128)(2,1)S(1)}, u32[]{:S(2)}, u32[]{:S(2)}) collective-permute-start(bf16[8,400,128]{2,1,0:T(8,128)(2,1)S(1)} %get-tuple-element.38), channel_id=1, source_target_pairs={{0,8},{8,0},{16,24},{24,16},{32,40},{40,32},{48,56},{56,48},{64,72... | collective-permute-start | bytes 2457608 | tf_op jit(solution)/shard_map/ppermute | solution.py:373
  50.9 2.0 %collective-permute-done.12 = bf16[8,400,128]{2,1,0:T(8,128)(2,1)S(1)} collective-permute-done((bf16[8,400,128]{2,1,0:T(8,128)(2,1)S(1)}, bf16[8,400,128]{2,1,0:T(8,128)(2,1)S(1)}, u32[]{:S(2)}, u32[]{:S(2)}) %collective-permute-start.12) | collective-permute-done | bytes 819232 | tf_op jit(solution)/shard_map/ppermute | solution.py:373
  52.9 0.2 add_convert_fusion
  53.1 15.7 %all_to_all.10.r_ref = bf16[8,400,128]{2,1,0:T(8,128)(2,1)S(1)} all-to-all(bf16[8,400,128]{2,1,0:T(8,128)(2,1)S(1)} %add_convert_fusion), channel_id=1, replica_groups={{0,16,32,48,64,80,96,112},{8,24,40,56,72,88,104,120},{1,17,33,49,65,81,..., dimensions={0} | all-to-all | bytes 1638400 | tf_op jit(solution)/shard_map/all_to_all | solution.py:375
  68.9 0.0 copy-done.7
  68.9 1.5 %shard_map.102 = (f32[1,1536]{1,0:T(1,128)}, f32[3,192,96]{2,1,0:T(8,128)}, f32[192,96]{1,0:T(8,128)}) custom-call(bf16[8,400,128]{2,1,0:T(8,128)(2,1)S(1)} %all_to_all.10.r_ref, bf16[1,1536]{1,0:T(2,128)(2,1)S(1)} %copy-done.8, f32[12,128]{1,0:T(8,128)S(1)} %bitcast.2), custom_call_target="tpu_custom_call" | custom-call | tf_op jit(solution)/shard_map/pallas_call | solution.py:293
  (13 shorter events, 0.1 us)
Async XLA Ops:
  0.6 3.5 %collective-permute-start = (bf16[1,1536]{1,0:T(2,128)(2,1)}, bf16[1,1536]{1,0:T(2,128)(2,1)S(1)}, u32[]{:S(2)}, u32[]{:S(2)}) collective-permute-start(bf16[1,1536]{1,0:T(2,128)(2,1)} %text_ref.1), channel_id=1, source_target_pairs={{0,8},{8,0},{16,24},{24,16},{32,40},{40,32},{48,56},{56,48},{64,72... | collective-permute-start | bytes 9224 | tf_op jit(solution)/shard_map/ppermute | solution.py:312
  2.1 0.9 %copy-start.4 = (bf16[8,12288]{1,0:T(8,128)(2,1)S(1)}, bf16[8,12288]{1,0:T(8,128)(2,1)}, u32[]{:S(2)}) copy-start(bf16[8,12288]{1,0:T(8,128)(2,1)} %tok_ref.1) | copy-start | bytes 589828
  4.3 9.4 %collective-permute-start.2 = (bf16[72,1536]{1,0:T(8,128)(2,1)S(1)}, bf16[72,1536]{1,0:T(8,128)(2,1)S(1)}, u32[]{:S(2)}, u32[]{:S(2)}) collective-permute-start(bf16[72,1536]{1,0:T(8,128)(2,1)S(1)} %dynamic_update_slice.7.refs_0_), channel_id=1, source_target_pairs={{0,1},{1,0},{2,3},{3,2},{4,5},{5,4},{6,7},{7,6},{8,9},{9,8},{10,11... | collective-permute-start | bytes 663560 | tf_op jit(solution)/shard_map/ppermute | solution.py:305
  7.3 9.4 %collective-permute-start.4 = (bf16[72,1536]{1,0:T(8,128)(2,1)S(1)}, bf16[72,1536]{1,0:T(8,128)(2,1)S(1)}, u32[]{:S(2)}, u32[]{:S(2)}) collective-permute-start(bf16[72,1536]{1,0:T(8,128)(2,1)S(1)} %dynamic_update_slice.7.refs_0_), channel_id=1, source_target_pairs={{0,4},{1,5},{2,6},{3,7},{4,0},{5,1},{6,2},{7,3},{8,12},{9,13},{10,... | collective-permute-start | bytes 663560 | tf_op jit(solution)/shard_map/ppermute | solution.py:305
  10.9 10.6 %collective-permute-start.1 = (bf16[72,1536]{1,0:T(8,128)(2,1)S(1)}, bf16[72,1536]{1,0:T(8,128)(2,1)S(1)}, u32[]{:S(2)}, u32[]{:S(2)}) collective-permute-start(bf16[72,1536]{1,0:T(8,128)(2,1)S(1)} %dynamic_update_slice.7.refs_0_), channel_id=1, source_target_pairs={{0,2},{1,3},{2,4},{3,5},{4,6},{5,7},{6,0},{7,1},{8,10},{9,11},{10,... | collective-permute-start | bytes 663560 | tf_op jit(solution)/shard_map/ppermute | solution.py:305
  11.7 10.0 %collective-permute-start.3 = (bf16[72,1536]{1,0:T(8,128)(2,1)S(1)}, bf16[72,1536]{1,0:T(8,128)(2,1)S(1)}, u32[]{:S(2)}, u32[]{:S(2)}) collective-permute-start(bf16[72,1536]{1,0:T(8,128)(2,1)S(1)} %dynamic_update_slice.7.refs_0_), channel_id=1, source_target_pairs={{0,6},{1,7},{2,0},{3,1},{4,2},{5,3},{6,4},{7,5},{8,14},{9,15},{10,... | collective-permute-start | bytes 663560 | tf_op jit(solution)/shard_map/ppermute | solution.py:305
  13.6 12.7 %collective-permute-start.5 = (bf16[72,1536]{1,0:T(8,128)(2,1)S(1)}, bf16[72,1536]{1,0:T(8,128)(2,1)S(1)}, u32[]{:S(2)}, u32[]{:S(2)}) collective-permute-start(bf16[72,1536]{1,0:T(8,128)(2,1)S(1)} %collective-permute-done.2.refs_1_), channel_id=1, source_target_pairs={{0,2},{1,3},{2,4},{3,5},{4,6},{5,7},{6,0},{7,1},{8,10},{9,11},{10,... | collective-permute-start | bytes 663560 | tf_op jit(solution)/shard_map/ppermute | solution.py:305
  14.6 11.8 %collective-permute-start.6 = (bf16[72,1536]{1,0:T(8,128)(2,1)S(1)}, bf16[72,1536]{1,0:T(8,128)(2,1)S(1)}, u32[]{:S(2)}, u32[]{:S(2)}) collective-permute-start(bf16[72,1536]{1,0:T(8,128)(2,1)S(1)} %collective-permute-done.2.refs_1_), channel_id=1, source_target_pairs={{0,6},{1,7},{2,0},{3,1},{4,2},{5,3},{6,4},{7,5},{8,14},{9,15},{10,... | collective-permute-start | bytes 663560 | tf_op jit(solution)/shard_map/ppermute | solution.py:305
  16.8 9.8 %collective-permute-start.7 = (bf16[72,1536]{1,0:T(8,128)(2,1)S(1)}, bf16[72,1536]{1,0:T(8,128)(2,1)S(1)}, u32[]{:S(2)}, u32[]{:S(2)}) collective-permute-start(bf16[72,1536]{1,0:T(8,128)(2,1)S(1)} %collective-permute-done.4.refs_4_), channel_id=1, source_target_pairs={{0,1},{1,0},{2,3},{3,2},{4,5},{5,4},{6,7},{7,6},{8,9},{9,8},{10,11... | collective-permute-start | bytes 663560 | tf_op jit(solution)/shard_map/ppermute | solution.py:305
  21.7 1.5 %copy-start.1 = (bf16[3,192,1536]{2,1,0:T(8,128)(2,1)S(1)}, bf16[3,192,1536]{2,1,0:T(8,128)(2,1)}, u32[]{:S(2)}) copy-start(bf16[3,192,1536]{2,1,0:T(8,128)(2,1)} %refs_5_.2) | copy-start | bytes 5308420
  23.2 0.7 copy-start.6
  25.0 2.2 %copy-start = (bf16[192,1536]{1,0:T(8,128)(2,1)S(1)}, bf16[192,1536]{1,0:T(8,128)(2,1)}, u32[]{:S(2)}) copy-start(bf16[192,1536]{1,0:T(8,128)(2,1)} %refs_16_.1) | copy-start | bytes 1769476
  26.6 8.0 %collective-permute-start.8 = (bf16[16,1536]{1,0:T(8,128)(2,1)S(1)}, bf16[16,1536]{1,0:T(8,128)(2,1)S(1)}, u32[]{:S(2)}, u32[]{:S(2)}) collective-permute-start(bf16[16,1536]{1,0:T(8,128)(2,1)S(1)} %shard_map.98), channel_id=1, source_target_pairs={{0,64},{8,72},{16,80},{24,88},{32,96},{40,104},{48,112},{56,120},{... | collective-permute-start | bytes 147464 | tf_op jit(solution)/shard_map/ppermute | solution.py:312
  28.5 0.7 copy-start.5
  29.1 12.9 %copy-start.2 = (bf16[512,192]{1,0:T(8,128)(2,1)}, bf16[512,192]{1,0:T(8,128)(2,1)S(1)}, u32[]{:S(2)}) copy-start(bf16[512,192]{1,0:T(8,128)(2,1)S(1)} %get-tuple-element.34.refs_13_) | copy-start | bytes 589828
  29.1 14.3 %all-to-all-start = ((bf16[8,8,1536]{2,1,0:T(8,128)(2,1)}), bf16[8,8,1536]{2,1,0:T(8,128)(2,1)S(1)}, u32[]{:S(2)}, u32[]{:S(2)}) async-start(bf16[8,8,1536]{2,1,0:T(8,128)(2,1)} %copy-done.5), calls=%async_computation | async-start | bytes 393216 | tf_op jit(solution)/shard_map/all_to_all | solution.py:364
  34.7 5.1 %collective-permute-start.10 = (bf16[32,1536]{1,0:T(8,128)(2,1)S(1)}, bf16[32,1536]{1,0:T(8,128)(2,1)S(1)}, u32[]{:S(2)}, u32[]{:S(2)}) collective-permute-start(bf16[32,1536]{1,0:T(8,128)(2,1)S(1)} %pad_maximum_fusion.refs_8_), channel_id=1, source_target_pairs={{0,32},{8,40},{16,48},{24,56},{32,0},{40,8},{48,16},{56,24},{64,96... | collective-permute-start | bytes 294920 | tf_op jit(solution)/shard_map/ppermute | solution.py:312
  37.5 4.5 %collective-permute-start.11 = (bf16[32,1536]{1,0:T(8,128)(2,1)S(1)}, bf16[32,1536]{1,0:T(8,128)(2,1)S(1)}, u32[]{:S(2)}, u32[]{:S(2)}) collective-permute-start(bf16[32,1536]{1,0:T(8,128)(2,1)S(1)} %pad_maximum_fusion.refs_8_), channel_id=1, source_target_pairs={{0,48},{8,56},{16,0},{24,8},{32,16},{40,24},{48,32},{56,40},{64,11... | collective-permute-start | bytes 294920 | tf_op jit(solution)/shard_map/ppermute | solution.py:312
  38.4 5.0 %collective-permute-start.9 = (bf16[32,1536]{1,0:T(8,128)(2,1)S(1)}, bf16[32,1536]{1,0:T(8,128)(2,1)S(1)}, u32[]{:S(2)}, u32[]{:S(2)}) collective-permute-start(bf16[32,1536]{1,0:T(8,128)(2,1)S(1)} %pad_maximum_fusion.refs_8_), channel_id=1, source_target_pairs={{0,16},{8,24},{16,32},{24,40},{32,48},{40,56},{48,0},{56,8},{64,80... | collective-permute-start | bytes 294920 | tf_op jit(solution)/shard_map/ppermute | solution.py:312
  43.4 1.0 %copy-start.3 = (bf16[512,192]{1,0:T(8,128)(2,1)S(1)}, bf16[512,192]{1,0:T(8,128)(2,1)}, u32[]{:S(2)}) copy-start(bf16[512,192]{1,0:T(8,128)(2,1)} %copy-done.2) | copy-start | bytes 589828
  48.4 4.5 %collective-permute-start.12 = (bf16[8,400,128]{2,1,0:T(8,128)(2,1)S(1)}, bf16[8,400,128]{2,1,0:T(8,128)(2,1)S(1)}, u32[]{:S(2)}, u32[]{:S(2)}) collective-permute-start(bf16[8,400,128]{2,1,0:T(8,128)(2,1)S(1)} %get-tuple-element.38), channel_id=1, source_target_pairs={{0,8},{8,0},{16,24},{24,16},{32,40},{40,32},{48,56},{56,48},{64,72... | collective-permute-start | bytes 2457608 | tf_op jit(solution)/shard_map/ppermute | solution.py:373
  52.9 16.0 %copy-start.7 = (f32[1536]{0:T(1024)S(1)}, f32[1536]{0:T(1024)}, u32[]{:S(2)}) copy-start(f32[1536]{0:T(1024)} %param.8) | copy-start | bytes 18436
  52.9 16.0 %copy-start.8 = (bf16[1,1536]{1,0:T(2,128)(2,1)S(1)}, bf16[1,1536]{1,0:T(2,128)(2,1)}, u32[]{:S(2)}) copy-start(bf16[1,1536]{1,0:T(2,128)(2,1)} %text_ref.1) | copy-start | bytes 9220

commit v10 on v9

--- a/solution.py
+++ b/solution.py
@@ -143,7 +143,7 @@
 
 
 def backward_kernel(*refs):
-    shards, own_ref, t_ref, refs = refs[:MP], refs[MP], refs[MP + 1], refs[MP + 2:]
+    shards, own_ref, t_ref, last_ref, refs = refs[:MP], *refs[MP:MP + 3], refs[MP + 3:]
     part_ref, *qkv_ref, att_ref, scalar_ref, wo_ref = refs[:7]
     keep_ref, give_ref, grad_ref, turn_ref, text_ref, both_ref = refs[7:]
     me = lax.axis_index("dp")
@@ -155,7 +155,7 @@
     scale = scalar_ref[0:1, :]
     image_inv = lax.rsqrt(jnp.sum(pooled * pooled, axis=-1, keepdims=True) + EPS)
     unit = pooled * image_inv
-    text = jnp.concatenate([own_ref[...], t_ref[...]], axis=0)
+    text = jnp.concatenate([own_ref[...], t_ref[...], last_ref[...]], axis=0)
     wide_text = text.astype(F32)
     square = pieces(wide_text * wide_text, 2)
     ones = jnp.ones((IMG, D), BF16)
@@ -363,12 +363,13 @@
     texts = [texts] + [over_dp(texts, 0, dx, 0) for dx in (1, 2, 3)]
     parts = lax.all_to_all(part, "mp", 0, 0)
     own_texts = texts[0]
-    texts, = call(join_kernel, [((96, D), BF16)], [], *texts[1:])
+    last_texts = texts[3]
+    texts, = call(join_kernel, [((64, D), BF16)], [], *texts[1:3])
     keep, give = call(
         backward_kernel,
         [((8, ROWS, 128), BF16)] * 2,
         [((512, 512), F32), ((256, 128), F32), ((256, 128), F32), ((2, 8, ROWS, 128), BF16)],
-        *shards, own_texts, texts, parts, *qkv, attended, scalars, out_weight,
+        *shards, own_texts, texts, last_texts, parts, *qkv, attended, scalars, out_weight,
     )
     other = lax.ppermute(give, "dp", [(i, i ^ 1) for i in range(DP)])
     send = (keep.astype(F32) + other.astype(F32)).astype(BF16)

time: 70.8 us -> 72 us (1.017)
  waiting for transfers between devices: 8.6 us -> 6.95 us
  blocking collectives: 15.7 us -> 17.3 us
    ppermute x5, waiting for transfers between devices: 4.39 us -> 2.74 us  [over_dp(): return lax.ppermute(block, 'dp', route)]
    all_to_all x1, blocking collectives: 15.7 us -> 17.3 us  [body(): lax.all_to_all(send, 'dp', 0, 0, axis_index_groups=[list(range(c, DP, 2))...]
    ppermute x5, starting transfers between devices: 6.27 us -> 7.48 us  [over_dp(): return lax.ppermute(block, 'dp', route)]
    unnamed x18 -> x16, local copies, waits for them, and re-layouts: 4.73 us -> 4.76 us
  transfers between devices with their start and end apart: 14 -> 14, of which waited for: 8 -> 6; matrix products, arithmetic and copies ran while one was open for 1% -> 1% of each run, Pallas kernels for 4% -> 5%
where the time goes in v10:
time: 72 us; the launch traced here: 71.5 us
  starting transfers between devices  30.2 us (42%)
  blocking collectives  17.3 us (24%)
  Pallas kernels  9.09 us (13%)
  waiting for transfers between devices  6.95 us (10%)
  local copies, waits for them, and re-layouts  5.64 us (8%)
  between operations  2.07 us (3%)
    all_to_all x1, blocking collectives, body(): lax.all_to_all(send, 'dp', 0, 0, axis_index_groups=[list(range(c, DP, 2))...  17.3 us
    ppermute x7, starting transfers between devices, over_mp(): return lax.ppermute(block, 'mp', route)  15.4 us
    pallas_call x9, Pallas kernels, call(): pl.pallas_call(kernel, out_shape=[jax.ShapeDtypeStruct(*o) for o in outs]...  9.09 us
    ppermute x5, starting transfers between devices, over_dp(): return lax.ppermute(block, 'dp', route)  7.48 us
    all_to_all x1, starting transfers between devices, body(): parts = lax.all_to_all(part, 'mp', 0, 0)  5.53 us
    unnamed x16, local copies, waits for them, and re-layouts  4.76 us
    ppermute x5, waiting for transfers between devices, over_dp(): return lax.ppermute(block, 'dp', route)  2.74 us
    ppermute x7, waiting for transfers between devices, over_mp(): return lax.ppermute(block, 'mp', route)  2.25 us
  transfers between devices with their start and end apart: 14, of which 6 were waited for; matrix products, arithmetic and copies ran while one was open for 1% of the time, Pallas kernels for 5%

profile of v10, /device:TPU:1, one launch (start us, length us, event | category | flops | bytes accessed | tf_op | source)
XLA Modules:
  0.0 71.5 jit_solution(7415619918361241152)
XLA Ops:
  0.6 1.5 %collective-permute-start = (bf16[1,1536]{1,0:T(2,128)(2,1)}, bf16[1,1536]{1,0:T(2,128)(2,1)S(1)}, u32[]{:S(2)}, u32[]{:S(2)}) collective-permute-start(bf16[1,1536]{1,0:T(2,128)(2,1)} %text_ref.1), channel_id=1, source_target_pairs={{0,8},{8,0},{16,24},{24,16},{32,40},{40,32},{48,56},{56,48},{64,72... | collective-permute-start | bytes 9224 | tf_op jit(solution)/shard_map/ppermute | solution.py:312
  2.1 0.9 %copy-done.4 = bf16[8,12288]{1,0:T(8,128)(2,1)S(1)} copy-done((bf16[8,12288]{1,0:T(8,128)(2,1)S(1)}, bf16[8,12288]{1,0:T(8,128)(2,1)}, u32[]{:S(2)}) %copy-start.4) | copy-done | bytes 196632
  3.1 0.3 shard_map.94
  3.4 0.8 %dynamic_update_slice.6 = bf16[72,1536]{1,0:T(8,128)(2,1)S(1)} dynamic-update-slice(bf16[72,1536]{1,0:T(8,128)(2,1)S(1)} %get-tuple-element.21, bf16[1,1536]{1,0:T(2,128)(2,1)} %text_ref.1, s32[]{:T(128)} %constant.0.clone.1, s32[]{:T(128)} %constant.1.clone.1) | dynamic-update-slice | bytes 6148 | tf_op jit(solution)/shard_map/dynamic_update_slice | solution.py:333
  4.2 0.0 collective-permute-done
  4.2 0.1 dynamic_update_slice.7.refs_0_
  4.3 3.1 %collective-permute-start.2 = (bf16[72,1536]{1,0:T(8,128)(2,1)S(1)}, bf16[72,1536]{1,0:T(8,128)(2,1)S(1)}, u32[]{:S(2)}, u32[]{:S(2)}) collective-permute-start(bf16[72,1536]{1,0:T(8,128)(2,1)S(1)} %dynamic_update_slice.7.refs_0_), channel_id=1, source_target_pairs={{0,1},{1,0},{2,3},{3,2},{4,5},{5,4},{6,7},{7,6},{8,9},{9,8},{10,11... | collective-permute-start | bytes 663560 | tf_op jit(solution)/shard_map/ppermute | solution.py:305
  7.3 3.6 %collective-permute-start.4 = (bf16[72,1536]{1,0:T(8,128)(2,1)S(1)}, bf16[72,1536]{1,0:T(8,128)(2,1)S(1)}, u32[]{:S(2)}, u32[]{:S(2)}) collective-permute-start(bf16[72,1536]{1,0:T(8,128)(2,1)S(1)} %dynamic_update_slice.7.refs_0_), channel_id=1, source_target_pairs={{0,4},{1,5},{2,6},{3,7},{4,0},{5,1},{6,2},{7,3},{8,12},{9,13},{10,... | collective-permute-start | bytes 663560 | tf_op jit(solution)/shard_map/ppermute | solution.py:305
  10.9 0.7 %collective-permute-start.1 = (bf16[72,1536]{1,0:T(8,128)(2,1)S(1)}, bf16[72,1536]{1,0:T(8,128)(2,1)S(1)}, u32[]{:S(2)}, u32[]{:S(2)}) collective-permute-start(bf16[72,1536]{1,0:T(8,128)(2,1)S(1)} %dynamic_update_slice.7.refs_0_), channel_id=1, source_target_pairs={{0,2},{1,3},{2,4},{3,5},{4,6},{5,7},{6,0},{7,1},{8,10},{9,11},{10,... | collective-permute-start | bytes 663560 | tf_op jit(solution)/shard_map/ppermute | solution.py:305
  11.7 1.9 %collective-permute-start.3 = (bf16[72,1536]{1,0:T(8,128)(2,1)S(1)}, bf16[72,1536]{1,0:T(8,128)(2,1)S(1)}, u32[]{:S(2)}, u32[]{:S(2)}) collective-permute-start(bf16[72,1536]{1,0:T(8,128)(2,1)S(1)} %dynamic_update_slice.7.refs_0_), channel_id=1, source_target_pairs={{0,6},{1,7},{2,0},{3,1},{4,2},{5,3},{6,4},{7,5},{8,14},{9,15},{10,... | collective-permute-start | bytes 663560 | tf_op jit(solution)/shard_map/ppermute | solution.py:305
  13.6 0.0 collective-permute-done.2.refs_1_
  13.6 1.0 %collective-permute-start.5 = (bf16[72,1536]{1,0:T(8,128)(2,1)S(1)}, bf16[72,1536]{1,0:T(8,128)(2,1)S(1)}, u32[]{:S(2)}, u32[]{:S(2)}) collective-permute-start(bf16[72,1536]{1,0:T(8,128)(2,1)S(1)} %collective-permute-done.2.refs_1_), channel_id=1, source_target_pairs={{0,2},{1,3},{2,4},{3,5},{4,6},{5,7},{6,0},{7,1},{8,10},{9,11},{10,... | collective-permute-start | bytes 663560 | tf_op jit(solution)/shard_map/ppermute | solution.py:305
  14.6 2.1 %collective-permute-start.6 = (bf16[72,1536]{1,0:T(8,128)(2,1)S(1)}, bf16[72,1536]{1,0:T(8,128)(2,1)S(1)}, u32[]{:S(2)}, u32[]{:S(2)}) collective-permute-start(bf16[72,1536]{1,0:T(8,128)(2,1)S(1)} %collective-permute-done.2.refs_1_), channel_id=1, source_target_pairs={{0,6},{1,7},{2,0},{3,1},{4,2},{5,3},{6,4},{7,5},{8,14},{9,15},{10,... | collective-permute-start | bytes 663560 | tf_op jit(solution)/shard_map/ppermute | solution.py:305
  16.7 0.0 collective-permute-done.4.refs_4_
  16.8 2.9 %collective-permute-start.7 = (bf16[72,1536]{1,0:T(8,128)(2,1)S(1)}, bf16[72,1536]{1,0:T(8,128)(2,1)S(1)}, u32[]{:S(2)}, u32[]{:S(2)}) collective-permute-start(bf16[72,1536]{1,0:T(8,128)(2,1)S(1)} %collective-permute-done.4.refs_4_), channel_id=1, source_target_pairs={{0,1},{1,0},{2,3},{3,2},{4,5},{5,4},{6,7},{7,6},{8,9},{9,8},{10,11... | collective-permute-start | bytes 663560 | tf_op jit(solution)/shard_map/ppermute | solution.py:305
  21.0 0.6 collective-permute-done.1.refs_2_
  21.6 0.1 collective-permute-done.3.refs_3_
  21.7 1.5 %copy-done.1 = bf16[3,192,1536]{2,1,0:T(8,128)(2,1)S(1)} copy-done((bf16[3,192,1536]{2,1,0:T(8,128)(2,1)S(1)}, bf16[3,192,1536]{2,1,0:T(8,128)(2,1)}, u32[]{:S(2)}) %copy-start.1) | copy-done | bytes 1769496
  23.2 0.7 copy-done.5
  23.9 1.1 %shard_map.96 = (bf16[3,320,192]{2,1,0:T(8,128)(2,1)S(1)}, bf16[3,192,1536]{2,1,0:T(8,128)(2,1)S(1)}) custom-call(bf16[72,1536]{1,0:T(8,128)(2,1)S(1)} %dynamic_update_slice.7.refs_0_, bf16[72,1536]{1,0:T(8,128)(2,1)S(1)} %collective-permute-done.2.refs_1_, bf16[72,1536]{1,0:T(8,128)(2,1)S(1)} %collective-permute-done.1.refs_2_, ...), custom_call_target="tpu_custom_call" | custom-call | tf_op jit(solution)/shard_map/pallas_call | solution.py:293
  25.0 0.0 copy-start
  25.0 1.3 %collective-permute-done.5.refs_5_.refs_0_ = bf16[72,1536]{1,0:T(8,128)(2,1)S(1)} collective-permute-done((bf16[72,1536]{1,0:T(8,128)(2,1)S(1)}, bf16[72,1536]{1,0:T(8,128)(2,1)S(1)}, u32[]{:S(2)}, u32[]{:S(2)}) %collective-permute-start.5) | collective-permute-done | bytes 221216 | tf_op jit(solution)/shard_map/ppermute | solution.py:305
  26.3 0.1 collective-permute-done.6.refs_6_.refs_1_
  26.5 0.1 shard_map.97.refs_1_
  26.6 0.0 collective-permute-done.7.refs_0_.refs_2_.refs_7_
  26.6 0.5 collective-permute-start.8
  27.1 0.0 copy-done
  27.1 2.0 %shard_map.100 = (bf16[8,8,1536]{2,1,0:T(8,128)(2,1)}, bf16[512,256]{1,0:T(8,128)(2,1)S(1)}, bf16[512,256]{1,0:T(8,128)(2,1)S(1)}, bf16[512,192]{1,0:T(8,128)(2,1)S(1)}, f32[8,192]{1,0:T(8,128)S(1)}) custom-call(bf16[72,1536]{1,0:T(8,128)(2,1)S(1)} %collective-permute-done.5.refs_5_.refs_0_, bf16[72,1536]{1,0:T(8,128)(2,1)S(1)} %collective-permute-done.6.refs_6_.refs_1_, ...), custom_call_target="tpu_custom_call" | custom-call | tf_op jit(solution)/shard_map/pallas_call | solution.py:293
  29.1 0.7 copy-done.2
  29.8 5.5 %all-to-all-start = ((bf16[8,8,1536]{2,1,0:T(8,128)(2,1)}), bf16[8,8,1536]{2,1,0:T(8,128)(2,1)S(1)}, u32[]{:S(2)}, u32[]{:S(2)}) async-start(bf16[8,8,1536]{2,1,0:T(8,128)(2,1)} %get-tuple-element.31), calls=%async_computation | async-start | bytes 393216 | tf_op jit(solution)/shard_map/all_to_all | solution.py:364
  35.4 0.0 collective-permute-done.8
  35.4 2.8 %collective-permute-start.10 = (bf16[32,1536]{1,0:T(8,128)(2,1)S(1)}, bf16[32,1536]{1,0:T(8,128)(2,1)S(1)}, u32[]{:S(2)}, u32[]{:S(2)}) collective-permute-start(bf16[32,1536]{1,0:T(8,128)(2,1)S(1)} %pad_maximum_fusion.refs_8_), channel_id=1, source_target_pairs={{0,32},{8,40},{16,48},{24,56},{32,0},{40,8},{48,16},{56,24},{64,96... | collective-permute-start | bytes 294920 | tf_op jit(solution)/shard_map/ppermute | solution.py:312
  38.2 0.3 collective-permute-start.9
  38.5 2.4 %collective-permute-start.11 = (bf16[32,1536]{1,0:T(8,128)(2,1)S(1)}, bf16[32,1536]{1,0:T(8,128)(2,1)S(1)}, u32[]{:S(2)}, u32[]{:S(2)}) collective-permute-start(bf16[32,1536]{1,0:T(8,128)(2,1)S(1)} %pad_maximum_fusion.refs_8_), channel_id=1, source_target_pairs={{0,48},{8,56},{16,0},{24,8},{32,16},{40,24},{48,32},{56,40},{64,11... | collective-permute-start | bytes 294920 | tf_op jit(solution)/shard_map/ppermute | solution.py:312
  40.9 0.0 collective-permute-done.10.refs_1_
  40.9 2.7 %collective-permute-done.9.refs_0_ = bf16[32,1536]{1,0:T(8,128)(2,1)S(1)} collective-permute-done((bf16[32,1536]{1,0:T(8,128)(2,1)S(1)}, bf16[32,1536]{1,0:T(8,128)(2,1)S(1)}, u32[]{:S(2)}, u32[]{:S(2)}) %collective-permute-start.9) | collective-permute-done | bytes 98336 | tf_op jit(solution)/shard_map/ppermute | solution.py:312
  43.7 0.0 collective-permute-done.11.refs_10_
  43.7 0.0 all-to-all-done.refs_11_
  43.7 0.0 copy-start.3
  43.7 0.9 %copy-done.3 = bf16[512,192]{1,0:T(8,128)(2,1)S(1)} copy-done((bf16[512,192]{1,0:T(8,128)(2,1)S(1)}, bf16[512,192]{1,0:T(8,128)(2,1)}, u32[]{:S(2)}) %copy-start.3) | copy-done | bytes 196632
  44.6 4.1 %shard_map.101 = (bf16[8,400,128]{2,1,0:T(8,128)(2,1)S(1)}, bf16[8,400,128]{2,1,0:T(8,128)(2,1)S(1)}) custom-call(bf16[72,1536]{1,0:T(8,128)(2,1)S(1)} %dynamic_update_slice.7.refs_0_, bf16[72,1536]{1,0:T(8,128)(2,1)S(1)} %collective-permute-done.2.refs_1_, bf16[72,1536]{1,0:T(8,128)(2,1)S(1)} %collective-permute-done.1.refs_2_, ...), custom_call_target="tpu_custom_call" | custom-call | tf_op jit(solution)/shard_map/pallas_call | solution.py:293
  48.7 1.8 %collective-permute-start.12 = (bf16[8,400,128]{2,1,0:T(8,128)(2,1)S(1)}, bf16[8,400,128]{2,1,0:T(8,128)(2,1)S(1)}, u32[]{:S(2)}, u32[]{:S(2)}) collective-permute-start(bf16[8,400,128]{2,1,0:T(8,128)(2,1)S(1)} %get-tuple-element.38), channel_id=1, source_target_pairs={{0,8},{8,0},{16,24},{24,16},{32,40},{40,32},{48,56},{56,48},{64,72... | collective-permute-start | bytes 2457608 | tf_op jit(solution)/shard_map/ppermute | solution.py:374
  50.5 2.0 %collective-permute-done.12 = bf16[8,400,128]{2,1,0:T(8,128)(2,1)S(1)} collective-permute-done((bf16[8,400,128]{2,1,0:T(8,128)(2,1)S(1)}, bf16[8,400,128]{2,1,0:T(8,128)(2,1)S(1)}, u32[]{:S(2)}, u32[]{:S(2)}) %collective-permute-start.12) | collective-permute-done | bytes 819232 | tf_op jit(solution)/shard_map/ppermute | solution.py:374
  52.5 0.2 add_convert_fusion
  52.7 17.3 %all_to_all.10.r_ref = bf16[8,400,128]{2,1,0:T(8,128)(2,1)S(1)} all-to-all(bf16[8,400,128]{2,1,0:T(8,128)(2,1)S(1)} %add_convert_fusion), channel_id=1, replica_groups={{0,16,32,48,64,80,96,112},{8,24,40,56,72,88,104,120},{1,17,33,49,65,81,..., dimensions={0} | all-to-all | bytes 1638400 | tf_op jit(solution)/shard_map/all_to_all | solution.py:376
  70.0 0.0 copy-done.6
  70.0 0.0 copy-done.7
  70.0 1.5 %shard_map.102 = (f32[1,1536]{1,0:T(1,128)}, f32[3,192,96]{2,1,0:T(8,128)}, f32[192,96]{1,0:T(8,128)}) custom-call(bf16[8,400,128]{2,1,0:T(8,128)(2,1)S(1)} %all_to_all.10.r_ref, bf16[1,1536]{1,0:T(2,128)(2,1)S(1)} %copy-done.7, f32[12,128]{1,0:T(8,128)S(1)} %bitcast.2), custom_call_target="tpu_custom_call" | custom-call | tf_op jit(solution)/shard_map/pallas_call | solution.py:293
  (11 shorter events, 0.1 us)
Async XLA Ops:
  0.6 3.5 %collective-permute-start = (bf16[1,1536]{1,0:T(2,128)(2,1)}, bf16[1,1536]{1,0:T(2,128)(2,1)S(1)}, u32[]{:S(2)}, u32[]{:S(2)}) collective-permute-start(bf16[1,1536]{1,0:T(2,128)(2,1)} %text_ref.1), channel_id=1, source_target_pairs={{0,8},{8,0},{16,24},{24,16},{32,40},{40,32},{48,56},{56,48},{64,72... | collective-permute-start | bytes 9224 | tf_op jit(solution)/shard_map/ppermute | solution.py:312
  2.1 0.9 %copy-start.4 = (bf16[8,12288]{1,0:T(8,128)(2,1)S(1)}, bf16[8,12288]{1,0:T(8,128)(2,1)}, u32[]{:S(2)}) copy-start(bf16[8,12288]{1,0:T(8,128)(2,1)} %tok_ref.1) | copy-start | bytes 589828
  4.3 9.4 %collective-permute-start.2 = (bf16[72,1536]{1,0:T(8,128)(2,1)S(1)}, bf16[72,1536]{1,0:T(8,128)(2,1)S(1)}, u32[]{:S(2)}, u32[]{:S(2)}) collective-permute-start(bf16[72,1536]{1,0:T(8,128)(2,1)S(1)} %dynamic_update_slice.7.refs_0_), channel_id=1, source_target_pairs={{0,1},{1,0},{2,3},{3,2},{4,5},{5,4},{6,7},{7,6},{8,9},{9,8},{10,11... | collective-permute-start | bytes 663560 | tf_op jit(solution)/shard_map/ppermute | solution.py:305
  7.3 9.4 %collective-permute-start.4 = (bf16[72,1536]{1,0:T(8,128)(2,1)S(1)}, bf16[72,1536]{1,0:T(8,128)(2,1)S(1)}, u32[]{:S(2)}, u32[]{:S(2)}) collective-permute-start(bf16[72,1536]{1,0:T(8,128)(2,1)S(1)} %dynamic_update_slice.7.refs_0_), channel_id=1, source_target_pairs={{0,4},{1,5},{2,6},{3,7},{4,0},{5,1},{6,2},{7,3},{8,12},{9,13},{10,... | collective-permute-start | bytes 663560 | tf_op jit(solution)/shard_map/ppermute | solution.py:305
  10.9 10.6 %collective-permute-start.1 = (bf16[72,1536]{1,0:T(8,128)(2,1)S(1)}, bf16[72,1536]{1,0:T(8,128)(2,1)S(1)}, u32[]{:S(2)}, u32[]{:S(2)}) collective-permute-start(bf16[72,1536]{1,0:T(8,128)(2,1)S(1)} %dynamic_update_slice.7.refs_0_), channel_id=1, source_target_pairs={{0,2},{1,3},{2,4},{3,5},{4,6},{5,7},{6,0},{7,1},{8,10},{9,11},{10,... | collective-permute-start | bytes 663560 | tf_op jit(solution)/shard_map/ppermute | solution.py:305
  11.7 10.0 %collective-permute-start.3 = (bf16[72,1536]{1,0:T(8,128)(2,1)S(1)}, bf16[72,1536]{1,0:T(8,128)(2,1)S(1)}, u32[]{:S(2)}, u32[]{:S(2)}) collective-permute-start(bf16[72,1536]{1,0:T(8,128)(2,1)S(1)} %dynamic_update_slice.7.refs_0_), channel_id=1, source_target_pairs={{0,6},{1,7},{2,0},{3,1},{4,2},{5,3},{6,4},{7,5},{8,14},{9,15},{10,... | collective-permute-start | bytes 663560 | tf_op jit(solution)/shard_map/ppermute | solution.py:305
  13.6 12.7 %collective-permute-start.5 = (bf16[72,1536]{1,0:T(8,128)(2,1)S(1)}, bf16[72,1536]{1,0:T(8,128)(2,1)S(1)}, u32[]{:S(2)}, u32[]{:S(2)}) collective-permute-start(bf16[72,1536]{1,0:T(8,128)(2,1)S(1)} %collective-permute-done.2.refs_1_), channel_id=1, source_target_pairs={{0,2},{1,3},{2,4},{3,5},{4,6},{5,7},{6,0},{7,1},{8,10},{9,11},{10,... | collective-permute-start | bytes 663560 | tf_op jit(solution)/shard_map/ppermute | solution.py:305
  14.6 11.8 %collective-permute-start.6 = (bf16[72,1536]{1,0:T(8,128)(2,1)S(1)}, bf16[72,1536]{1,0:T(8,128)(2,1)S(1)}, u32[]{:S(2)}, u32[]{:S(2)}) collective-permute-start(bf16[72,1536]{1,0:T(8,128)(2,1)S(1)} %collective-permute-done.2.refs_1_), channel_id=1, source_target_pairs={{0,6},{1,7},{2,0},{3,1},{4,2},{5,3},{6,4},{7,5},{8,14},{9,15},{10,... | collective-permute-start | bytes 663560 | tf_op jit(solution)/shard_map/ppermute | solution.py:305
  16.8 9.8 %collective-permute-start.7 = (bf16[72,1536]{1,0:T(8,128)(2,1)S(1)}, bf16[72,1536]{1,0:T(8,128)(2,1)S(1)}, u32[]{:S(2)}, u32[]{:S(2)}) collective-permute-start(bf16[72,1536]{1,0:T(8,128)(2,1)S(1)} %collective-permute-done.4.refs_4_), channel_id=1, source_target_pairs={{0,1},{1,0},{2,3},{3,2},{4,5},{5,4},{6,7},{7,6},{8,9},{9,8},{10,11... | collective-permute-start | bytes 663560 | tf_op jit(solution)/shard_map/ppermute | solution.py:305
  21.7 1.5 %copy-start.1 = (bf16[3,192,1536]{2,1,0:T(8,128)(2,1)S(1)}, bf16[3,192,1536]{2,1,0:T(8,128)(2,1)}, u32[]{:S(2)}) copy-start(bf16[3,192,1536]{2,1,0:T(8,128)(2,1)} %refs_5_.2) | copy-start | bytes 5308420
  23.2 0.7 copy-start.5
  25.0 2.2 %copy-start = (bf16[192,1536]{1,0:T(8,128)(2,1)S(1)}, bf16[192,1536]{1,0:T(8,128)(2,1)}, u32[]{:S(2)}) copy-start(bf16[192,1536]{1,0:T(8,128)(2,1)} %refs_17_.1) | copy-start | bytes 1769476
  26.6 8.7 %collective-permute-start.8 = (bf16[16,1536]{1,0:T(8,128)(2,1)S(1)}, bf16[16,1536]{1,0:T(8,128)(2,1)S(1)}, u32[]{:S(2)}, u32[]{:S(2)}) collective-permute-start(bf16[16,1536]{1,0:T(8,128)(2,1)S(1)} %shard_map.98), channel_id=1, source_target_pairs={{0,64},{8,72},{16,80},{24,88},{32,96},{40,104},{48,112},{56,120},{... | collective-permute-start | bytes 147464 | tf_op jit(solution)/shard_map/ppermute | solution.py:312
  29.1 0.7 copy-start.2
  29.8 13.8 %all-to-all-start = ((bf16[8,8,1536]{2,1,0:T(8,128)(2,1)}), bf16[8,8,1536]{2,1,0:T(8,128)(2,1)S(1)}, u32[]{:S(2)}, u32[]{:S(2)}) async-start(bf16[8,8,1536]{2,1,0:T(8,128)(2,1)} %get-tuple-element.31), calls=%async_computation | async-start | bytes 393216 | tf_op jit(solution)/shard_map/all_to_all | solution.py:364
  35.4 5.5 %collective-permute-start.10 = (bf16[32,1536]{1,0:T(8,128)(2,1)S(1)}, bf16[32,1536]{1,0:T(8,128)(2,1)S(1)}, u32[]{:S(2)}, u32[]{:S(2)}) collective-permute-start(bf16[32,1536]{1,0:T(8,128)(2,1)S(1)} %pad_maximum_fusion.refs_8_), channel_id=1, source_target_pairs={{0,32},{8,40},{16,48},{24,56},{32,0},{40,8},{48,16},{56,24},{64,96... | collective-permute-start | bytes 294920 | tf_op jit(solution)/shard_map/ppermute | solution.py:312
  38.2 5.4 %collective-permute-start.9 = (bf16[32,1536]{1,0:T(8,128)(2,1)S(1)}, bf16[32,1536]{1,0:T(8,128)(2,1)S(1)}, u32[]{:S(2)}, u32[]{:S(2)}) collective-permute-start(bf16[32,1536]{1,0:T(8,128)(2,1)S(1)} %pad_maximum_fusion.refs_8_), channel_id=1, source_target_pairs={{0,16},{8,24},{16,32},{24,40},{32,48},{40,56},{48,0},{56,8},{64,80... | collective-permute-start | bytes 294920 | tf_op jit(solution)/shard_map/ppermute | solution.py:312
  38.5 5.1 %collective-permute-start.11 = (bf16[32,1536]{1,0:T(8,128)(2,1)S(1)}, bf16[32,1536]{1,0:T(8,128)(2,1)S(1)}, u32[]{:S(2)}, u32[]{:S(2)}) collective-permute-start(bf16[32,1536]{1,0:T(8,128)(2,1)S(1)} %pad_maximum_fusion.refs_8_), channel_id=1, source_target_pairs={{0,48},{8,56},{16,0},{24,8},{32,16},{40,24},{48,32},{56,40},{64,11... | collective-permute-start | bytes 294920 | tf_op jit(solution)/shard_map/ppermute | solution.py:312
  43.7 1.0 %copy-start.3 = (bf16[512,192]{1,0:T(8,128)(2,1)S(1)}, bf16[512,192]{1,0:T(8,128)(2,1)}, u32[]{:S(2)}) copy-start(bf16[512,192]{1,0:T(8,128)(2,1)} %copy-done.2) | copy-start | bytes 589828
  48.7 3.8 %collective-permute-start.12 = (bf16[8,400,128]{2,1,0:T(8,128)(2,1)S(1)}, bf16[8,400,128]{2,1,0:T(8,128)(2,1)S(1)}, u32[]{:S(2)}, u32[]{:S(2)}) collective-permute-start(bf16[8,400,128]{2,1,0:T(8,128)(2,1)S(1)} %get-tuple-element.38), channel_id=1, source_target_pairs={{0,8},{8,0},{16,24},{24,16},{32,40},{40,32},{48,56},{56,48},{64,72... | collective-permute-start | bytes 2457608 | tf_op jit(solution)/shard_map/ppermute | solution.py:374
  52.5 17.5 %copy-start.6 = (f32[1536]{0:T(1024)S(1)}, f32[1536]{0:T(1024)}, u32[]{:S(2)}) copy-start(f32[1536]{0:T(1024)} %param.8) | copy-start | bytes 18436
  52.5 17.5 %copy-start.7 = (bf16[1,1536]{1,0:T(2,128)(2,1)S(1)}, bf16[1,1536]{1,0:T(2,128)(2,1)}, u32[]{:S(2)}) copy-start(bf16[1,1536]{1,0:T(2,128)(2,1)} %text_ref.1) | copy-start | bytes 9220
